TPU v7x, 32 devices: a whole 2x2x4 slice. The times are simulated.
32 devices in a mesh: groups: 2 (over x), rows: 16 (over z, y, core).
Axes of the slice: x: 2, y: 2, z: 4, core: 2. Of those that a mesh axis runs over, the one named last changes fastest.
Arguments:
- grid_inputs: bfloat16 [474, 4096], P(None, ('groups', 'rows')), parts along dimension 1, may hold values from -6 to 6
- link_features: float32 [4, 4096], P(None, 'rows'), may hold values from -6 to 6
- link_partition: int32 [2048, 2], P('rows'), may hold values from 0 to 15, all different within a row; in each aligned block of 128 rows (0 to 127, 128 to 255, ...) at most 32 rows name the same one
- link_node: int32 [2048, 2], P('rows'), may hold values from 0 to 383
- mesh_start: bfloat16 [6144, 512], P('rows'), may hold values from -6 to 6
- edge_features: float32 [4, 49152], P(None, 'rows'), may hold values from -6 to 6
- edge_senders: int32 [6144, 8], P('rows'), may hold values from 0 to 639, as said below
- halo_lists: int32 [16, 16, 16], P('rows'), may hold values from -1 to 383, as said below
- embed_first: bfloat16 [474, 512], replicated, may hold values from -0.25 to 0.25
- embed_second: bfloat16 [512, 512], replicated, may hold values from -0.25 to 0.25
- link_embed: float32 [4, 512], replicated, may hold values from -3 to 3
- link_first: bfloat16 [1536, 512], replicated, may hold values from -0.15625 to 0.15625
- link_second: bfloat16 [512, 512], replicated, may hold values from -0.25 to 0.25
- update_first: bfloat16 [1024, 512], replicated, may hold values from -0.1875 to 0.1875
- update_second: bfloat16 [512, 512], replicated, may hold values from -0.25 to 0.25
- edge_embed: float32 [4, 512], replicated, may hold values from -3 to 3
- process_first: bfloat16 [2, 1536, 512], replicated, may hold values from -0.15625 to 0.15625
- process_second: bfloat16 [2, 512, 512], replicated, may hold values from -0.25 to 0.25
- process_update_first: bfloat16 [2, 1024, 512], replicated, may hold values from -0.1875 to 0.1875
- process_update_second: bfloat16 [2, 512, 512], replicated, may hold values from -0.25 to 0.25
- update_gain: float32 [3, 512], replicated, may hold values from 0.5 to 1.5
Outputs:
- mesh_state: bfloat16 [12288, 512], P(('groups', 'rows')), parts along dimension 0
There are 2 independent parts, one for each index of `groups`. A program takes and returns all parts, laid end to end along the dimension named above; an argument that names none is the same for every part. Nothing has to cross between parts.
Inputs may be any that keep to these rules, and one draw needn't show every extreme that they name: `link_partition`: the 2 partitions named by one cell differ. Among the cells of one slab no partition is named more than 32 times, and some slab names some partition exactly 32 times. Every partition is named. `halo_lists`: each entry is a node index of the owning device o, or -1 for an empty slot; filled slots come first in every list. The lists of o to the devices o + 1 and o - 1 (modulo 16) are full; its list to o + 8 holds exactly 4 nodes; any other list to another device holds at most 4; the list to itself is empty. `edge_senders`: an entry s below 384 is node s of the receiving node's own partition d; an entry s = 384 + o * 16 + t names slot t of halo_lists[o, d], which is filled. Every filled slot of a list to d is named by some edge of a node of d.
All inputs are finite; a program needn't handle non-finite values.
Results may differ from a plain program's by a relative error of at most 0.015.
Values may be sent and summed in bfloat16 or wider, within the bound.
No kernel may reach another device: no remote copies, remote signals or barrier semaphores. Data moves between devices by JAX's collectives and lax.ppermute only.
A program may use at most 128 MiB of HBM per device.

v0:
```python
import functools

import jax
import jax.numpy as jnp
from jax import lax
from jax.experimental import pallas as pl
from jax.experimental.pallas import tpu as pltpu
from jax.sharding import PartitionSpec as P

epsilon = 1e-05
f32 = jnp.float32
bf16 = jnp.bfloat16
MIB = 2**20
EXTRA = 32


def dot(left, right, left_dim=1, right_dim=0):
    return lax.dot_general(
        left, right, (((left_dim,), (right_dim,)), ((), ())), preferred_element_type=f32
    )


def silu(values):
    half = 0.5 * values
    return half + half * jnp.tanh(half)


def normalize(values):
    scale = 1.0 / values.shape[-1]
    center = values - jnp.sum(values, axis=-1, keepdims=True) * scale
    spread = jnp.sum(center * center, axis=-1, keepdims=True) * scale
    return center * lax.rsqrt(spread + epsilon)


def iota(shape, dim):
    return lax.broadcasted_iota(jnp.int32, shape, dim)


def split3(values):
    high = values.astype(bf16).astype(f32)
    rest = values - high
    middle = rest.astype(bf16).astype(f32)
    return high, middle, rest - middle


def store_pieces(ref, values, order, base=0):
    pieces = split3(values)
    rows = values.shape[0]
    for place, piece in enumerate(order):
        ref[base + place * rows : base + (place + 1) * rows, :] = pieces[piece]


LEFT_ORDER = (0, 0, 0, 1, 1, 2)
RIGHT_ORDER = (0, 1, 2, 0, 1, 0)


class Load:
    def __init__(self, source, target, semaphore):
        self.copy = pltpu.make_async_copy(source, target, semaphore)
        self.target = target
        self.waiting = True
        self.copy.start()

    def __call__(self):
        if self.waiting:
            self.copy.wait()
            self.waiting = False
        return self.target


def run(kernel, name, outs, args, scratch=(), flops=10**9):
    plans = []
    for arg in args:
        if not isinstance(arg, tuple):
            arg = (arg, None, 1)
        array, take, count = arg
        if take is None:
            shape = array.shape
        else:
            shape = jax.eval_shape(lambda x, take=take: take(x, 0), array).shape
        plans.append((array, take, count, shape))
    n_in, n_out = len(plans), len(outs)
    starts, total = [], 0
    for plan in plans:
        starts.append(total)
        total += plan[2]
    out_starts, out_total = [], 0
    for out in outs:
        out_starts.append(out_total)
        out_total += out[2]
    arrays, places = [], []
    for plan in plans:
        known = [i for i, array in enumerate(arrays) if array is plan[0]]
        if known:
            places.append(known[0])
        else:
            places.append(len(arrays))
            arrays.append(plan[0])

    def whole(*refs):
        ins = refs[: len(arrays)]
        out_refs = refs[len(arrays) : len(arrays) + n_out]
        rest = refs[len(arrays) + n_out :]
        in_vmem, out_vmem = rest[:n_in], rest[n_in : n_in + n_out]
        in_sems, out_sems = rest[n_in + n_out : n_in + n_out + 2]
        loads = []
        for i, (array, take, count, shape) in enumerate(plans):
            source = ins[places[i]]
            pieces = []
            for piece in range(count):
                view = source if take is None else take(source.at, piece)
                target = in_vmem[i] if count == 1 else in_vmem[i].at[piece]
                pieces.append(Load(view, target, in_sems.at[starts[i] + piece]))
            loads.append(pieces[0] if count == 1 else pieces)
        pending = []

        def store(i, value, piece=None):
            target = out_vmem[i] if piece is None else out_vmem[i].at[piece]
            out = out_refs[i] if piece is None else out_refs[i].at[piece]
            target[...] = value
            copy = pltpu.make_async_copy(target, out, out_sems.at[out_starts[i] + (piece or 0)])
            copy.start()
            pending.append(copy)

        kernel(loads, store, *rest[n_in + n_out + 2 :])
        for pieces in loads:
            for load in pieces if isinstance(pieces, list) else [pieces]:
                load()
        for copy in pending:
            copy.wait()

    spec = pl.BlockSpec(memory_space=pl.ANY)
    in_scratch = [
        pltpu.VMEM(shape if count == 1 else (count,) + shape, array.dtype)
        for array, _, count, shape in plans
    ]
    return pl.pallas_call(
        whole,
        out_shape=[jax.ShapeDtypeStruct(out[0], out[1]) for out in outs],
        in_specs=[spec] * len(arrays),
        out_specs=[spec] * n_out,
        scratch_shapes=in_scratch
        + [pltpu.VMEM(out[0], out[1]) for out in outs]
        + [pltpu.SemaphoreType.DMA((total,)), pltpu.SemaphoreType.DMA((out_total,))]
        + list(scratch),
        compiler_params=pltpu.CompilerParams(vmem_limit_bytes=60 * MIB),
        cost_estimate=pl.CostEstimate(flops=flops, bytes_accessed=8 * MIB, transcendentals=0),
        name=name,
    )(*arrays)


def rows_of(start, stop, step=None):
    if step is None:
        return lambda ref, i: ref[start:stop]
    return lambda ref, i: ref[step, start:stop]


def piece_of(ref, i):
    return ref[i]


def fixed(step):
    return lambda ref, i: ref[step]


def pack_kernel(devices, loads, store, columns, extra):
    grid, features, partition, node = loads
    channels, cells = grid.target.shape
    fanout = partition.target.shape[0]
    links = cells * fanout
    width = columns.shape[0]
    slots = 2 * links
    capacity = slots // devices
    place = iota((cells, links), 1)
    repeat = jnp.where(
        functools.reduce(
            jnp.logical_or,
            [place == iota((cells, links), 0) + k * cells for k in range(fanout)],
        ),
        1.0,
        0.0,
    ).astype(bf16)
    order = iota((links, links), 0)
    turn = iota((links, links), 1)
    upper = jnp.where(order <= turn, 1.0, 0.0).astype(bf16)
    spread = jnp.where(order == turn % cells * fanout + turn // cells, 1.0, 0.0).astype(bf16)
    extra[...] = jnp.zeros_like(extra)
    columns[width - EXTRA - 16 : width - EXTRA, :] = jnp.zeros((16, links), bf16)
    store_pieces(extra, features()[...], LEFT_ORDER)
    target = jnp.concatenate([partition()[k : k + 1, :] for k in range(fanout)], axis=1)
    nodes = jnp.concatenate([node()[k : k + 1, :] for k in range(fanout)], axis=1) + 1
    extra[...] = dot(extra[...].astype(bf16), spread)
    extra[24:25, :] = (nodes >> 4).astype(f32)
    extra[25:26, :] = (nodes & 15).astype(f32)
    matches = jnp.where(iota((devices, links), 0) == target, 1.0, 0.0)
    counts = dot(matches.astype(bf16), upper)
    rank = jnp.sum(counts * matches, axis=0, keepdims=True).astype(jnp.int32) - 1
    slot = target * capacity + rank
    select = jnp.where(iota((slots, links), 0) == slot, 1.0, 0.0).astype(bf16)
    columns[0:channels, :] = dot(grid()[...], repeat).astype(bf16)
    columns[width - EXTRA : width, :] = extra[...].astype(bf16)
    store(0, dot(select, columns[...], 1, 1).astype(bf16))


def side_kernel(far, loads, store, pieces, turned, table):
    features, embed, start, link_receiver, update_start, lists = loads
    owned, width = start.target.shape
    edges = features.target.shape[1]
    degree = edges // owned
    devices, slots = lists.target.shape[1:]
    pieces[...] = jnp.zeros_like(pieces)
    turned[...] = jnp.zeros_like(turned)
    table[...] = jnp.zeros_like(table)
    store_pieces(pieces, features()[...], LEFT_ORDER)
    turned[:, 0:EXTRA] = jnp.transpose(pieces[...])
    store_pieces(table, embed()[...], RIGHT_ORDER)
    matrix = table[...].astype(bf16)
    for j in range(degree):
        left = turned[pl.ds(j, owned, stride=degree), :].astype(bf16)
        store(0, normalize(silu(dot(left, matrix))).astype(bf16), j)
    store(1, dot(start()[...], link_receiver()[...]).astype(bf16))
    store(2, dot(start()[...], update_start()[...]))
    lists = lists()[0]
    me = lax.axis_index("rows")
    rows = devices * far + 2 * slots
    row = iota((rows, 1), 0)
    near = row - devices * far
    after = (me + 1) % devices
    before = (me + devices - 1) % devices
    reader = jnp.where(near < 0, row // far, jnp.where(near < slots, after, before))
    place = jnp.where(near < 0, row % far, near % slots)
    picks = jnp.where(iota((rows, devices), 1) == reader, 1.0, 0.0).astype(bf16)
    high = dot(picks, (lists >> 4).astype(f32).astype(bf16))
    low = dot(picks, (lists & 15).astype(f32).astype(bf16))
    chosen = jnp.where(iota((rows, slots), 1) == place, high * 16.0 + low, 0.0)
    column = jnp.sum(chosen, axis=1, keepdims=True).astype(jnp.int32)
    store(3, jnp.where(iota((rows, owned), 1) == column, 1.0, 0.0).astype(bf16))


def update(state, summand, second, gain):
    hidden = silu(summand).astype(bf16)
    return (state.astype(f32) + gain * normalize(dot(hidden, second))).astype(bf16)


def send(store, base, state, sender, select, devices, far, slots):
    sent = dot(state, sender).astype(bf16)
    outgoing = dot(select, sent).astype(bf16)
    count = devices * far
    store(base + 1, outgoing[0:count])
    store(base + 2, outgoing[count : count + slots])
    store(base + 3, outgoing[count + slots : count + 2 * slots])
    store(base, sent)


def link_kernel(sizes, loads, store, first, table, messages):
    (
        terms,
        embed_first,
        embed_second,
        link_embed,
        link_sender,
        link_edge,
        receiver,
        link_second,
        base,
        update_first,
        update_second,
        gain,
        start,
        sender_first,
        select,
    ) = loads
    owned, width = start.target.shape
    slots = terms.target.shape[0]
    channels = embed_first.target.shape[0]
    tail = table.shape[0]
    first[...] = jnp.zeros_like(first)
    table[...] = jnp.zeros_like(table)
    lanes = iota((8, tail), 1)
    weights = jnp.where(
        lanes == tail - EXTRA + 24, 16.0, jnp.where(lanes == tail - EXTRA + 25, 1.0, 0.0)
    ).astype(bf16)
    chunk = 256
    first[0:channels, :] = embed_first()[...]
    store_pieces(table, link_embed()[...], RIGHT_ORDER, tail - EXTRA)
    matrix = table[...].astype(bf16)
    terms = terms()
    for begin in range(0, slots, chunk):
        rows = slice(begin, begin + chunk)
        extra = terms[rows, width - tail :]
        hidden = silu(dot(terms[rows, :], first[...])).astype(bf16)
        grid_state = normalize(dot(hidden, embed_second()[...])).astype(bf16)
        sender = dot(grid_state, link_sender()[...]).astype(bf16).astype(f32)
        link_state = normalize(silu(dot(extra, matrix))).astype(bf16)
        link_terms = (sender + dot(link_state, link_edge()[...])).astype(bf16)
        parts = extra.astype(f32)
        node = (
            parts[:, tail - EXTRA + 24 : tail - EXTRA + 25] * 16.0
            + parts[:, tail - EXTRA + 25 : tail - EXTRA + 26]
        ).astype(jnp.int32)
        pick = jnp.where(iota((chunk, owned), 1) == node - 1, 1.0, 0.0).astype(bf16)
        summand = link_terms.astype(f32) + dot(pick, receiver()[...])
        message = normalize(dot(silu(summand).astype(bf16), link_second()[...]))
        messages[rows, :] = message.astype(bf16)
    nodes = dot(weights, terms[:, width - tail :], 1, 1)[0:1, :].astype(jnp.int32)
    collect = jnp.where(iota((owned, slots), 0) == nodes - 1, 1.0, 0.0).astype(bf16)
    summed = dot(collect, messages[...]).astype(bf16)
    summand = base()[...] + dot(summed, update_first()[...])
    state = update(start()[...], summand, update_second()[...], gain()[0:1, :])
    store(0, state)
    send(store, 1, state, sender_first()[...], select()[...], *sizes)


def local_kernel(loads, store):
    senders, state, receiver_first, sent, edge_first, edges = loads
    degree, owned = senders.target.shape
    columns = jnp.transpose(senders()[...].astype(f32)).astype(jnp.int32)
    kept = dot(state()[...], receiver_first()[...]).astype(bf16).astype(f32)
    for j in range(degree):
        local = jnp.where(iota((owned, owned), 1) == columns[:, j : j + 1], 1.0, 0.0)
        part = dot(local.astype(bf16), sent()[...]) + dot(edges[j]()[...], edge_first()[...])
        store(0, part + kept, j)


def edge_kernel(step, last, sizes, loads, store, table):
    (senders, far_rows, from_before, from_after, second, sums) = loads[:6]
    (state, state_first, summed_first, update_second, gain) = loads[6:11]
    if not last:
        edges, sender_first, select = loads[11:]
    devices, far, slots = sizes
    degree, owned = senders.target.shape
    count = devices * far
    rows = table.shape[0]
    me = lax.axis_index("rows")
    after = (me + 1) % devices
    before = (me + devices - 1) % devices
    senders = senders()[...]
    halo = senders - owned
    owner = halo // slots
    place = halo % slots
    index = jnp.where(
        owner == before,
        count + place,
        jnp.where(owner == after, count + slots + place, owner * far + place),
    )
    index = jnp.where(halo < 0, -1, index)
    columns = jnp.transpose(index.astype(f32)).astype(jnp.int32)
    table[count + 2 * slots :, :] = jnp.zeros((rows - count - 2 * slots, table.shape[1]), bf16)
    table[0:count, :] = far_rows()[...]
    table[count : count + slots, :] = from_before()[...]
    table[count + slots : count + 2 * slots, :] = from_after()[...]
    total = jnp.zeros(state.target.shape, f32)
    for j in range(degree):
        pick = jnp.where(iota((owned, rows), 1) == columns[:, j : j + 1], 1.0, 0.0)
        summand = sums[j]()[...] + dot(pick.astype(bf16), table[...])
        hidden = silu(summand).astype(bf16)
        message = normalize(dot(hidden, second()[...])).astype(bf16).astype(f32)
        total = total + message
        if not last:
            store(5, (edges[j]()[...].astype(f32) + message).astype(bf16), j)
    summand = dot(state()[...], state_first()[...]) + dot(
        total.astype(bf16), summed_first()[...]
    )
    state = update(
        state()[...], summand, update_second()[...], gain()[step + 1 : step + 2, :]
    )
    store(0, state)
    if not last:
        send(store, 1, state, sender_first()[...], select()[...], *sizes)


def body(
    grid_inputs,
    link_features,
    link_partition,
    link_node,
    mesh_start,
    edge_features,
    edge_senders,
    halo_lists,
    embed_first,
    embed_second,
    link_embed,
    link_first,
    link_second,
    update_first,
    update_second,
    edge_embed,
    process_first,
    process_second,
    process_update_first,
    process_update_second,
    update_gain,
):
    owned, width = mesh_start.shape
    devices = lax.axis_size("rows")
    cells = grid_inputs.shape[1]
    links = cells * link_partition.shape[1]
    slots = 2 * links
    degree = edge_senders.shape[1]
    edges = owned * degree
    halo_slots = halo_lists.shape[2]
    far = 8
    sizes = (devices, far, halo_slots)
    halo_rows = devices * far + 2 * halo_slots
    senders = edge_senders.T

    def exchange(values):
        values = values.reshape(devices, -1, width)
        return lax.all_to_all(values, "rows", split_axis=0, concat_axis=0, tiled=True).reshape(
            -1, width
        )

    def halo(outgoing):
        up = [(i, (i + 1) % devices) for i in range(devices)]
        down = [(i, (i + devices - 1) % devices) for i in range(devices)]
        from_before = lax.ppermute(outgoing[1], "rows", up)
        from_after = lax.ppermute(outgoing[2], "rows", down)
        return exchange(outgoing[0]), from_before, from_after

    sending = [
        ((owned, width), bf16, 1),
        ((devices * far, width), bf16, 1),
        ((halo_slots, width), bf16, 1),
        ((halo_slots, width), bf16, 1),
    ]
    (packed,) = run(
        functools.partial(pack_kernel, devices),
        "pack",
        [((slots, width), bf16, 1)],
        (grid_inputs, link_features, link_partition.T, link_node.T),
        [pltpu.VMEM((width, links), bf16), pltpu.VMEM((EXTRA, links), f32)],
    )
    terms = exchange(packed)
    edge_state, receiver, base, select = run(
        functools.partial(side_kernel, far),
        "side",
        [
            ((degree, owned, width), bf16, degree),
            ((owned, width), bf16, 1),
            ((owned, width), f32, 1),
            ((halo_rows, owned), bf16, 1),
        ],
        (
            edge_features,
            edge_embed,
            mesh_start,
            (link_first, rows_of(width, 2 * width), 1),
            (update_first, rows_of(0, width), 1),
            halo_lists,
        ),
        [
            pltpu.VMEM((EXTRA, edges), f32),
            pltpu.VMEM((edges, 128), f32),
            pltpu.VMEM((128, width), f32),
        ],
        flops=10**10,
    )
    state, sent, *outgoing = run(
        functools.partial(link_kernel, sizes),
        "link",
        [((owned, width), bf16, 1)] + sending,
        (
            terms,
            embed_first,
            embed_second,
            link_embed,
            (link_first, rows_of(0, width), 1),
            (link_first, rows_of(2 * width, 3 * width), 1),
            receiver,
            link_second,
            base,
            (update_first, rows_of(width, 2 * width), 1),
            update_second,
            update_gain,
            mesh_start,
            (process_first, rows_of(0, width, 0), 1),
            select,
        ),
        [
            pltpu.VMEM((width, width), bf16),
            pltpu.VMEM((128, width), f32),
            pltpu.VMEM((slots, width), bf16),
        ],
    )
    steps = process_first.shape[0]
    for step in range(steps):
        last = step + 1 == steps
        incoming = halo(outgoing)
        (sums,) = run(
            local_kernel,
            f"local{step}",
            [((degree, owned, width), f32, degree)],
            (
                senders,
                state,
                (process_first, rows_of(width, 2 * width, step), 1),
                sent,
                (process_first, rows_of(2 * width, 3 * width, step), 1),
                (edge_state, piece_of, degree),
            ),
            flops=10**10,
        )
        outs = [((owned, width), bf16, 1)]
        extra = []
        if not last:
            outs += sending + [((degree, owned, width), bf16, degree)]
            extra = [
                (edge_state, piece_of, degree),
                (process_first, rows_of(0, width, step + 1), 1),
                select,
            ]
        results = run(
            functools.partial(edge_kernel, step, last, sizes),
            f"edge{step}",
            outs,
            [
                senders,
                *incoming,
                (process_second, fixed(step), 1),
                (sums, piece_of, degree),
                state,
                (process_update_first, rows_of(0, width, step), 1),
                (process_update_first, rows_of(width, 2 * width, step), 1),
                (process_update_second, fixed(step), 1),
                update_gain,
            ]
            + extra,
            [pltpu.VMEM((-(-halo_rows // 128) * 128, width), bf16)],
        )
        if last:
            return results[0]
        state, sent, *outgoing, edge_state = results


def solution(mesh):
    return jax.shard_map(
        body,
        mesh=mesh,
        in_specs=(
            P(None, ("groups", "rows")),
            P(None, "rows"),
            P("rows", None),
            P("rows", None),
            P("rows", None),
            P(None, "rows"),
            P("rows", None),
            P("rows", None, None),
        )
        + (P(),) * 13,
        out_specs=P(("groups", "rows"), None),
        check_vma=False,
    )
```

profile of v0, /device:TPU:0, one launch (start us, length us, event | category | flops | bytes accessed | tf_op | source)
XLA Modules:
  0.0 90.9 jit_solution(7939542877779119248)
XLA Ops:
  0.0 2.3 %pack.1 = bf16[512,512]{1,0:T(8,128)(2,1)} custom-call(bf16[474,128]{1,0:T(8,128)(2,1)} %refs_0_.2, f32[4,256]{1,0:T(4,128)} %refs_1_.3, s32[2,128]{1,0:T(2,128)} %bitcast.19, s32[2,128]{1,0:T(2,128)} %bitcast.20), custom_call_target="tpu_custom_call" | custom-call | flops 1000000000 | bytes 8388608 | tf_op jit(solution)/shard_map/pack/pallas_call | solution.py:137
  2.3 7.4 %all-to-all-start = ((bf16[16,32,512]{2,1,0:T(8,128)(2,1)}), bf16[16,32,512]{2,1,0:T(8,128)(2,1)S(1)}, u32[]{:S(2)}, u32[]{:S(2)}) async-start(bf16[16,32,512]{2,1,0:T(8,128)(2,1)} %bitcast.11), calls=%async_computation | async-start | bytes 1048576 | tf_op jit(solution)/shard_map/all_to_all | solution.py:410
  9.7 6.0 %side.1 = (bf16[8,384,512]{2,1,0:T(8,128)(2,1)}, bf16[384,512]{1,0:T(8,128)(2,1)}, f32[384,512]{1,0:T(8,128)}, bf16[160,384]{1,0:T(8,128)(2,1)}) custom-call(f32[4,3072]{1,0:T(4,128)} %refs_0_.3, f32[4,512]{1,0:T(4,128)} %refs_1_.4, bf16[384,512]{1,0:T(8,128)(2,1)} %refs_11_.2, bf16[1536,512]{1,0:T(8,128)(2,1)} %refs_4_.5, bf16[1024,512]{1,0:T(8,128)(2,1)} %refs_8_.3, ...), custom_call_target="tpu_custom_call" | custom-call | flops 10000000000 | bytes 8388608 | tf_op jit(solution)/shard_map/side/pallas_call | solution.py:137
  15.8 8.4 %all-to-all-done = bf16[16,32,512]{2,1,0:T(8,128)(2,1)S(1)} async-done(((bf16[16,32,512]{2,1,0:T(8,128)(2,1)}), bf16[16,32,512]{2,1,0:T(8,128)(2,1)S(1)}, u32[]{:S(2)}, u32[]{:S(2)}) %all-to-all-start) | async-done | bytes 524320 | tf_op jit(solution)/shard_map/all_to_all | solution.py:410
  24.2 0.8 copy-done
  25.0 8.6 %link.1 = (bf16[384,512]{1,0:T(8,128)(2,1)}, bf16[384,512]{1,0:T(8,128)(2,1)}, bf16[128,512]{1,0:T(8,128)(2,1)}, bf16[16,512]{1,0:T(8,128)(2,1)}, bf16[16,512]{1,0:T(8,128)(2,1)}) custom-call(bf16[512,512]{1,0:T(8,128)(2,1)} %bitcast.9, bf16[474,512]{1,0:T(8,128)(2,1)} %refs_1_.5, bf16[512,512]{1,0:T(8,128)(2,1)} %refs_2_.5, f32[4,512]{1,0:T(4,128)} %refs_3_.3, ...), custom_call_target="tpu_custom_call" | custom-call | flops 1000000000 | bytes 8388608 | tf_op jit(solution)/shard_map/link/pallas_call | solution.py:137
  33.6 4.1 %all-to-all-start.1 = ((bf16[16,8,512]{2,1,0:T(8,128)(2,1)}), bf16[16,8,512]{2,1,0:T(8,128)(2,1)S(1)}, u32[]{:S(2)}, u32[]{:S(2)}) async-start(bf16[16,8,512]{2,1,0:T(8,128)(2,1)} %bitcast.14), calls=%async_computation.1 | async-start | bytes 262144 | tf_op jit(solution)/shard_map/all_to_all | solution.py:410
  37.7 0.4 collective-permute-start
  38.1 4.2 %collective-permute-start.1 = (bf16[16,512]{1,0:T(8,128)(2,1)}, bf16[16,512]{1,0:T(8,128)(2,1)S(1)}, u32[]{:S(2)}, u32[]{:S(2)}) collective-permute-start(bf16[16,512]{1,0:T(8,128)(2,1)} %get-tuple-element.25), channel_id=1, source_target_pairs={{0,15},{1,0},{2,1},{3,2},{4,3},{5,4},{6,5},{7,6},{8,7},{9,8},{10,9... | collective-permute-start | bytes 49160 | tf_op jit(solution)/shard_map/ppermute | solution.py:418
  42.4 7.4 %local0.1.refs_5_ = f32[8,384,512]{2,1,0:T(8,128)} custom-call(s32[8,384]{1,0:T(8,128)} %bitcast.15, bf16[384,512]{1,0:T(8,128)(2,1)} %get-tuple-element.26.refs_1_.refs_6_, bf16[2,1536,512]{2,1,0:T(8,128)(2,1)} %refs_2_.7, bf16[384,512]{1,0:T(8,128)(2,1)} %get-tuple-element.27.refs_3_, bf16[8,384,512]{2,1,0:T(8,128)(2,1)} %get-tuple-element.28.refs_4_.refs_10_), custom_call_target="tpu_custom_call" | custom-call | flops 10000000000 | bytes 8388608 | tf_op jit(solution)/shard_map/local0/pallas_call | solution.py:137
  49.8 0.0 collective-permute-done.refs_2_
  49.9 0.5 copy-done.3
  50.4 0.0 copy-done.4
  50.4 0.1 copy-done.1
  50.5 13.8 %edge0.1 = (bf16[384,512]{1,0:T(8,128)(2,1)}, bf16[384,512]{1,0:T(8,128)(2,1)}, bf16[128,512]{1,0:T(8,128)(2,1)}, bf16[16,512]{1,0:T(8,128)(2,1)}, bf16[16,512]{...) custom-call(s32[8,384]{1,0:T(8,128)} %bitcast.16, bf16[128,512]{1,0:T(8,128)(2,1)} %bitcast.10, bf16[16,512]{1,0:T(8,128)(2,1)} %copy-done.3, ...), custom_call_target="tpu_custom_call" | custom-call | flops 1000000000 | bytes 8388608 | tf_op jit(solution)/shard_map/edge0/pallas_call | solution.py:137
  64.3 3.5 %all-to-all-start.2 = ((bf16[16,8,512]{2,1,0:T(8,128)(2,1)}), bf16[16,8,512]{2,1,0:T(8,128)(2,1)S(1)}, u32[]{:S(2)}, u32[]{:S(2)}) async-start(bf16[16,8,512]{2,1,0:T(8,128)(2,1)} %bitcast.13), calls=%async_computation.2 | async-start | bytes 262144 | tf_op jit(solution)/shard_map/all_to_all | solution.py:410
  67.8 0.3 collective-permute-start.2
  68.1 4.3 %collective-permute-start.3 = (bf16[16,512]{1,0:T(8,128)(2,1)}, bf16[16,512]{1,0:T(8,128)(2,1)S(1)}, u32[]{:S(2)}, u32[]{:S(2)}) collective-permute-start(bf16[16,512]{1,0:T(8,128)(2,1)} %get-tuple-element.31), channel_id=1, source_target_pairs={{0,15},{1,0},{2,1},{3,2},{4,3},{5,4},{6,5},{7,6},{8,7},{9,8},{10,9... | collective-permute-start | bytes 49160 | tf_op jit(solution)/shard_map/ppermute | solution.py:418
  72.5 7.4 %local1.1.refs_5_ = f32[8,384,512]{2,1,0:T(8,128)} custom-call(s32[8,384]{1,0:T(8,128)} %bitcast.17, bf16[384,512]{1,0:T(8,128)(2,1)} %get-tuple-element.32.refs_1_.refs_6_, bf16[2,1536,512]{2,1,0:T(8,128)(2,1)} %refs_2_.7, bf16[384,512]{1,0:T(8,128)(2,1)} %get-tuple-element.33.refs_3_, bf16[8,384,512]{2,1,0:T(8,128)(2,1)} %get-tuple-element.34.refs_4_), custom_call_target="tpu_custom_call" | custom-call | flops 10000000000 | bytes 8388608 | tf_op jit(solution)/shard_map/local1/pallas_call | solution.py:137
  79.9 0.0 collective-permute-done.3.refs_3_
  80.0 0.5 copy-done.5
  80.5 0.0 copy-done.6
  80.5 0.1 copy-done.2
  80.6 10.1 %edge1.1 = bf16[384,512]{1,0:T(8,128)(2,1)} custom-call(s32[8,384]{1,0:T(8,128)} %bitcast.18, bf16[128,512]{1,0:T(8,128)(2,1)} %bitcast.12, bf16[16,512]{1,0:T(8,128)(2,1)} %copy-done.5, bf16[16,512]{1,0:T(8,128)(2,1)} %copy-done.6, bf16[2,512,512]{2,1,0:T(8,128)(2,1)} %refs_4_.7, f32[8,384,512]{2,1,0:T(8,128)} %local1.1.refs_5_, ...), custom_call_target="tpu_custom_call" | custom-call | flops 1000000000 | bytes 8388608 | tf_op jit(solution)/shard_map/edge1/pallas_call | solution.py:137
  (11 shorter events, 0.0 us)
Async XLA Ops:
  2.3 21.9 %all-to-all-start = ((bf16[16,32,512]{2,1,0:T(8,128)(2,1)}), bf16[16,32,512]{2,1,0:T(8,128)(2,1)S(1)}, u32[]{:S(2)}, u32[]{:S(2)}) async-start(bf16[16,32,512]{2,1,0:T(8,128)(2,1)} %bitcast.11), calls=%async_computation | async-start | bytes 1048576 | tf_op jit(solution)/shard_map/all_to_all | solution.py:410
  24.2 0.8 copy-start
  33.6 16.2 %all-to-all-start.1 = ((bf16[16,8,512]{2,1,0:T(8,128)(2,1)}), bf16[16,8,512]{2,1,0:T(8,128)(2,1)S(1)}, u32[]{:S(2)}, u32[]{:S(2)}) async-start(bf16[16,8,512]{2,1,0:T(8,128)(2,1)} %bitcast.14), calls=%async_computation.1 | async-start | bytes 262144 | tf_op jit(solution)/shard_map/all_to_all | solution.py:410
  37.7 12.1 %collective-permute-start = (bf16[16,512]{1,0:T(8,128)(2,1)}, bf16[16,512]{1,0:T(8,128)(2,1)S(1)}, u32[]{:S(2)}, u32[]{:S(2)}) collective-permute-start(bf16[16,512]{1,0:T(8,128)(2,1)} %get-tuple-element.24), channel_id=1, source_target_pairs={{0,1},{1,2},{2,3},{3,4},{4,5},{5,6},{6,7},{7,8},{8,9},{9,10},{10,1... | collective-permute-start | bytes 49160 | tf_op jit(solution)/shard_map/ppermute | solution.py:417
  38.1 11.7 %collective-permute-start.1 = (bf16[16,512]{1,0:T(8,128)(2,1)}, bf16[16,512]{1,0:T(8,128)(2,1)S(1)}, u32[]{:S(2)}, u32[]{:S(2)}) collective-permute-start(bf16[16,512]{1,0:T(8,128)(2,1)} %get-tuple-element.25), channel_id=1, source_target_pairs={{0,15},{1,0},{2,1},{3,2},{4,3},{5,4},{6,5},{7,6},{8,7},{9,8},{10,9... | collective-permute-start | bytes 49160 | tf_op jit(solution)/shard_map/ppermute | solution.py:418
  49.8 0.6 copy-start.3
  49.8 0.6 copy-start.4
  49.9 0.7 copy-start.1
  64.3 15.7 %all-to-all-start.2 = ((bf16[16,8,512]{2,1,0:T(8,128)(2,1)}), bf16[16,8,512]{2,1,0:T(8,128)(2,1)S(1)}, u32[]{:S(2)}, u32[]{:S(2)}) async-start(bf16[16,8,512]{2,1,0:T(8,128)(2,1)} %bitcast.13), calls=%async_computation.2 | async-start | bytes 262144 | tf_op jit(solution)/shard_map/all_to_all | solution.py:410
  67.8 12.1 %collective-permute-start.2 = (bf16[16,512]{1,0:T(8,128)(2,1)}, bf16[16,512]{1,0:T(8,128)(2,1)S(1)}, u32[]{:S(2)}, u32[]{:S(2)}) collective-permute-start(bf16[16,512]{1,0:T(8,128)(2,1)} %get-tuple-element.30), channel_id=1, source_target_pairs={{0,1},{1,2},{2,3},{3,4},{4,5},{5,6},{6,7},{7,8},{8,9},{9,10},{10,1... | collective-permute-start | bytes 49160 | tf_op jit(solution)/shard_map/ppermute | solution.py:417
  68.1 11.8 %collective-permute-start.3 = (bf16[16,512]{1,0:T(8,128)(2,1)}, bf16[16,512]{1,0:T(8,128)(2,1)S(1)}, u32[]{:S(2)}, u32[]{:S(2)}) collective-permute-start(bf16[16,512]{1,0:T(8,128)(2,1)} %get-tuple-element.31), channel_id=1, source_target_pairs={{0,15},{1,0},{2,1},{3,2},{4,3},{5,4},{6,5},{7,6},{8,7},{9,8},{10,9... | collective-permute-start | bytes 49160 | tf_op jit(solution)/shard_map/ppermute | solution.py:418
  79.9 0.6 copy-start.5
  79.9 0.6 copy-start.6
  80.0 0.7 copy-start.2
where the time goes:
time: 91.5 us; the launch traced here: 90.9 us
  Pallas kernels  55.7 us (61%)
  starting transfers between devices  24.3 us (27%)
  waiting for transfers between devices  8.46 us (9%)
  local copies, waits for them, and re-layouts  2.11 us (2%)
    pallas_call x7, Pallas kernels, run(): pl.pallas_call(whole, out_shape=[jax.ShapeDtypeStruct(out[0], out[1]) for...  55.7 us
    all_to_all x3, starting transfers between devices, exchange(): lax.all_to_all(values, 'rows', split_axis=0, concat_axis=0, tiled=True)  15 us
    ppermute x2, starting transfers between devices, halo(): from_after = lax.ppermute(outgoing[2], 'rows', down)  8.55 us
    all_to_all x3, waiting for transfers between devices, exchange(): lax.all_to_all(values, 'rows', split_axis=0, concat_axis=0, tiled=True)  8.45 us
    unnamed x14, local copies, waits for them, and re-layouts  2.11 us
  transfers between devices with their start and end apart: 7, of which 1 were waited for; matrix products, arithmetic and copies ran while one was open for 0% of the time, Pallas kernels for 23%

commit v1 on v0

--- a/solution.py
+++ b/solution.py
@@ -88,6 +88,12 @@
     for out in outs:
         out_starts.append(out_total)
         out_total += out[2]
+    start_order = [(i, 0) for i in range(n_in) if plans[i][2] == 1]
+    split = [i for i in range(n_in) if plans[i][2] > 1]
+    if split:
+        at = len([i for i in range(split[0]) if plans[i][2] == 1])
+        pieces = [(i, piece) for piece in range(plans[split[0]][2]) for i in split]
+        start_order[at:at] = pieces
     arrays, places = [], []
     for plan in plans:
         known = [i for i, array in enumerate(arrays) if array is plan[0]]
@@ -103,15 +109,14 @@
         rest = refs[len(arrays) + n_out :]
         in_vmem, out_vmem = rest[:n_in], rest[n_in : n_in + n_out]
         in_sems, out_sems = rest[n_in + n_out : n_in + n_out + 2]
-        loads = []
-        for i, (array, take, count, shape) in enumerate(plans):
+        loads = [[None] * count for _, _, count, _ in plans]
+        for i, piece in start_order:
+            _, take, count, _ = plans[i]
             source = ins[places[i]]
-            pieces = []
-            for piece in range(count):
-                view = source if take is None else take(source.at, piece)
-                target = in_vmem[i] if count == 1 else in_vmem[i].at[piece]
-                pieces.append(Load(view, target, in_sems.at[starts[i] + piece]))
-            loads.append(pieces[0] if count == 1 else pieces)
+            view = source if take is None else take(source.at, piece)
+            target = in_vmem[i] if count == 1 else in_vmem[i].at[piece]
+            loads[i][piece] = Load(view, target, in_sems.at[starts[i] + piece])
+        loads = [pieces if len(pieces) > 1 else pieces[0] for pieces in loads]
         pending = []
 
         def store(i, value, piece=None):
@@ -129,7 +134,7 @@
         for copy in pending:
             copy.wait()
 
-    spec = pl.BlockSpec(memory_space=pl.ANY)
+    spec = pl.BlockSpec(memory_space=pltpu.HBM)
     in_scratch = [
         pltpu.VMEM(shape if count == 1 else (count,) + shape, array.dtype)
         for array, _, count, shape in plans
@@ -202,8 +207,8 @@
     store(0, dot(select, columns[...], 1, 1).astype(bf16))
 
 
-def side_kernel(far, loads, store, pieces, turned, table):
-    features, embed, start, link_receiver, update_start, lists = loads
+def side_kernel(loads, store, pieces, turned, table):
+    features, embed, edge_first, start, link_receiver, update_start, lists = loads
     owned, width = start.target.shape
     edges = features.target.shape[1]
     degree = edges // owned
@@ -217,24 +222,20 @@
     matrix = table[...].astype(bf16)
     for j in range(degree):
         left = turned[pl.ds(j, owned, stride=degree), :].astype(bf16)
-        store(0, normalize(silu(dot(left, matrix))).astype(bf16), j)
-    store(1, dot(start()[...], link_receiver()[...]).astype(bf16))
-    store(2, dot(start()[...], update_start()[...]))
+        edge_state = normalize(silu(dot(left, matrix))).astype(bf16)
+        store(0, edge_state, j)
+        store(1, dot(edge_state, edge_first()[...]).astype(bf16), j)
+    store(2, dot(start()[...], link_receiver()[...]).astype(bf16))
+    store(3, dot(start()[...], update_start()[...]))
     lists = lists()[0]
-    me = lax.axis_index("rows")
-    rows = devices * far + 2 * slots
+    rows = devices * slots
     row = iota((rows, 1), 0)
-    near = row - devices * far
-    after = (me + 1) % devices
-    before = (me + devices - 1) % devices
-    reader = jnp.where(near < 0, row // far, jnp.where(near < slots, after, before))
-    place = jnp.where(near < 0, row % far, near % slots)
-    picks = jnp.where(iota((rows, devices), 1) == reader, 1.0, 0.0).astype(bf16)
+    picks = jnp.where(iota((rows, devices), 1) == row // slots, 1.0, 0.0).astype(bf16)
     high = dot(picks, (lists >> 4).astype(f32).astype(bf16))
     low = dot(picks, (lists & 15).astype(f32).astype(bf16))
-    chosen = jnp.where(iota((rows, slots), 1) == place, high * 16.0 + low, 0.0)
+    chosen = jnp.where(iota((rows, slots), 1) == row % slots, high * 16.0 + low, 0.0)
     column = jnp.sum(chosen, axis=1, keepdims=True).astype(jnp.int32)
-    store(3, jnp.where(iota((rows, owned), 1) == column, 1.0, 0.0).astype(bf16))
+    store(4, jnp.where(iota((rows, owned), 1) == column, 1.0, 0.0).astype(bf16))
 
 
 def update(state, summand, second, gain):
@@ -242,17 +243,13 @@
     return (state.astype(f32) + gain * normalize(dot(hidden, second))).astype(bf16)
 
 
-def send(store, base, state, sender, select, devices, far, slots):
+def send(store, base, state, sender, select):
     sent = dot(state, sender).astype(bf16)
-    outgoing = dot(select, sent).astype(bf16)
-    count = devices * far
-    store(base + 1, outgoing[0:count])
-    store(base + 2, outgoing[count : count + slots])
-    store(base + 3, outgoing[count + slots : count + 2 * slots])
-    store(base, sent)
-
-
-def link_kernel(sizes, loads, store, first, table, messages):
+    store(base, dot(select, sent).astype(bf16))
+    store(base + 1, sent)
+
+
+def link_kernel(loads, store, first, table, messages):
     (
         terms,
         embed_first,
@@ -308,56 +305,41 @@
     summand = base()[...] + dot(summed, update_first()[...])
     state = update(start()[...], summand, update_second()[...], gain()[0:1, :])
     store(0, state)
-    send(store, 1, state, sender_first()[...], select()[...], *sizes)
-
-
-def local_kernel(loads, store):
-    senders, state, receiver_first, sent, edge_first, edges = loads
+    send(store, 1, state, sender_first()[...], select()[...])
+
+
+def local_kernel(step, loads, store):
+    senders, state, receiver_first, sent = loads[:4]
+    parts = loads[-1]
     degree, owned = senders.target.shape
     columns = jnp.transpose(senders()[...].astype(f32)).astype(jnp.int32)
     kept = dot(state()[...], receiver_first()[...]).astype(bf16).astype(f32)
     for j in range(degree):
         local = jnp.where(iota((owned, owned), 1) == columns[:, j : j + 1], 1.0, 0.0)
-        part = dot(local.astype(bf16), sent()[...]) + dot(edges[j]()[...], edge_first()[...])
-        store(0, part + kept, j)
-
-
-def edge_kernel(step, last, sizes, loads, store, table):
-    (senders, far_rows, from_before, from_after, second, sums) = loads[:6]
-    (state, state_first, summed_first, update_second, gain) = loads[6:11]
+        part = parts[j]()[...]
+        if step:
+            part = dot(part, loads[4]()[...])
+        part = dot(local.astype(bf16), sent()[...]) + part.astype(f32)
+        store(0, (part + kept).astype(bf16), j)
+
+
+def edge_kernel(step, last, loads, store):
+    senders, incoming, second, sums = loads[:4]
+    (state, state_first, summed_first, update_second, gain) = loads[4:9]
     if not last:
-        edges, sender_first, select = loads[11:]
-    devices, far, slots = sizes
+        edges, sender_first, select = loads[9:]
     degree, owned = senders.target.shape
-    count = devices * far
-    rows = table.shape[0]
-    me = lax.axis_index("rows")
-    after = (me + 1) % devices
-    before = (me + devices - 1) % devices
-    senders = senders()[...]
-    halo = senders - owned
-    owner = halo // slots
-    place = halo % slots
-    index = jnp.where(
-        owner == before,
-        count + place,
-        jnp.where(owner == after, count + slots + place, owner * far + place),
-    )
-    index = jnp.where(halo < 0, -1, index)
-    columns = jnp.transpose(index.astype(f32)).astype(jnp.int32)
-    table[count + 2 * slots :, :] = jnp.zeros((rows - count - 2 * slots, table.shape[1]), bf16)
-    table[0:count, :] = far_rows()[...]
-    table[count : count + slots, :] = from_before()[...]
-    table[count + slots : count + 2 * slots, :] = from_after()[...]
+    rows = incoming.target.shape[0]
+    columns = jnp.transpose((senders()[...] - owned).astype(f32)).astype(jnp.int32)
     total = jnp.zeros(state.target.shape, f32)
     for j in range(degree):
         pick = jnp.where(iota((owned, rows), 1) == columns[:, j : j + 1], 1.0, 0.0)
-        summand = sums[j]()[...] + dot(pick.astype(bf16), table[...])
+        summand = sums[j]()[...].astype(f32) + dot(pick.astype(bf16), incoming()[...])
         hidden = silu(summand).astype(bf16)
         message = normalize(dot(hidden, second()[...])).astype(bf16).astype(f32)
         total = total + message
         if not last:
-            store(5, (edges[j]()[...].astype(f32) + message).astype(bf16), j)
+            store(3, (edges[j]()[...].astype(f32) + message).astype(bf16), j)
     summand = dot(state()[...], state_first()[...]) + dot(
         total.astype(bf16), summed_first()[...]
     )
@@ -366,7 +348,7 @@
     )
     store(0, state)
     if not last:
-        send(store, 1, state, sender_first()[...], select()[...], *sizes)
+        send(store, 1, state, sender_first()[...], select()[...])
 
 
 def body(
@@ -400,9 +382,7 @@
     degree = edge_senders.shape[1]
     edges = owned * degree
     halo_slots = halo_lists.shape[2]
-    far = 8
-    sizes = (devices, far, halo_slots)
-    halo_rows = devices * far + 2 * halo_slots
+    halo_rows = devices * halo_slots
     senders = edge_senders.T
 
     def exchange(values):
@@ -411,19 +391,7 @@
             -1, width
         )
 
-    def halo(outgoing):
-        up = [(i, (i + 1) % devices) for i in range(devices)]
-        down = [(i, (i + devices - 1) % devices) for i in range(devices)]
-        from_before = lax.ppermute(outgoing[1], "rows", up)
-        from_after = lax.ppermute(outgoing[2], "rows", down)
-        return exchange(outgoing[0]), from_before, from_after
-
-    sending = [
-        ((owned, width), bf16, 1),
-        ((devices * far, width), bf16, 1),
-        ((halo_slots, width), bf16, 1),
-        ((halo_slots, width), bf16, 1),
-    ]
+    sending = [((halo_rows, width), bf16, 1), ((owned, width), bf16, 1)]
     (packed,) = run(
         functools.partial(pack_kernel, devices),
         "pack",
@@ -432,10 +400,11 @@
         [pltpu.VMEM((width, links), bf16), pltpu.VMEM((EXTRA, links), f32)],
     )
     terms = exchange(packed)
-    edge_state, receiver, base, select = run(
-        functools.partial(side_kernel, far),
+    edge_state, parts, receiver, base, select = run(
+        side_kernel,
         "side",
         [
+            ((degree, owned, width), bf16, degree),
             ((degree, owned, width), bf16, degree),
             ((owned, width), bf16, 1),
             ((owned, width), f32, 1),
@@ -444,6 +413,7 @@
         (
             edge_features,
             edge_embed,
+            (process_first, rows_of(2 * width, 3 * width, 0), 1),
             mesh_start,
             (link_first, rows_of(width, 2 * width), 1),
             (update_first, rows_of(0, width), 1),
@@ -456,8 +426,8 @@
         ],
         flops=10**10,
     )
-    state, sent, *outgoing = run(
-        functools.partial(link_kernel, sizes),
+    state, outgoing, sent = run(
+        link_kernel,
         "link",
         [((owned, width), bf16, 1)] + sending,
         (
@@ -486,19 +456,20 @@
     steps = process_first.shape[0]
     for step in range(steps):
         last = step + 1 == steps
-        incoming = halo(outgoing)
+        incoming = exchange(outgoing)
+        extra = [] if step == 0 else [(process_first, rows_of(2 * width, 3 * width, step), 1)]
         (sums,) = run(
-            local_kernel,
+            functools.partial(local_kernel, step),
             f"local{step}",
-            [((degree, owned, width), f32, degree)],
-            (
+            [((degree, owned, width), bf16, degree)],
+            [
                 senders,
                 state,
                 (process_first, rows_of(width, 2 * width, step), 1),
                 sent,
-                (process_first, rows_of(2 * width, 3 * width, step), 1),
-                (edge_state, piece_of, degree),
-            ),
+            ]
+            + extra
+            + [(parts, piece_of, degree)],
             flops=10**10,
         )
         outs = [((owned, width), bf16, 1)]
@@ -511,12 +482,12 @@
                 select,
             ]
         results = run(
-            functools.partial(edge_kernel, step, last, sizes),
+            functools.partial(edge_kernel, step, last),
             f"edge{step}",
             outs,
             [
                 senders,
-                *incoming,
+                incoming,
                 (process_second, fixed(step), 1),
                 (sums, piece_of, degree),
                 state,
@@ -526,11 +497,11 @@
                 update_gain,
             ]
             + extra,
-            [pltpu.VMEM((-(-halo_rows // 128) * 128, width), bf16)],
         )
         if last:
             return results[0]
-        state, sent, *outgoing, edge_state = results
+        state, outgoing, sent, edge_state = results
+        parts = edge_state
 
 
 def solution(mesh):

time: 91.5 us -> 86.1 us (0.941)
  starting transfers between devices: 24.3 us -> 15.3 us
  waiting for transfers between devices: 8.46 us -> 12.8 us
    ppermute x4 -> x0, starting transfers between devices: 9.25 us -> none  [the longest x2 8.55 us: halo(): from_after = lax.ppermute(outgoing[2], 'rows', down)]
    all_to_all x3, waiting for transfers between devices: 8.45 us -> 12.8 us  [exchange(): lax.all_to_all(values, 'rows', split_axis=0, concat_axis=0, tiled=True)]
    unnamed x14 -> x6, local copies, waits for them, and re-layouts: 2.11 us -> 2.21 us
  transfers between devices with their start and end apart: 7 -> 3, of which waited for: 1 -> 3; matrix products, arithmetic and copies ran while one was open for 0% -> 0% of each run, Pallas kernels for 23% -> 25%
where the time goes in v1:
time: 86.1 us; the launch traced here: 85.4 us
  Pallas kernels  54.8 us (64%)
  starting transfers between devices  15.3 us (18%)
  waiting for transfers between devices  12.8 us (15%)
  local copies, waits for them, and re-layouts  2.21 us (3%)
    pallas_call x7, Pallas kernels, run(): pl.pallas_call(whole, out_shape=[jax.ShapeDtypeStruct(out[0], out[1]) for...  54.8 us
    all_to_all x3, starting transfers between devices, exchange(): lax.all_to_all(values, 'rows', split_axis=0, concat_axis=0, tiled=True)  15.3 us
    all_to_all x3, waiting for transfers between devices, exchange(): lax.all_to_all(values, 'rows', split_axis=0, concat_axis=0, tiled=True)  12.8 us
    unnamed x6, local copies, waits for them, and re-layouts  2.21 us
  transfers between devices with their start and end apart: 3, of which 3 were waited for; matrix products, arithmetic and copies ran while one was open for 0% of the time, Pallas kernels for 25%

profile of v1, /device:TPU:0, one launch (start us, length us, event | category | flops | bytes accessed | tf_op | source)
XLA Modules:
  0.0 85.4 jit_solution(10206322688281873744)
XLA Ops:
  0.0 2.3 %pack.1 = bf16[512,512]{1,0:T(8,128)(2,1)} custom-call(bf16[474,128]{1,0:T(8,128)(2,1)} %refs_0_.2, f32[4,256]{1,0:T(4,128)} %refs_1_.3, s32[2,128]{1,0:T(2,128)} %bitcast.19, s32[2,128]{1,0:T(2,128)} %bitcast.20), custom_call_target="tpu_custom_call" | custom-call | flops 1000000000 | bytes 8388608 | tf_op jit(solution)/shard_map/pack/pallas_call | solution.py:142
  2.3 7.4 %all-to-all-start = ((bf16[16,32,512]{2,1,0:T(8,128)(2,1)}), bf16[16,32,512]{2,1,0:T(8,128)(2,1)S(1)}, u32[]{:S(2)}, u32[]{:S(2)}) async-start(bf16[16,32,512]{2,1,0:T(8,128)(2,1)} %bitcast.12), calls=%async_computation | async-start | bytes 1048576 | tf_op jit(solution)/shard_map/all_to_all | solution.py:390
  9.7 8.7 %side.1 = (bf16[8,384,512]{2,1,0:T(8,128)(2,1)}, bf16[8,384,512]{2,1,0:T(8,128)(2,1)}, bf16[384,512]{1,0:T(8,128)(2,1)}, f32[384,512]{1,0:T(8,128)}, bf16[256,384]{1,0:T(8,128)(2,1)}) custom-call(f32[4,3072]{1,0:T(4,128)} %refs_0_.3, f32[4,512]{1,0:T(4,128)} %refs_1_.4, bf16[2,1536,512]{2,1,0:T(8,128)(2,1)} %refs_2_.10, bf16[384,512]{1,0:T(8,128)(2,1)} %refs_11_.1, ...), custom_call_target="tpu_custom_call" | custom-call | flops 10000000000 | bytes 8388608 | tf_op jit(solution)/shard_map/side/pallas_call | solution.py:142
  18.5 5.7 %all-to-all-done = bf16[16,32,512]{2,1,0:T(8,128)(2,1)S(1)} async-done(((bf16[16,32,512]{2,1,0:T(8,128)(2,1)}), bf16[16,32,512]{2,1,0:T(8,128)(2,1)S(1)}, u32[]{:S(2)}, u32[]{:S(2)}) %all-to-all-start) | async-done | bytes 524320 | tf_op jit(solution)/shard_map/all_to_all | solution.py:390
  24.2 0.0 copy-start
  24.2 0.8 copy-done
  25.0 8.6 %link.1 = (bf16[384,512]{1,0:T(8,128)(2,1)}, bf16[256,512]{1,0:T(8,128)(2,1)}, bf16[384,512]{1,0:T(8,128)(2,1)}) custom-call(bf16[512,512]{1,0:T(8,128)(2,1)} %bitcast.9, bf16[474,512]{1,0:T(8,128)(2,1)} %refs_1_.5, bf16[512,512]{1,0:T(8,128)(2,1)} %refs_2_.7, f32[4,512]{1,0:T(4,128)} %refs_3_.3, bf16[1536,512]{1,0:T(8,128)(2,1)} %refs_4_.3, ...), custom_call_target="tpu_custom_call" | custom-call | flops 1000000000 | bytes 8388608 | tf_op jit(solution)/shard_map/link/pallas_call | solution.py:142
  33.6 4.1 %all-to-all-start.1 = ((bf16[16,16,512]{2,1,0:T(8,128)(2,1)}), bf16[16,16,512]{2,1,0:T(8,128)(2,1)S(1)}, u32[]{:S(2)}, u32[]{:S(2)}) async-start(bf16[16,16,512]{2,1,0:T(8,128)(2,1)} %bitcast.14), calls=%async_computation.1 | async-start | bytes 524288 | tf_op jit(solution)/shard_map/all_to_all | solution.py:390
  37.7 5.5 %local0.1.refs_3_ = bf16[8,384,512]{2,1,0:T(8,128)(2,1)} custom-call(s32[8,384]{1,0:T(8,128)} %bitcast.15, bf16[384,512]{1,0:T(8,128)(2,1)} %get-tuple-element.21.refs_1_.refs_4_, bf16[2,1536,512]{2,1,0:T(8,128)(2,1)} %refs_2_.10, bf16[384,512]{1,0:T(8,128)(2,1)} %get-tuple-element.22.refs_3_, bf16[8,384,512]{2,1,0:T(8,128)(2,1)} %get-tuple-element.23.refs_4_), custom_call_target="tpu_custom_call" | custom-call | flops 10000000000 | bytes 8388608 | tf_op jit(solution)/shard_map/local0/pallas_call | solution.py:142
  43.3 4.5 %all-to-all-done.1 = bf16[16,16,512]{2,1,0:T(8,128)(2,1)S(1)} async-done(((bf16[16,16,512]{2,1,0:T(8,128)(2,1)}), bf16[16,16,512]{2,1,0:T(8,128)(2,1)S(1)}, u32[]{:S(2)}, u32[]{:S(2)}) %all-to-all-start.1) | async-done | bytes 262176 | tf_op jit(solution)/shard_map/all_to_all | solution.py:390
  47.8 0.0 copy-start.1
  47.8 0.7 copy-done.1
  48.5 12.4 %edge0.1 = (bf16[384,512]{1,0:T(8,128)(2,1)}, bf16[256,512]{1,0:T(8,128)(2,1)}, bf16[384,512]{1,0:T(8,128)(2,1)}, bf16[8,384,512]{2,1,0:T(8,128)(2,1)}) custom-call(s32[8,384]{1,0:T(8,128)} %bitcast.16, bf16[256,512]{1,0:T(8,128)(2,1)} %bitcast.10, bf16[2,512,512]{2,1,0:T(8,128)(2,1)} %refs_2_.11, bf16[8,384,512]{2,1,0:T(8,128)(2,1)} %local0.1.refs_3_, ...), custom_call_target="tpu_custom_call" | custom-call | flops 1000000000 | bytes 8388608 | tf_op jit(solution)/shard_map/edge0/pallas_call | solution.py:142
  60.9 3.8 %all-to-all-start.2 = ((bf16[16,16,512]{2,1,0:T(8,128)(2,1)}), bf16[16,16,512]{2,1,0:T(8,128)(2,1)S(1)}, u32[]{:S(2)}, u32[]{:S(2)}) async-start(bf16[16,16,512]{2,1,0:T(8,128)(2,1)} %bitcast.13), calls=%async_computation.2 | async-start | bytes 524288 | tf_op jit(solution)/shard_map/all_to_all | solution.py:390
  64.7 7.2 %local1.1.refs_3_ = bf16[8,384,512]{2,1,0:T(8,128)(2,1)} custom-call(s32[8,384]{1,0:T(8,128)} %bitcast.17, bf16[384,512]{1,0:T(8,128)(2,1)} %get-tuple-element.26.refs_1_.refs_4_, bf16[2,1536,512]{2,1,0:T(8,128)(2,1)} %refs_2_.10, bf16[384,512]{1,0:T(8,128)(2,1)} %get-tuple-element.27.refs_3_, bf16[8,384,512]{2,1,0:T(8,128)(2,1)} %get-tuple-element.28.refs_4_), custom_call_target="tpu_custom_call" | custom-call | flops 10000000000 | bytes 8388608 | tf_op jit(solution)/shard_map/local1/pallas_call | solution.py:142
  71.9 2.6 %all-to-all-done.2 = bf16[16,16,512]{2,1,0:T(8,128)(2,1)S(1)} async-done(((bf16[16,16,512]{2,1,0:T(8,128)(2,1)}), bf16[16,16,512]{2,1,0:T(8,128)(2,1)S(1)}, u32[]{:S(2)}, u32[]{:S(2)}) %all-to-all-start.2) | async-done | bytes 262176 | tf_op jit(solution)/shard_map/all_to_all | solution.py:390
  74.5 0.0 copy-start.2
  74.5 0.7 copy-done.2
  75.2 10.0 %edge1.1 = bf16[384,512]{1,0:T(8,128)(2,1)} custom-call(s32[8,384]{1,0:T(8,128)} %bitcast.18, bf16[256,512]{1,0:T(8,128)(2,1)} %bitcast.11, bf16[2,512,512]{2,1,0:T(8,128)(2,1)} %refs_2_.11, bf16[8,384,512]{2,1,0:T(8,128)(2,1)} %local1.1.refs_3_, bf16[384,512]{1,0:T(8,128)(2,1)} %get-tuple-element.26.refs_1_.refs_4_, bf16[2,1024,512]{2,1,0:T(8,128)(2,1)} %refs_5_.5, ...), custom_call_target="tpu_custom_call" | custom-call | flops 1000000000 | bytes 8388608 | tf_op jit(solution)/shard_map/edge1/pallas_call | solution.py:142
Async XLA Ops:
  2.3 21.9 %all-to-all-start = ((bf16[16,32,512]{2,1,0:T(8,128)(2,1)}), bf16[16,32,512]{2,1,0:T(8,128)(2,1)S(1)}, u32[]{:S(2)}, u32[]{:S(2)}) async-start(bf16[16,32,512]{2,1,0:T(8,128)(2,1)} %bitcast.12), calls=%async_computation | async-start | bytes 1048576 | tf_op jit(solution)/shard_map/all_to_all | solution.py:390
  24.2 0.8 copy-start
  33.6 14.2 %all-to-all-start.1 = ((bf16[16,16,512]{2,1,0:T(8,128)(2,1)}), bf16[16,16,512]{2,1,0:T(8,128)(2,1)S(1)}, u32[]{:S(2)}, u32[]{:S(2)}) async-start(bf16[16,16,512]{2,1,0:T(8,128)(2,1)} %bitcast.14), calls=%async_computation.1 | async-start | bytes 524288 | tf_op jit(solution)/shard_map/all_to_all | solution.py:390
  47.8 0.7 copy-start.1
  60.9 13.6 %all-to-all-start.2 = ((bf16[16,16,512]{2,1,0:T(8,128)(2,1)}), bf16[16,16,512]{2,1,0:T(8,128)(2,1)S(1)}, u32[]{:S(2)}, u32[]{:S(2)}) async-start(bf16[16,16,512]{2,1,0:T(8,128)(2,1)} %bitcast.13), calls=%async_computation.2 | async-start | bytes 524288 | tf_op jit(solution)/shard_map/all_to_all | solution.py:390
  74.5 0.7 copy-start.2

commit v2 on v1

--- a/solution.py
+++ b/solution.py
@@ -12,6 +12,7 @@
 bf16 = jnp.bfloat16
 MIB = 2**20
 EXTRA = 32
+CHUNK = 32
 
 
 def dot(left, right, left_dim=1, right_dim=0):
@@ -122,7 +123,10 @@
         def store(i, value, piece=None):
             target = out_vmem[i] if piece is None else out_vmem[i].at[piece]
             out = out_refs[i] if piece is None else out_refs[i].at[piece]
-            target[...] = value
+            if callable(value):
+                value(target)
+            else:
+                target[...] = value
             copy = pltpu.make_async_copy(target, out, out_sems.at[out_starts[i] + (piece or 0)])
             copy.start()
             pending.append(copy)
@@ -308,9 +312,9 @@
     send(store, 1, state, sender_first()[...], select()[...])
 
 
-def local_kernel(step, loads, store):
+def local_kernel(step, last, loads, store):
     senders, state, receiver_first, sent = loads[:4]
-    parts = loads[-1]
+    parts = loads[5 if step else 4]
     degree, owned = senders.target.shape
     columns = jnp.transpose(senders()[...].astype(f32)).astype(jnp.int32)
     kept = dot(state()[...], receiver_first()[...]).astype(bf16).astype(f32)
@@ -318,36 +322,64 @@
         local = jnp.where(iota((owned, owned), 1) == columns[:, j : j + 1], 1.0, 0.0)
         part = parts[j]()[...]
         if step:
-            part = dot(part, loads[4]()[...])
+            edge_state = (part.astype(f32) + loads[6][j]()[...].astype(f32)).astype(bf16)
+            if not last:
+                store(1, edge_state, j)
+            part = dot(edge_state, loads[4]()[...])
         part = dot(local.astype(bf16), sent()[...]) + part.astype(f32)
         store(0, (part + kept).astype(bf16), j)
 
 
-def edge_kernel(step, last, loads, store):
+def edge_kernel(step, last, loads, store, summands, hiddens, results, total):
     senders, incoming, second, sums = loads[:4]
     (state, state_first, summed_first, update_second, gain) = loads[4:9]
-    if not last:
-        edges, sender_first, select = loads[9:]
     degree, owned = senders.target.shape
     rows = incoming.target.shape[0]
     columns = jnp.transpose((senders()[...] - owned).astype(f32)).astype(jnp.int32)
-    total = jnp.zeros(state.target.shape, f32)
+
+    def lead(j):
+        pick = jnp.where(iota((owned, rows), 1) == columns[:, j : j + 1], 1.0, 0.0)
+        summands[j % 2] = dot(pick.astype(bf16), incoming()[...])
+
+    def middle(j):
+        part = sums[j]()
+        for begin in range(0, owned, CHUNK):
+            some = slice(begin, begin + CHUNK)
+            summand = part[some, :].astype(f32) + summands[j % 2, some, :]
+            hiddens[j % 2, some, :] = silu(summand).astype(bf16)
+        results[j % 2] = dot(hiddens[j % 2], second()[...])
+
+    def tail(j):
+        def fill(target):
+            for begin in range(0, owned, CHUNK):
+                some = slice(begin, begin + CHUNK)
+                message = normalize(results[j % 2, some, :]).astype(bf16)
+                if target is not None:
+                    target[some, :] = message
+                message = message.astype(f32)
+                total[some, :] = message if j == 0 else total[some, :] + message
+
+        if last:
+            fill(None)
+        else:
+            store(3, fill, j)
+
+    lead(0)
+    middle(0)
     for j in range(degree):
-        pick = jnp.where(iota((owned, rows), 1) == columns[:, j : j + 1], 1.0, 0.0)
-        summand = sums[j]()[...].astype(f32) + dot(pick.astype(bf16), incoming()[...])
-        hidden = silu(summand).astype(bf16)
-        message = normalize(dot(hidden, second()[...])).astype(bf16).astype(f32)
-        total = total + message
-        if not last:
-            store(3, (edges[j]()[...].astype(f32) + message).astype(bf16), j)
+        if j + 1 < degree:
+            lead(j + 1)
+            middle(j + 1)
+        tail(j)
     summand = dot(state()[...], state_first()[...]) + dot(
-        total.astype(bf16), summed_first()[...]
+        total[...].astype(bf16), summed_first()[...]
     )
     state = update(
         state()[...], summand, update_second()[...], gain()[step + 1 : step + 2, :]
     )
     store(0, state)
     if not last:
+        sender_first, select = loads[9:]
         send(store, 1, state, sender_first()[...], select()[...])
 
 
@@ -457,11 +489,14 @@
     for step in range(steps):
         last = step + 1 == steps
         incoming = exchange(outgoing)
-        extra = [] if step == 0 else [(process_first, rows_of(2 * width, 3 * width, step), 1)]
-        (sums,) = run(
-            functools.partial(local_kernel, step),
+        extra = []
+        if step:
+            extra = [(process_first, rows_of(2 * width, 3 * width, step), 1)]
+            parts = edge_state
+        (sums, *kept) = run(
+            functools.partial(local_kernel, step, last),
             f"local{step}",
-            [((degree, owned, width), bf16, degree)],
+            [((degree, owned, width), bf16, degree)] * (1 if last or step == 0 else 2),
             [
                 senders,
                 state,
@@ -469,18 +504,17 @@
                 sent,
             ]
             + extra
-            + [(parts, piece_of, degree)],
+            + [(parts, piece_of, degree)]
+            + ([(message, piece_of, degree)] if step else []),
             flops=10**10,
         )
+        if kept:
+            edge_state = kept[0]
         outs = [((owned, width), bf16, 1)]
         extra = []
         if not last:
             outs += sending + [((degree, owned, width), bf16, degree)]
-            extra = [
-                (edge_state, piece_of, degree),
-                (process_first, rows_of(0, width, step + 1), 1),
-                select,
-            ]
+            extra = [(process_first, rows_of(0, width, step + 1), 1), select]
         results = run(
             functools.partial(edge_kernel, step, last),
             f"edge{step}",
@@ -497,11 +531,16 @@
                 update_gain,
             ]
             + extra,
+            [
+                pltpu.VMEM((2, owned, width), f32),
+                pltpu.VMEM((2, owned, width), bf16),
+                pltpu.VMEM((2, owned, width), f32),
+                pltpu.VMEM((owned, width), f32),
+            ],
         )
         if last:
             return results[0]
-        state, outgoing, sent, edge_state = results
-        parts = edge_state
+        state, outgoing, sent, message = results
 
 
 def solution(mesh):

time: 86.1 us -> 81.8 us (0.950)
  Pallas kernels: 54.8 us -> 51.2 us
    pallas_call x7, Pallas kernels: 54.8 us -> 51.2 us  [run(): pl.pallas_call(whole, out_shape=[jax.ShapeDtypeStruct(out[0], out[1]) for...]
  transfers between devices with their start and end apart: 3 -> 3, of which waited for: 3 -> 3; matrix products, arithmetic and copies ran while one was open for 0% -> 0% of each run, Pallas kernels for 25% -> 27%
where the time goes in v2:
time: 81.8 us; the launch traced here: 81.1 us
  Pallas kernels  51.2 us (63%)
  starting transfers between devices  15.3 us (19%)
  waiting for transfers between devices  12.2 us (15%)
  local copies, waits for them, and re-layouts  2.2 us (3%)
    pallas_call x7, Pallas kernels, run(): pl.pallas_call(whole, out_shape=[jax.ShapeDtypeStruct(out[0], out[1]) for...  51.2 us
    all_to_all x3, starting transfers between devices, exchange(): lax.all_to_all(values, 'rows', split_axis=0, concat_axis=0, tiled=True)  15.3 us
    all_to_all x3, waiting for transfers between devices, exchange(): lax.all_to_all(values, 'rows', split_axis=0, concat_axis=0, tiled=True)  12.2 us
    unnamed x6, local copies, waits for them, and re-layouts  2.2 us
  transfers between devices with their start and end apart: 3, of which 3 were waited for; matrix products, arithmetic and copies ran while one was open for 0% of the time, Pallas kernels for 27%

profile of v2, /device:TPU:0, one launch (start us, length us, event | category | flops | bytes accessed | tf_op | source)
XLA Modules:
  0.0 81.1 jit_solution(12787080620331174612)
XLA Ops:
  0.0 2.3 %pack.1 = bf16[512,512]{1,0:T(8,128)(2,1)} custom-call(bf16[474,128]{1,0:T(8,128)(2,1)} %refs_0_.2, f32[4,256]{1,0:T(4,128)} %refs_1_.3, s32[2,128]{1,0:T(2,128)} %bitcast.19, s32[2,128]{1,0:T(2,128)} %bitcast.20), custom_call_target="tpu_custom_call" | custom-call | flops 1000000000 | bytes 8388608 | tf_op jit(solution)/shard_map/pack/pallas_call | solution.py:146
  2.3 7.4 %all-to-all-start = ((bf16[16,32,512]{2,1,0:T(8,128)(2,1)}), bf16[16,32,512]{2,1,0:T(8,128)(2,1)S(1)}, u32[]{:S(2)}, u32[]{:S(2)}) async-start(bf16[16,32,512]{2,1,0:T(8,128)(2,1)} %bitcast.12), calls=%async_computation | async-start | bytes 1048576 | tf_op jit(solution)/shard_map/all_to_all | solution.py:422
  9.7 8.7 %side.1 = (bf16[8,384,512]{2,1,0:T(8,128)(2,1)}, bf16[8,384,512]{2,1,0:T(8,128)(2,1)}, bf16[384,512]{1,0:T(8,128)(2,1)}, f32[384,512]{1,0:T(8,128)}, bf16[256,384]{1,0:T(8,128)(2,1)}) custom-call(f32[4,3072]{1,0:T(4,128)} %refs_0_.3, f32[4,512]{1,0:T(4,128)} %refs_1_.4, bf16[2,1536,512]{2,1,0:T(8,128)(2,1)} %refs_2_.10, bf16[384,512]{1,0:T(8,128)(2,1)} %refs_11_.1, ...), custom_call_target="tpu_custom_call" | custom-call | flops 10000000000 | bytes 8388608 | tf_op jit(solution)/shard_map/side/pallas_call | solution.py:146
  18.5 5.7 %all-to-all-done = bf16[16,32,512]{2,1,0:T(8,128)(2,1)S(1)} async-done(((bf16[16,32,512]{2,1,0:T(8,128)(2,1)}), bf16[16,32,512]{2,1,0:T(8,128)(2,1)S(1)}, u32[]{:S(2)}, u32[]{:S(2)}) %all-to-all-start) | async-done | bytes 524320 | tf_op jit(solution)/shard_map/all_to_all | solution.py:422
  24.2 0.0 copy-start
  24.2 0.8 copy-done
  25.0 8.6 %link.1 = (bf16[384,512]{1,0:T(8,128)(2,1)}, bf16[256,512]{1,0:T(8,128)(2,1)}, bf16[384,512]{1,0:T(8,128)(2,1)}) custom-call(bf16[512,512]{1,0:T(8,128)(2,1)} %bitcast.9, bf16[474,512]{1,0:T(8,128)(2,1)} %refs_1_.5, bf16[512,512]{1,0:T(8,128)(2,1)} %refs_2_.7, f32[4,512]{1,0:T(4,128)} %refs_3_.3, bf16[1536,512]{1,0:T(8,128)(2,1)} %refs_4_.3, ...), custom_call_target="tpu_custom_call" | custom-call | flops 1000000000 | bytes 8388608 | tf_op jit(solution)/shard_map/link/pallas_call | solution.py:146
  33.6 4.1 %all-to-all-start.1 = ((bf16[16,16,512]{2,1,0:T(8,128)(2,1)}), bf16[16,16,512]{2,1,0:T(8,128)(2,1)S(1)}, u32[]{:S(2)}, u32[]{:S(2)}) async-start(bf16[16,16,512]{2,1,0:T(8,128)(2,1)} %bitcast.14), calls=%async_computation.1 | async-start | bytes 524288 | tf_op jit(solution)/shard_map/all_to_all | solution.py:422
  37.7 5.5 %local0.1.refs_3_ = bf16[8,384,512]{2,1,0:T(8,128)(2,1)} custom-call(s32[8,384]{1,0:T(8,128)} %bitcast.15, bf16[384,512]{1,0:T(8,128)(2,1)} %get-tuple-element.21.refs_1_.refs_4_, bf16[2,1536,512]{2,1,0:T(8,128)(2,1)} %refs_2_.10, bf16[384,512]{1,0:T(8,128)(2,1)} %get-tuple-element.22.refs_3_, bf16[8,384,512]{2,1,0:T(8,128)(2,1)} %get-tuple-element.23.refs_4_), custom_call_target="tpu_custom_call" | custom-call | flops 10000000000 | bytes 8388608 | tf_op jit(solution)/shard_map/local0/pallas_call | solution.py:146
  43.3 4.5 %all-to-all-done.1 = bf16[16,16,512]{2,1,0:T(8,128)(2,1)S(1)} async-done(((bf16[16,16,512]{2,1,0:T(8,128)(2,1)}), bf16[16,16,512]{2,1,0:T(8,128)(2,1)S(1)}, u32[]{:S(2)}, u32[]{:S(2)}) %all-to-all-start.1) | async-done | bytes 262176 | tf_op jit(solution)/shard_map/all_to_all | solution.py:422
  47.8 0.0 copy-start.1
  47.8 0.7 copy-done.1
  48.5 9.5 %edge0.1 = (bf16[384,512]{1,0:T(8,128)(2,1)}, bf16[256,512]{1,0:T(8,128)(2,1)}, bf16[384,512]{1,0:T(8,128)(2,1)}, bf16[8,384,512]{2,1,0:T(8,128)(2,1)}) custom-call(s32[8,384]{1,0:T(8,128)} %bitcast.16, bf16[256,512]{1,0:T(8,128)(2,1)} %bitcast.10, bf16[2,512,512]{2,1,0:T(8,128)(2,1)} %refs_2_.11, bf16[8,384,512]{2,1,0:T(8,128)(2,1)} %local0.1.refs_3_, ...), custom_call_target="tpu_custom_call" | custom-call | flops 1000000000 | bytes 8388608 | tf_op jit(solution)/shard_map/edge0/pallas_call | solution.py:146
  58.1 3.8 %all-to-all-start.2 = ((bf16[16,16,512]{2,1,0:T(8,128)(2,1)}), bf16[16,16,512]{2,1,0:T(8,128)(2,1)S(1)}, u32[]{:S(2)}, u32[]{:S(2)}) async-start(bf16[16,16,512]{2,1,0:T(8,128)(2,1)} %bitcast.13), calls=%async_computation.2 | async-start | bytes 524288 | tf_op jit(solution)/shard_map/all_to_all | solution.py:422
  61.8 7.8 %local1.1.refs_3_ = bf16[8,384,512]{2,1,0:T(8,128)(2,1)} custom-call(s32[8,384]{1,0:T(8,128)} %bitcast.17, bf16[384,512]{1,0:T(8,128)(2,1)} %get-tuple-element.25.refs_1_.refs_4_, bf16[2,1536,512]{2,1,0:T(8,128)(2,1)} %refs_2_.10, bf16[384,512]{1,0:T(8,128)(2,1)} %get-tuple-element.26.refs_3_, bf16[8,384,512]{2,1,0:T(8,128)(2,1)} %get-tuple-element.27.refs_4_, ...), custom_call_target="tpu_custom_call" | custom-call | flops 10000000000 | bytes 8388608 | tf_op jit(solution)/shard_map/local1/pallas_call | solution.py:146
  69.7 1.9 %all-to-all-done.2 = bf16[16,16,512]{2,1,0:T(8,128)(2,1)S(1)} async-done(((bf16[16,16,512]{2,1,0:T(8,128)(2,1)}), bf16[16,16,512]{2,1,0:T(8,128)(2,1)S(1)}, u32[]{:S(2)}, u32[]{:S(2)}) %all-to-all-start.2) | async-done | bytes 262176 | tf_op jit(solution)/shard_map/all_to_all | solution.py:422
  71.6 0.0 copy-start.2
  71.6 0.7 copy-done.2
  72.3 8.6 %edge1.1 = bf16[384,512]{1,0:T(8,128)(2,1)} custom-call(s32[8,384]{1,0:T(8,128)} %bitcast.18, bf16[256,512]{1,0:T(8,128)(2,1)} %bitcast.11, bf16[2,512,512]{2,1,0:T(8,128)(2,1)} %refs_2_.11, bf16[8,384,512]{2,1,0:T(8,128)(2,1)} %local1.1.refs_3_, bf16[384,512]{1,0:T(8,128)(2,1)} %get-tuple-element.25.refs_1_.refs_4_, bf16[2,1024,512]{2,1,0:T(8,128)(2,1)} %refs_5_.5, ...), custom_call_target="tpu_custom_call" | custom-call | flops 1000000000 | bytes 8388608 | tf_op jit(solution)/shard_map/edge1/pallas_call | solution.py:146
Async XLA Ops:
  2.3 21.9 %all-to-all-start = ((bf16[16,32,512]{2,1,0:T(8,128)(2,1)}), bf16[16,32,512]{2,1,0:T(8,128)(2,1)S(1)}, u32[]{:S(2)}, u32[]{:S(2)}) async-start(bf16[16,32,512]{2,1,0:T(8,128)(2,1)} %bitcast.12), calls=%async_computation | async-start | bytes 1048576 | tf_op jit(solution)/shard_map/all_to_all | solution.py:422
  24.2 0.8 copy-start
  33.6 14.2 %all-to-all-start.1 = ((bf16[16,16,512]{2,1,0:T(8,128)(2,1)}), bf16[16,16,512]{2,1,0:T(8,128)(2,1)S(1)}, u32[]{:S(2)}, u32[]{:S(2)}) async-start(bf16[16,16,512]{2,1,0:T(8,128)(2,1)} %bitcast.14), calls=%async_computation.1 | async-start | bytes 524288 | tf_op jit(solution)/shard_map/all_to_all | solution.py:422
  47.8 0.7 copy-start.1
  58.1 13.6 %all-to-all-start.2 = ((bf16[16,16,512]{2,1,0:T(8,128)(2,1)}), bf16[16,16,512]{2,1,0:T(8,128)(2,1)S(1)}, u32[]{:S(2)}, u32[]{:S(2)}) async-start(bf16[16,16,512]{2,1,0:T(8,128)(2,1)} %bitcast.13), calls=%async_computation.2 | async-start | bytes 524288 | tf_op jit(solution)/shard_map/all_to_all | solution.py:422
  71.6 0.7 copy-start.2

commit v3 on v2

--- a/solution.py
+++ b/solution.py
@@ -53,6 +53,14 @@
 
 LEFT_ORDER = (0, 0, 0, 1, 1, 2)
 RIGHT_ORDER = (0, 1, 2, 0, 1, 0)
+
+
+class Held:
+    def __init__(self, target):
+        self.target = target
+
+    def __call__(self):
+        return self.target
 
 
 class Load:
@@ -110,7 +118,10 @@
         rest = refs[len(arrays) + n_out :]
         in_vmem, out_vmem = rest[:n_in], rest[n_in : n_in + n_out]
         in_sems, out_sems = rest[n_in + n_out : n_in + n_out + 2]
-        loads = [[None] * count for _, _, count, _ in plans]
+        loads = [[None] * max(count, 1) for _, _, count, _ in plans]
+        for i, (_, _, count, _) in enumerate(plans):
+            if count == 0:
+                loads[i][0] = Held(ins[places[i]])
         for i, piece in start_order:
             _, take, count, _ = plans[i]
             source = ins[places[i]]
@@ -123,10 +134,14 @@
         def store(i, value, piece=None):
             target = out_vmem[i] if piece is None else out_vmem[i].at[piece]
             out = out_refs[i] if piece is None else out_refs[i].at[piece]
+            if outs[i][2] == 0:
+                target = out
             if callable(value):
                 value(target)
             else:
                 target[...] = value
+            if outs[i][2] == 0:
+                return
             copy = pltpu.make_async_copy(target, out, out_sems.at[out_starts[i] + (piece or 0)])
             copy.start()
             pending.append(copy)
@@ -138,19 +153,30 @@
         for copy in pending:
             copy.wait()
 
-    spec = pl.BlockSpec(memory_space=pltpu.HBM)
-    in_scratch = [
-        pltpu.VMEM(shape if count == 1 else (count,) + shape, array.dtype)
-        for array, _, count, shape in plans
+    hbm = pl.BlockSpec(memory_space=pltpu.HBM)
+    vmem = pl.BlockSpec(memory_space=pltpu.VMEM)
+    held = [
+        any(place == i and plan[2] == 0 for place, plan in zip(places, plans))
+        for i in range(len(arrays))
     ]
+
+    def room(shape, dtype, count):
+        if count == 0:
+            return pltpu.VMEM((8, 128), f32)
+        return pltpu.VMEM(shape if count == 1 else (count,) + shape, dtype)
+
+    in_scratch = [room(shape, array.dtype, count) for array, _, count, shape in plans]
     return pl.pallas_call(
         whole,
         out_shape=[jax.ShapeDtypeStruct(out[0], out[1]) for out in outs],
-        in_specs=[spec] * len(arrays),
-        out_specs=[spec] * n_out,
+        in_specs=[vmem if here else hbm for here in held],
+        out_specs=[hbm if out[2] else vmem for out in outs],
         scratch_shapes=in_scratch
-        + [pltpu.VMEM(out[0], out[1]) for out in outs]
-        + [pltpu.SemaphoreType.DMA((total,)), pltpu.SemaphoreType.DMA((out_total,))]
+        + [room(out[0], out[1], min(out[2], 1)) for out in outs]
+        + [
+            pltpu.SemaphoreType.DMA((max(total, 1),)),
+            pltpu.SemaphoreType.DMA((max(out_total, 1),)),
+        ]
         + list(scratch),
         compiler_params=pltpu.CompilerParams(vmem_limit_bytes=60 * MIB),
         cost_estimate=pl.CostEstimate(flops=flops, bytes_accessed=8 * MIB, transcendentals=0),
@@ -312,22 +338,44 @@
     send(store, 1, state, sender_first()[...], select()[...])
 
 
-def local_kernel(step, last, loads, store):
+def local_kernel(step, last, loads, store, summands, kept, edges):
     senders, state, receiver_first, sent = loads[:4]
     parts = loads[5 if step else 4]
     degree, owned = senders.target.shape
     columns = jnp.transpose(senders()[...].astype(f32)).astype(jnp.int32)
-    kept = dot(state()[...], receiver_first()[...]).astype(bf16).astype(f32)
+    kept[...] = dot(state()[...], receiver_first()[...]).astype(bf16).astype(f32)
+
+    def lead(j):
+        local = jnp.where(iota((owned, owned), 1) == columns[:, j : j + 1], 1.0, 0.0)
+        summand = dot(local.astype(bf16), sent()[...])
+        if step:
+            target = edges.at[j]
+            old, message = parts[j](), loads[6][j]()
+            for begin in range(0, owned, CHUNK):
+                some = slice(begin, begin + CHUNK)
+                edge_state = old[some, :].astype(f32) + message[some, :].astype(f32)
+                target[some, :] = edge_state.astype(bf16)
+            if not last:
+                store(1, target[...], j)
+            summand = summand + dot(target[...], loads[4]()[...])
+        summands[j % 2] = summand
+
+    def tail(j):
+        def fill(target):
+            for begin in range(0, owned, CHUNK):
+                some = slice(begin, begin + CHUNK)
+                summand = summands[j % 2, some, :] + kept[some, :]
+                if not step:
+                    summand = summand + parts[j]()[some, :].astype(f32)
+                target[some, :] = summand.astype(bf16)
+
+        store(0, fill, j)
+
+    lead(0)
     for j in range(degree):
-        local = jnp.where(iota((owned, owned), 1) == columns[:, j : j + 1], 1.0, 0.0)
-        part = parts[j]()[...]
-        if step:
-            edge_state = (part.astype(f32) + loads[6][j]()[...].astype(f32)).astype(bf16)
-            if not last:
-                store(1, edge_state, j)
-            part = dot(edge_state, loads[4]()[...])
-        part = dot(local.astype(bf16), sent()[...]) + part.astype(f32)
-        store(0, (part + kept).astype(bf16), j)
+        if j + 1 < degree:
+            lead(j + 1)
+        tail(j)
 
 
 def edge_kernel(step, last, loads, store, summands, hiddens, results, total):
@@ -423,11 +471,11 @@
             -1, width
         )
 
-    sending = [((halo_rows, width), bf16, 1), ((owned, width), bf16, 1)]
+    sending = [((halo_rows, width), bf16, 0), ((owned, width), bf16, 0)]
     (packed,) = run(
         functools.partial(pack_kernel, devices),
         "pack",
-        [((slots, width), bf16, 1)],
+        [((slots, width), bf16, 0)],
         (grid_inputs, link_features, link_partition.T, link_node.T),
         [pltpu.VMEM((width, links), bf16), pltpu.VMEM((EXTRA, links), f32)],
     )
@@ -461,9 +509,9 @@
     state, outgoing, sent = run(
         link_kernel,
         "link",
-        [((owned, width), bf16, 1)] + sending,
+        [((owned, width), bf16, 0)] + sending,
         (
-            terms,
+            (terms, None, 0),
             embed_first,
             embed_second,
             link_embed,
@@ -493,24 +541,29 @@
         if step:
             extra = [(process_first, rows_of(2 * width, 3 * width, step), 1)]
             parts = edge_state
-        (sums, *kept) = run(
+        (sums, *later) = run(
             functools.partial(local_kernel, step, last),
             f"local{step}",
             [((degree, owned, width), bf16, degree)] * (1 if last or step == 0 else 2),
             [
                 senders,
-                state,
+                (state, None, 0),
                 (process_first, rows_of(width, 2 * width, step), 1),
-                sent,
+                (sent, None, 0),
             ]
             + extra
             + [(parts, piece_of, degree)]
             + ([(message, piece_of, degree)] if step else []),
+            [
+                pltpu.VMEM((2, owned, width), f32),
+                pltpu.VMEM((owned, width), f32),
+                pltpu.VMEM((degree, owned, width), bf16),
+            ],
             flops=10**10,
         )
-        if kept:
-            edge_state = kept[0]
-        outs = [((owned, width), bf16, 1)]
+        if later:
+            edge_state = later[0]
+        outs = [((owned, width), bf16, 1 if last else 0)]
         extra = []
         if not last:
             outs += sending + [((degree, owned, width), bf16, degree)]
@@ -521,10 +574,10 @@
             outs,
             [
                 senders,
-                incoming,
+                (incoming, None, 0),
                 (process_second, fixed(step), 1),
                 (sums, piece_of, degree),
-                state,
+                (state, None, 0),
                 (process_update_first, rows_of(0, width, step), 1),
                 (process_update_first, rows_of(width, 2 * width, step), 1),
                 (process_update_second, fixed(step), 1),

time: 81.8 us -> 84.9 us (1.038)
  Pallas kernels: 51.2 us -> 56.6 us
  waiting for transfers between devices: 12.2 us -> 9.92 us
    pallas_call x7, Pallas kernels: 51.2 us -> 56.6 us  [run(): pl.pallas_call(whole, out_shape=[jax.ShapeDtypeStruct(out[0], out[1]) for...]
    all_to_all x3, waiting for transfers between devices: 12.2 us -> 9.92 us  [exchange(): lax.all_to_all(values, 'rows', split_axis=0, concat_axis=0, tiled=True)]
  transfers between devices with their start and end apart: 3 -> 3, of which waited for: 3 -> 3; matrix products, arithmetic and copies ran while one was open for 0% -> 0% of each run, Pallas kernels for 27% -> 29%
where the time goes in v3:
time: 84.9 us; the launch traced here: 84.2 us
  Pallas kernels  56.6 us (67%)
  starting transfers between devices  15.3 us (18%)
  waiting for transfers between devices  9.92 us (12%)
  local copies, waits for them, and re-layouts  2.2 us (3%)
    pallas_call x7, Pallas kernels, run(): pl.pallas_call(whole, out_shape=[jax.ShapeDtypeStruct(out[0], out[1]) for...  56.6 us
    all_to_all x3, starting transfers between devices, exchange(): lax.all_to_all(values, 'rows', split_axis=0, concat_axis=0, tiled=True)  15.3 us
    all_to_all x3, waiting for transfers between devices, exchange(): lax.all_to_all(values, 'rows', split_axis=0, concat_axis=0, tiled=True)  9.92 us
    unnamed x6, local copies, waits for them, and re-layouts  2.2 us
  transfers between devices with their start and end apart: 3, of which 3 were waited for; matrix products, arithmetic and copies ran while one was open for 0% of the time, Pallas kernels for 29%

profile of v3, /device:TPU:0, one launch (start us, length us, event | category | flops | bytes accessed | tf_op | source)
XLA Modules:
  0.0 84.2 jit_solution(4912062350745132089)
XLA Ops:
  0.0 2.3 %pack.1 = bf16[512,512]{1,0:T(8,128)(2,1)} custom-call(bf16[474,128]{1,0:T(8,128)(2,1)} %refs_0_.2, f32[4,256]{1,0:T(4,128)} %refs_1_.3, s32[2,128]{1,0:T(2,128)} %bitcast.19, s32[2,128]{1,0:T(2,128)} %bitcast.20), custom_call_target="tpu_custom_call" | custom-call | flops 1000000000 | bytes 8388608 | tf_op jit(solution)/shard_map/pack/pallas_call | solution.py:169
  2.3 7.4 %all-to-all-start = ((bf16[16,32,512]{2,1,0:T(8,128)(2,1)}), bf16[16,32,512]{2,1,0:T(8,128)(2,1)S(1)}, u32[]{:S(2)}, u32[]{:S(2)}) async-start(bf16[16,32,512]{2,1,0:T(8,128)(2,1)} %bitcast.12), calls=%async_computation | async-start | bytes 1048576 | tf_op jit(solution)/shard_map/all_to_all | solution.py:470
  9.7 8.7 %side.1 = (bf16[8,384,512]{2,1,0:T(8,128)(2,1)}, bf16[8,384,512]{2,1,0:T(8,128)(2,1)}, bf16[384,512]{1,0:T(8,128)(2,1)}, f32[384,512]{1,0:T(8,128)}, bf16[256,384]{1,0:T(8,128)(2,1)}) custom-call(f32[4,3072]{1,0:T(4,128)} %refs_0_.3, f32[4,512]{1,0:T(4,128)} %refs_1_.4, bf16[2,1536,512]{2,1,0:T(8,128)(2,1)} %refs_2_.10, bf16[384,512]{1,0:T(8,128)(2,1)} %refs_11_.1, ...), custom_call_target="tpu_custom_call" | custom-call | flops 10000000000 | bytes 8388608 | tf_op jit(solution)/shard_map/side/pallas_call | solution.py:169
  18.5 5.7 %all-to-all-done = bf16[16,32,512]{2,1,0:T(8,128)(2,1)S(1)} async-done(((bf16[16,32,512]{2,1,0:T(8,128)(2,1)}), bf16[16,32,512]{2,1,0:T(8,128)(2,1)S(1)}, u32[]{:S(2)}, u32[]{:S(2)}) %all-to-all-start) | async-done | bytes 524320 | tf_op jit(solution)/shard_map/all_to_all | solution.py:470
  24.2 0.0 copy-start
  24.2 0.8 copy-done
  25.0 9.5 %link.1 = (bf16[384,512]{1,0:T(8,128)(2,1)}, bf16[256,512]{1,0:T(8,128)(2,1)}, bf16[384,512]{1,0:T(8,128)(2,1)}) custom-call(bf16[512,512]{1,0:T(8,128)(2,1)} %bitcast.9, bf16[474,512]{1,0:T(8,128)(2,1)} %refs_1_.5, bf16[512,512]{1,0:T(8,128)(2,1)} %refs_2_.7, f32[4,512]{1,0:T(4,128)} %refs_3_.3, bf16[1536,512]{1,0:T(8,128)(2,1)} %refs_4_.3, ...), custom_call_target="tpu_custom_call" | custom-call | flops 1000000000 | bytes 8388608 | tf_op jit(solution)/shard_map/link/pallas_call | solution.py:169
  34.5 4.1 %all-to-all-start.1 = ((bf16[16,16,512]{2,1,0:T(8,128)(2,1)}), bf16[16,16,512]{2,1,0:T(8,128)(2,1)S(1)}, u32[]{:S(2)}, u32[]{:S(2)}) async-start(bf16[16,16,512]{2,1,0:T(8,128)(2,1)} %bitcast.14), calls=%async_computation.1 | async-start | bytes 524288 | tf_op jit(solution)/shard_map/all_to_all | solution.py:470
  38.6 6.9 %local0.1.refs_3_ = bf16[8,384,512]{2,1,0:T(8,128)(2,1)} custom-call(s32[8,384]{1,0:T(8,128)} %bitcast.15, bf16[384,512]{1,0:T(8,128)(2,1)} %get-tuple-element.21.refs_1_.refs_4_, bf16[2,1536,512]{2,1,0:T(8,128)(2,1)} %refs_2_.10, bf16[384,512]{1,0:T(8,128)(2,1)} %get-tuple-element.22.refs_3_, bf16[8,384,512]{2,1,0:T(8,128)(2,1)} %get-tuple-element.23.refs_4_), custom_call_target="tpu_custom_call" | custom-call | flops 10000000000 | bytes 8388608 | tf_op jit(solution)/shard_map/local0/pallas_call | solution.py:169
  45.5 3.1 %all-to-all-done.1 = bf16[16,16,512]{2,1,0:T(8,128)(2,1)S(1)} async-done(((bf16[16,16,512]{2,1,0:T(8,128)(2,1)}), bf16[16,16,512]{2,1,0:T(8,128)(2,1)S(1)}, u32[]{:S(2)}, u32[]{:S(2)}) %all-to-all-start.1) | async-done | bytes 262176 | tf_op jit(solution)/shard_map/all_to_all | solution.py:470
  48.7 0.0 copy-start.1
  48.7 0.7 copy-done.1
  49.4 10.7 %edge0.1 = (bf16[384,512]{1,0:T(8,128)(2,1)}, bf16[256,512]{1,0:T(8,128)(2,1)}, bf16[384,512]{1,0:T(8,128)(2,1)}, bf16[8,384,512]{2,1,0:T(8,128)(2,1)}) custom-call(s32[8,384]{1,0:T(8,128)} %bitcast.16, bf16[256,512]{1,0:T(8,128)(2,1)} %bitcast.10, bf16[2,512,512]{2,1,0:T(8,128)(2,1)} %refs_2_.11, bf16[8,384,512]{2,1,0:T(8,128)(2,1)} %local0.1.refs_3_, ...), custom_call_target="tpu_custom_call" | custom-call | flops 1000000000 | bytes 8388608 | tf_op jit(solution)/shard_map/edge0/pallas_call | solution.py:169
  60.1 3.8 %all-to-all-start.2 = ((bf16[16,16,512]{2,1,0:T(8,128)(2,1)}), bf16[16,16,512]{2,1,0:T(8,128)(2,1)S(1)}, u32[]{:S(2)}, u32[]{:S(2)}) async-start(bf16[16,16,512]{2,1,0:T(8,128)(2,1)} %bitcast.13), calls=%async_computation.2 | async-start | bytes 524288 | tf_op jit(solution)/shard_map/all_to_all | solution.py:470
  63.9 8.7 %local1.1.refs_3_ = bf16[8,384,512]{2,1,0:T(8,128)(2,1)} custom-call(s32[8,384]{1,0:T(8,128)} %bitcast.17, bf16[384,512]{1,0:T(8,128)(2,1)} %get-tuple-element.25.refs_1_.refs_4_, bf16[2,1536,512]{2,1,0:T(8,128)(2,1)} %refs_2_.10, bf16[384,512]{1,0:T(8,128)(2,1)} %get-tuple-element.26.refs_3_, bf16[8,384,512]{2,1,0:T(8,128)(2,1)} %get-tuple-element.27.refs_4_, ...), custom_call_target="tpu_custom_call" | custom-call | flops 10000000000 | bytes 8388608 | tf_op jit(solution)/shard_map/local1/pallas_call | solution.py:169
  72.6 1.1 %all-to-all-done.2 = bf16[16,16,512]{2,1,0:T(8,128)(2,1)S(1)} async-done(((bf16[16,16,512]{2,1,0:T(8,128)(2,1)}), bf16[16,16,512]{2,1,0:T(8,128)(2,1)S(1)}, u32[]{:S(2)}, u32[]{:S(2)}) %all-to-all-start.2) | async-done | bytes 262176 | tf_op jit(solution)/shard_map/all_to_all | solution.py:470
  73.7 0.0 copy-start.2
  73.7 0.7 copy-done.2
  74.4 9.7 %edge1.1 = bf16[384,512]{1,0:T(8,128)(2,1)} custom-call(s32[8,384]{1,0:T(8,128)} %bitcast.18, bf16[256,512]{1,0:T(8,128)(2,1)} %bitcast.11, bf16[2,512,512]{2,1,0:T(8,128)(2,1)} %refs_2_.11, bf16[8,384,512]{2,1,0:T(8,128)(2,1)} %local1.1.refs_3_, bf16[384,512]{1,0:T(8,128)(2,1)} %get-tuple-element.25.refs_1_.refs_4_, bf16[2,1024,512]{2,1,0:T(8,128)(2,1)} %refs_5_.5, ...), custom_call_target="tpu_custom_call" | custom-call | flops 1000000000 | bytes 8388608 | tf_op jit(solution)/shard_map/edge1/pallas_call | solution.py:169
Async XLA Ops:
  2.3 21.9 %all-to-all-start = ((bf16[16,32,512]{2,1,0:T(8,128)(2,1)}), bf16[16,32,512]{2,1,0:T(8,128)(2,1)S(1)}, u32[]{:S(2)}, u32[]{:S(2)}) async-start(bf16[16,32,512]{2,1,0:T(8,128)(2,1)} %bitcast.12), calls=%async_computation | async-start | bytes 1048576 | tf_op jit(solution)/shard_map/all_to_all | solution.py:470
  24.2 0.8 copy-start
  34.5 14.2 %all-to-all-start.1 = ((bf16[16,16,512]{2,1,0:T(8,128)(2,1)}), bf16[16,16,512]{2,1,0:T(8,128)(2,1)S(1)}, u32[]{:S(2)}, u32[]{:S(2)}) async-start(bf16[16,16,512]{2,1,0:T(8,128)(2,1)} %bitcast.14), calls=%async_computation.1 | async-start | bytes 524288 | tf_op jit(solution)/shard_map/all_to_all | solution.py:470
  48.7 0.7 copy-start.1
  60.1 13.6 %all-to-all-start.2 = ((bf16[16,16,512]{2,1,0:T(8,128)(2,1)}), bf16[16,16,512]{2,1,0:T(8,128)(2,1)S(1)}, u32[]{:S(2)}, u32[]{:S(2)}) async-start(bf16[16,16,512]{2,1,0:T(8,128)(2,1)} %bitcast.13), calls=%async_computation.2 | async-start | bytes 524288 | tf_op jit(solution)/shard_map/all_to_all | solution.py:470
  73.7 0.7 copy-start.2

commit v4 on v3

--- a/solution.py
+++ b/solution.py
@@ -178,7 +178,7 @@
             pltpu.SemaphoreType.DMA((max(out_total, 1),)),
         ]
         + list(scratch),
-        compiler_params=pltpu.CompilerParams(vmem_limit_bytes=60 * MIB),
+        compiler_params=pltpu.CompilerParams(vmem_limit_bytes=56 * MIB),
         cost_estimate=pl.CostEstimate(flops=flops, bytes_accessed=8 * MIB, transcendentals=0),
         name=name,
     )(*arrays)
@@ -471,11 +471,11 @@
             -1, width
         )
 
-    sending = [((halo_rows, width), bf16, 0), ((owned, width), bf16, 0)]
+    sending = [((halo_rows, width), bf16, 1), ((owned, width), bf16, 1)]
     (packed,) = run(
         functools.partial(pack_kernel, devices),
         "pack",
-        [((slots, width), bf16, 0)],
+        [((slots, width), bf16, 1)],
         (grid_inputs, link_features, link_partition.T, link_node.T),
         [pltpu.VMEM((width, links), bf16), pltpu.VMEM((EXTRA, links), f32)],
     )
@@ -509,7 +509,7 @@
     state, outgoing, sent = run(
         link_kernel,
         "link",
-        [((owned, width), bf16, 0)] + sending,
+        [((owned, width), bf16, 1)] + sending,
         (
             (terms, None, 0),
             embed_first,
@@ -547,9 +547,9 @@
             [((degree, owned, width), bf16, degree)] * (1 if last or step == 0 else 2),
             [
                 senders,
-                (state, None, 0),
+                state,
                 (process_first, rows_of(width, 2 * width, step), 1),
-                (sent, None, 0),
+                sent,
             ]
             + extra
             + [(parts, piece_of, degree)]
@@ -563,7 +563,7 @@
         )
         if later:
             edge_state = later[0]
-        outs = [((owned, width), bf16, 1 if last else 0)]
+        outs = [((owned, width), bf16, 1)]
         extra = []
         if not last:
             outs += sending + [((degree, owned, width), bf16, degree)]
@@ -577,7 +577,7 @@
                 (incoming, None, 0),
                 (process_second, fixed(step), 1),
                 (sums, piece_of, degree),
-                (state, None, 0),
+                state,
                 (process_update_first, rows_of(0, width, step), 1),
                 (process_update_first, rows_of(width, 2 * width, step), 1),
                 (process_update_second, fixed(step), 1),

time: 84.9 us -> 84.6 us (level)
  Pallas kernels: 56.6 us -> 54.6 us
  waiting for transfers between devices: 9.92 us -> 11.6 us
    pallas_call x7, Pallas kernels: 56.6 us -> 54.6 us  [run(): pl.pallas_call(whole, out_shape=[jax.ShapeDtypeStruct(out[0], out[1]) for...]
    all_to_all x3, waiting for transfers between devices: 9.92 us -> 11.6 us  [exchange(): lax.all_to_all(values, 'rows', split_axis=0, concat_axis=0, tiled=True)]
  transfers between devices with their start and end apart: 3 -> 3, of which waited for: 3 -> 3; matrix products, arithmetic and copies ran while one was open for 0% -> 0% of each run, Pallas kernels for 29% -> 27%
where the time goes in v4:
time: 84.6 us; the launch traced here: 83.9 us
  Pallas kernels  54.6 us (65%)
  starting transfers between devices  15.3 us (18%)
  waiting for transfers between devices  11.6 us (14%)
  local copies, waits for them, and re-layouts  2.2 us (3%)
    pallas_call x7, Pallas kernels, run(): pl.pallas_call(whole, out_shape=[jax.ShapeDtypeStruct(out[0], out[1]) for...  54.6 us
    all_to_all x3, starting transfers between devices, exchange(): lax.all_to_all(values, 'rows', split_axis=0, concat_axis=0, tiled=True)  15.3 us
    all_to_all x3, waiting for transfers between devices, exchange(): lax.all_to_all(values, 'rows', split_axis=0, concat_axis=0, tiled=True)  11.6 us
    unnamed x6, local copies, waits for them, and re-layouts  2.2 us
  transfers between devices with their start and end apart: 3, of which 3 were waited for; matrix products, arithmetic and copies ran while one was open for 0% of the time, Pallas kernels for 27%

profile of v4, /device:TPU:0, one launch (start us, length us, event | category | flops | bytes accessed | tf_op | source)
XLA Modules:
  0.0 83.9 jit_solution(12600930275519022690)
XLA Ops:
  0.0 2.3 %pack.1 = bf16[512,512]{1,0:T(8,128)(2,1)} custom-call(bf16[474,128]{1,0:T(8,128)(2,1)} %refs_0_.2, f32[4,256]{1,0:T(4,128)} %refs_1_.3, s32[2,128]{1,0:T(2,128)} %bitcast.19, s32[2,128]{1,0:T(2,128)} %bitcast.20), custom_call_target="tpu_custom_call" | custom-call | flops 1000000000 | bytes 8388608 | tf_op jit(solution)/shard_map/pack/pallas_call | solution.py:169
  2.3 7.4 %all-to-all-start = ((bf16[16,32,512]{2,1,0:T(8,128)(2,1)}), bf16[16,32,512]{2,1,0:T(8,128)(2,1)S(1)}, u32[]{:S(2)}, u32[]{:S(2)}) async-start(bf16[16,32,512]{2,1,0:T(8,128)(2,1)} %bitcast.12), calls=%async_computation | async-start | bytes 1048576 | tf_op jit(solution)/shard_map/all_to_all | solution.py:470
  9.7 8.7 %side.1 = (bf16[8,384,512]{2,1,0:T(8,128)(2,1)}, bf16[8,384,512]{2,1,0:T(8,128)(2,1)}, bf16[384,512]{1,0:T(8,128)(2,1)}, f32[384,512]{1,0:T(8,128)}, bf16[256,384]{1,0:T(8,128)(2,1)}) custom-call(f32[4,3072]{1,0:T(4,128)} %refs_0_.3, f32[4,512]{1,0:T(4,128)} %refs_1_.4, bf16[2,1536,512]{2,1,0:T(8,128)(2,1)} %refs_2_.10, bf16[384,512]{1,0:T(8,128)(2,1)} %refs_11_.1, ...), custom_call_target="tpu_custom_call" | custom-call | flops 10000000000 | bytes 8388608 | tf_op jit(solution)/shard_map/side/pallas_call | solution.py:169
  18.5 5.7 %all-to-all-done = bf16[16,32,512]{2,1,0:T(8,128)(2,1)S(1)} async-done(((bf16[16,32,512]{2,1,0:T(8,128)(2,1)}), bf16[16,32,512]{2,1,0:T(8,128)(2,1)S(1)}, u32[]{:S(2)}, u32[]{:S(2)}) %all-to-all-start) | async-done | bytes 524320 | tf_op jit(solution)/shard_map/all_to_all | solution.py:470
  24.2 0.0 copy-start
  24.2 0.8 copy-done
  25.0 9.5 %link.1 = (bf16[384,512]{1,0:T(8,128)(2,1)}, bf16[256,512]{1,0:T(8,128)(2,1)}, bf16[384,512]{1,0:T(8,128)(2,1)}) custom-call(bf16[512,512]{1,0:T(8,128)(2,1)} %bitcast.9, bf16[474,512]{1,0:T(8,128)(2,1)} %refs_1_.5, bf16[512,512]{1,0:T(8,128)(2,1)} %refs_2_.7, f32[4,512]{1,0:T(4,128)} %refs_3_.3, bf16[1536,512]{1,0:T(8,128)(2,1)} %refs_4_.3, ...), custom_call_target="tpu_custom_call" | custom-call | flops 1000000000 | bytes 8388608 | tf_op jit(solution)/shard_map/link/pallas_call | solution.py:169
  34.5 4.1 %all-to-all-start.1 = ((bf16[16,16,512]{2,1,0:T(8,128)(2,1)}), bf16[16,16,512]{2,1,0:T(8,128)(2,1)S(1)}, u32[]{:S(2)}, u32[]{:S(2)}) async-start(bf16[16,16,512]{2,1,0:T(8,128)(2,1)} %bitcast.14), calls=%async_computation.1 | async-start | bytes 524288 | tf_op jit(solution)/shard_map/all_to_all | solution.py:470
  38.6 6.1 %local0.1.refs_3_ = bf16[8,384,512]{2,1,0:T(8,128)(2,1)} custom-call(s32[8,384]{1,0:T(8,128)} %bitcast.15, bf16[384,512]{1,0:T(8,128)(2,1)} %get-tuple-element.21.refs_1_.refs_4_, bf16[2,1536,512]{2,1,0:T(8,128)(2,1)} %refs_2_.10, bf16[384,512]{1,0:T(8,128)(2,1)} %get-tuple-element.22.refs_3_, bf16[8,384,512]{2,1,0:T(8,128)(2,1)} %get-tuple-element.23.refs_4_), custom_call_target="tpu_custom_call" | custom-call | flops 10000000000 | bytes 8388608 | tf_op jit(solution)/shard_map/local0/pallas_call | solution.py:169
  44.7 3.9 %all-to-all-done.1 = bf16[16,16,512]{2,1,0:T(8,128)(2,1)S(1)} async-done(((bf16[16,16,512]{2,1,0:T(8,128)(2,1)}), bf16[16,16,512]{2,1,0:T(8,128)(2,1)S(1)}, u32[]{:S(2)}, u32[]{:S(2)}) %all-to-all-start.1) | async-done | bytes 262176 | tf_op jit(solution)/shard_map/all_to_all | solution.py:470
  48.7 0.0 copy-start.1
  48.7 0.7 copy-done.1
  49.4 10.5 %edge0.1 = (bf16[384,512]{1,0:T(8,128)(2,1)}, bf16[256,512]{1,0:T(8,128)(2,1)}, bf16[384,512]{1,0:T(8,128)(2,1)}, bf16[8,384,512]{2,1,0:T(8,128)(2,1)}) custom-call(s32[8,384]{1,0:T(8,128)} %bitcast.16, bf16[256,512]{1,0:T(8,128)(2,1)} %bitcast.10, bf16[2,512,512]{2,1,0:T(8,128)(2,1)} %refs_2_.11, bf16[8,384,512]{2,1,0:T(8,128)(2,1)} %local0.1.refs_3_, ...), custom_call_target="tpu_custom_call" | custom-call | flops 1000000000 | bytes 8388608 | tf_op jit(solution)/shard_map/edge0/pallas_call | solution.py:169
  59.9 3.8 %all-to-all-start.2 = ((bf16[16,16,512]{2,1,0:T(8,128)(2,1)}), bf16[16,16,512]{2,1,0:T(8,128)(2,1)S(1)}, u32[]{:S(2)}, u32[]{:S(2)}) async-start(bf16[16,16,512]{2,1,0:T(8,128)(2,1)} %bitcast.13), calls=%async_computation.2 | async-start | bytes 524288 | tf_op jit(solution)/shard_map/all_to_all | solution.py:470
  63.6 7.8 %local1.1.refs_3_ = bf16[8,384,512]{2,1,0:T(8,128)(2,1)} custom-call(s32[8,384]{1,0:T(8,128)} %bitcast.17, bf16[384,512]{1,0:T(8,128)(2,1)} %get-tuple-element.25.refs_1_.refs_4_, bf16[2,1536,512]{2,1,0:T(8,128)(2,1)} %refs_2_.10, bf16[384,512]{1,0:T(8,128)(2,1)} %get-tuple-element.26.refs_3_, bf16[8,384,512]{2,1,0:T(8,128)(2,1)} %get-tuple-element.27.refs_4_, ...), custom_call_target="tpu_custom_call" | custom-call | flops 10000000000 | bytes 8388608 | tf_op jit(solution)/shard_map/local1/pallas_call | solution.py:169
  71.5 1.9 %all-to-all-done.2 = bf16[16,16,512]{2,1,0:T(8,128)(2,1)S(1)} async-done(((bf16[16,16,512]{2,1,0:T(8,128)(2,1)}), bf16[16,16,512]{2,1,0:T(8,128)(2,1)S(1)}, u32[]{:S(2)}, u32[]{:S(2)}) %all-to-all-start.2) | async-done | bytes 262176 | tf_op jit(solution)/shard_map/all_to_all | solution.py:470
  73.4 0.0 copy-start.2
  73.4 0.7 copy-done.2
  74.1 9.6 %edge1.1 = bf16[384,512]{1,0:T(8,128)(2,1)} custom-call(s32[8,384]{1,0:T(8,128)} %bitcast.18, bf16[256,512]{1,0:T(8,128)(2,1)} %bitcast.11, bf16[2,512,512]{2,1,0:T(8,128)(2,1)} %refs_2_.11, bf16[8,384,512]{2,1,0:T(8,128)(2,1)} %local1.1.refs_3_, bf16[384,512]{1,0:T(8,128)(2,1)} %get-tuple-element.25.refs_1_.refs_4_, bf16[2,1024,512]{2,1,0:T(8,128)(2,1)} %refs_5_.5, ...), custom_call_target="tpu_custom_call" | custom-call | flops 1000000000 | bytes 8388608 | tf_op jit(solution)/shard_map/edge1/pallas_call | solution.py:169
Async XLA Ops:
  2.3 21.9 %all-to-all-start = ((bf16[16,32,512]{2,1,0:T(8,128)(2,1)}), bf16[16,32,512]{2,1,0:T(8,128)(2,1)S(1)}, u32[]{:S(2)}, u32[]{:S(2)}) async-start(bf16[16,32,512]{2,1,0:T(8,128)(2,1)} %bitcast.12), calls=%async_computation | async-start | bytes 1048576 | tf_op jit(solution)/shard_map/all_to_all | solution.py:470
  24.2 0.8 copy-start
  34.5 14.2 %all-to-all-start.1 = ((bf16[16,16,512]{2,1,0:T(8,128)(2,1)}), bf16[16,16,512]{2,1,0:T(8,128)(2,1)S(1)}, u32[]{:S(2)}, u32[]{:S(2)}) async-start(bf16[16,16,512]{2,1,0:T(8,128)(2,1)} %bitcast.14), calls=%async_computation.1 | async-start | bytes 524288 | tf_op jit(solution)/shard_map/all_to_all | solution.py:470
  48.7 0.7 copy-start.1
  59.9 13.6 %all-to-all-start.2 = ((bf16[16,16,512]{2,1,0:T(8,128)(2,1)}), bf16[16,16,512]{2,1,0:T(8,128)(2,1)S(1)}, u32[]{:S(2)}, u32[]{:S(2)}) async-start(bf16[16,16,512]{2,1,0:T(8,128)(2,1)} %bitcast.13), calls=%async_computation.2 | async-start | bytes 524288 | tf_op jit(solution)/shard_map/all_to_all | solution.py:470
  73.4 0.7 copy-start.2

commit v5 on v2

--- a/solution.py
+++ b/solution.py
@@ -23,6 +23,11 @@
 
 def silu(values):
     half = 0.5 * values
+    return half + half * jnp.tanh(half)
+
+
+def silu16(values):
+    half = (0.5 * values).astype(bf16)
     return half + half * jnp.tanh(half)
 
 
@@ -118,9 +123,9 @@
             target = in_vmem[i] if count == 1 else in_vmem[i].at[piece]
             loads[i][piece] = Load(view, target, in_sems.at[starts[i] + piece])
         loads = [pieces if len(pieces) > 1 else pieces[0] for pieces in loads]
-        pending = []
-
-        def store(i, value, piece=None):
+        pending, waiting = [], []
+
+        def store(i, value, piece=None, hold=False):
             target = out_vmem[i] if piece is None else out_vmem[i].at[piece]
             out = out_refs[i] if piece is None else out_refs[i].at[piece]
             if callable(value):
@@ -128,13 +133,22 @@
             else:
                 target[...] = value
             copy = pltpu.make_async_copy(target, out, out_sems.at[out_starts[i] + (piece or 0)])
-            copy.start()
-            pending.append(copy)
-
+            waiting.append(copy)
+            if not hold:
+                flush()
+
+        def flush():
+            for copy in waiting:
+                copy.start()
+            pending.extend(waiting)
+            waiting.clear()
+
+        store.flush = flush
         kernel(loads, store, *rest[n_in + n_out + 2 :])
         for pieces in loads:
             for load in pieces if isinstance(pieces, list) else [pieces]:
                 load()
+        flush()
         for copy in pending:
             copy.wait()
 
@@ -253,12 +267,12 @@
     store(base + 1, sent)
 
 
-def link_kernel(loads, store, first, table, messages):
+def link_kernel(loads, store, first, table, messages, hidden, edge_state, picks):
     (
         terms,
         embed_first,
+        link_embed,
         embed_second,
-        link_embed,
         link_sender,
         link_edge,
         receiver,
@@ -275,36 +289,48 @@
     slots = terms.target.shape[0]
     channels = embed_first.target.shape[0]
     tail = table.shape[0]
-    first[...] = jnp.zeros_like(first)
-    table[...] = jnp.zeros_like(table)
     lanes = iota((8, tail), 1)
     weights = jnp.where(
         lanes == tail - EXTRA + 24, 16.0, jnp.where(lanes == tail - EXTRA + 25, 1.0, 0.0)
     ).astype(bf16)
-    chunk = 256
+    chunks = [slice(begin, begin + 128) for begin in range(0, slots, 128)]
+
+    def each(values, function):
+        parts = [values[i : i + CHUNK, :] for i in range(0, values.shape[0], CHUNK)]
+        return jnp.concatenate([function(part).astype(bf16) for part in parts], axis=0)
+
+    table[...] = jnp.zeros_like(table)
+    first[channels // 16 * 16 :, :] = jnp.zeros((width - channels // 16 * 16, width), bf16)
     first[0:channels, :] = embed_first()[...]
     store_pieces(table, link_embed()[...], RIGHT_ORDER, tail - EXTRA)
     matrix = table[...].astype(bf16)
     terms = terms()
-    for begin in range(0, slots, chunk):
-        rows = slice(begin, begin + chunk)
+    for rows in chunks:
+        hidden[rows, :] = each(dot(terms[rows, :], first[...]), silu)
         extra = terms[rows, width - tail :]
-        hidden = silu(dot(terms[rows, :], first[...])).astype(bf16)
-        grid_state = normalize(dot(hidden, embed_second()[...])).astype(bf16)
-        sender = dot(grid_state, link_sender()[...]).astype(bf16).astype(f32)
-        link_state = normalize(silu(dot(extra, matrix))).astype(bf16)
-        link_terms = (sender + dot(link_state, link_edge()[...])).astype(bf16)
+        edge_state[rows, :] = each(dot(extra, matrix), lambda x: normalize(silu(x)))
         parts = extra.astype(f32)
         node = (
             parts[:, tail - EXTRA + 24 : tail - EXTRA + 25] * 16.0
             + parts[:, tail - EXTRA + 25 : tail - EXTRA + 26]
         ).astype(jnp.int32)
-        pick = jnp.where(iota((chunk, owned), 1) == node - 1, 1.0, 0.0).astype(bf16)
-        summand = link_terms.astype(f32) + dot(pick, receiver()[...])
-        message = normalize(dot(silu(summand).astype(bf16), link_second()[...]))
-        messages[rows, :] = message.astype(bf16)
+        pick = jnp.where(iota((rows.stop - rows.start, owned), 1) == node - 1, 1.0, 0.0)
+        picks[rows, :] = pick.astype(bf16)
     nodes = dot(weights, terms[:, width - tail :], 1, 1)[0:1, :].astype(jnp.int32)
     collect = jnp.where(iota((owned, slots), 0) == nodes - 1, 1.0, 0.0).astype(bf16)
+    for load in (embed_second, link_sender, link_edge, receiver, link_second):
+        load()
+    for rows in chunks:
+        hidden[rows, :] = each(dot(hidden[rows, :], embed_second()[...]), normalize)
+    for rows in chunks:
+        sender = dot(hidden[rows, :], link_sender()[...]).astype(bf16).astype(f32)
+        link_terms = (sender + dot(edge_state[rows, :], link_edge()[...])).astype(bf16)
+        summand = link_terms.astype(f32) + dot(picks[rows, :], receiver()[...])
+        hidden[rows, :] = each(summand, silu)
+    for rows in chunks:
+        messages[rows, :] = each(dot(hidden[rows, :], link_second()[...]), normalize)
+    for load in (base, update_first, update_second, gain, start, sender_first, select):
+        load()
     summed = dot(collect, messages[...]).astype(bf16)
     summand = base()[...] + dot(summed, update_first()[...])
     state = update(start()[...], summand, update_second()[...], gain()[0:1, :])
@@ -342,11 +368,14 @@
         summands[j % 2] = dot(pick.astype(bf16), incoming()[...])
 
     def middle(j):
-        part = sums[j]()
+        if j in (0, 2):
+            for load in sums[j : 2 if j == 0 else degree]:
+                load()
+        part = sums[j].target
         for begin in range(0, owned, CHUNK):
             some = slice(begin, begin + CHUNK)
             summand = part[some, :].astype(f32) + summands[j % 2, some, :]
-            hiddens[j % 2, some, :] = silu(summand).astype(bf16)
+            hiddens[j % 2, some, :] = silu16(summand)
         results[j % 2] = dot(hiddens[j % 2], second()[...])
 
     def tail(j):
@@ -362,7 +391,7 @@
         if last:
             fill(None)
         else:
-            store(3, fill, j)
+            store(3, fill, j, j % 4 != 3)
 
     lead(0)
     middle(0)
@@ -465,8 +494,8 @@
         (
             terms,
             embed_first,
+            link_embed,
             embed_second,
-            link_embed,
             (link_first, rows_of(0, width), 1),
             (link_first, rows_of(2 * width, 3 * width), 1),
             receiver,
@@ -483,6 +512,9 @@
             pltpu.VMEM((width, width), bf16),
             pltpu.VMEM((128, width), f32),
             pltpu.VMEM((slots, width), bf16),
+            pltpu.VMEM((slots, width), bf16),
+            pltpu.VMEM((slots, width), bf16),
+            pltpu.VMEM((slots, owned), bf16),
         ],
     )
     steps = process_first.shape[0]

time: 81.8 us -> 80.9 us (0.989)
  Pallas kernels: 51.2 us -> 50.2 us
    pallas_call x7, Pallas kernels: 51.2 us -> 50.2 us  [run(): pl.pallas_call(whole, out_shape=[jax.ShapeDtypeStruct(out[0], out[1]) for...]
  transfers between devices with their start and end apart: 3 -> 3, of which waited for: 3 -> 3; matrix products, arithmetic and copies ran while one was open for 0% -> 0% of each run, Pallas kernels for 27% -> 28%
where the time goes in v5:
time: 80.9 us; the launch traced here: 80.1 us
  Pallas kernels  50.2 us (62%)
  starting transfers between devices  15.3 us (19%)
  waiting for transfers between devices  12.2 us (15%)
  local copies, waits for them, and re-layouts  2.2 us (3%)
    pallas_call x7, Pallas kernels, run(): pl.pallas_call(whole, out_shape=[jax.ShapeDtypeStruct(out[0], out[1]) for...  50.2 us
    all_to_all x3, starting transfers between devices, exchange(): lax.all_to_all(values, 'rows', split_axis=0, concat_axis=0, tiled=True)  15.3 us
    all_to_all x3, waiting for transfers between devices, exchange(): lax.all_to_all(values, 'rows', split_axis=0, concat_axis=0, tiled=True)  12.2 us
    unnamed x6, local copies, waits for them, and re-layouts  2.2 us
  transfers between devices with their start and end apart: 3, of which 3 were waited for; matrix products, arithmetic and copies ran while one was open for 0% of the time, Pallas kernels for 28%

profile of v5, /device:TPU:0, one launch (start us, length us, event | category | flops | bytes accessed | tf_op | source)
XLA Modules:
  0.0 80.1 jit_solution(10261444719409050694)
XLA Ops:
  0.0 2.3 %pack.1 = bf16[512,512]{1,0:T(8,128)(2,1)} custom-call(bf16[474,128]{1,0:T(8,128)(2,1)} %refs_0_.2, f32[4,256]{1,0:T(4,128)} %refs_1_.3, s32[2,128]{1,0:T(2,128)} %bitcast.19, s32[2,128]{1,0:T(2,128)} %bitcast.20), custom_call_target="tpu_custom_call" | custom-call | flops 1000000000 | bytes 8388608 | tf_op jit(solution)/shard_map/pack/pallas_call | solution.py:160
  2.3 7.4 %all-to-all-start = ((bf16[16,32,512]{2,1,0:T(8,128)(2,1)}), bf16[16,32,512]{2,1,0:T(8,128)(2,1)S(1)}, u32[]{:S(2)}, u32[]{:S(2)}) async-start(bf16[16,32,512]{2,1,0:T(8,128)(2,1)} %bitcast.12), calls=%async_computation | async-start | bytes 1048576 | tf_op jit(solution)/shard_map/all_to_all | solution.py:451
  9.7 8.7 %side.1 = (bf16[8,384,512]{2,1,0:T(8,128)(2,1)}, bf16[8,384,512]{2,1,0:T(8,128)(2,1)}, bf16[384,512]{1,0:T(8,128)(2,1)}, f32[384,512]{1,0:T(8,128)}, bf16[256,384]{1,0:T(8,128)(2,1)}) custom-call(f32[4,3072]{1,0:T(4,128)} %refs_0_.3, f32[4,512]{1,0:T(4,128)} %refs_1_.4, bf16[2,1536,512]{2,1,0:T(8,128)(2,1)} %refs_2_.10, bf16[384,512]{1,0:T(8,128)(2,1)} %refs_11_.1, ...), custom_call_target="tpu_custom_call" | custom-call | flops 10000000000 | bytes 8388608 | tf_op jit(solution)/shard_map/side/pallas_call | solution.py:160
  18.5 5.7 %all-to-all-done = bf16[16,32,512]{2,1,0:T(8,128)(2,1)S(1)} async-done(((bf16[16,32,512]{2,1,0:T(8,128)(2,1)}), bf16[16,32,512]{2,1,0:T(8,128)(2,1)S(1)}, u32[]{:S(2)}, u32[]{:S(2)}) %all-to-all-start) | async-done | bytes 524320 | tf_op jit(solution)/shard_map/all_to_all | solution.py:451
  24.2 0.0 copy-start
  24.2 0.8 copy-done
  25.0 7.0 %link.1 = (bf16[384,512]{1,0:T(8,128)(2,1)}, bf16[256,512]{1,0:T(8,128)(2,1)}, bf16[384,512]{1,0:T(8,128)(2,1)}) custom-call(bf16[512,512]{1,0:T(8,128)(2,1)} %bitcast.9, bf16[474,512]{1,0:T(8,128)(2,1)} %refs_1_.5, f32[4,512]{1,0:T(4,128)} %refs_2_.7, bf16[512,512]{1,0:T(8,128)(2,1)} %refs_3_.3, bf16[1536,512]{1,0:T(8,128)(2,1)} %refs_4_.3, ...), custom_call_target="tpu_custom_call" | custom-call | flops 1000000000 | bytes 8388608 | tf_op jit(solution)/shard_map/link/pallas_call | solution.py:160
  32.0 4.1 %all-to-all-start.1 = ((bf16[16,16,512]{2,1,0:T(8,128)(2,1)}), bf16[16,16,512]{2,1,0:T(8,128)(2,1)S(1)}, u32[]{:S(2)}, u32[]{:S(2)}) async-start(bf16[16,16,512]{2,1,0:T(8,128)(2,1)} %bitcast.14), calls=%async_computation.1 | async-start | bytes 524288 | tf_op jit(solution)/shard_map/all_to_all | solution.py:451
  36.1 5.5 %local0.1.refs_3_ = bf16[8,384,512]{2,1,0:T(8,128)(2,1)} custom-call(s32[8,384]{1,0:T(8,128)} %bitcast.15, bf16[384,512]{1,0:T(8,128)(2,1)} %get-tuple-element.21.refs_1_.refs_4_, bf16[2,1536,512]{2,1,0:T(8,128)(2,1)} %refs_2_.10, bf16[384,512]{1,0:T(8,128)(2,1)} %get-tuple-element.22.refs_3_, bf16[8,384,512]{2,1,0:T(8,128)(2,1)} %get-tuple-element.23.refs_4_), custom_call_target="tpu_custom_call" | custom-call | flops 10000000000 | bytes 8388608 | tf_op jit(solution)/shard_map/local0/pallas_call | solution.py:160
  41.6 4.5 %all-to-all-done.1 = bf16[16,16,512]{2,1,0:T(8,128)(2,1)S(1)} async-done(((bf16[16,16,512]{2,1,0:T(8,128)(2,1)}), bf16[16,16,512]{2,1,0:T(8,128)(2,1)S(1)}, u32[]{:S(2)}, u32[]{:S(2)}) %all-to-all-start.1) | async-done | bytes 262176 | tf_op jit(solution)/shard_map/all_to_all | solution.py:451
  46.1 0.0 copy-start.1
  46.1 0.7 copy-done.1
  46.9 9.9 %edge0.1 = (bf16[384,512]{1,0:T(8,128)(2,1)}, bf16[256,512]{1,0:T(8,128)(2,1)}, bf16[384,512]{1,0:T(8,128)(2,1)}, bf16[8,384,512]{2,1,0:T(8,128)(2,1)}) custom-call(s32[8,384]{1,0:T(8,128)} %bitcast.16, bf16[256,512]{1,0:T(8,128)(2,1)} %bitcast.10, bf16[2,512,512]{2,1,0:T(8,128)(2,1)} %refs_2_.11, bf16[8,384,512]{2,1,0:T(8,128)(2,1)} %local0.1.refs_3_, ...), custom_call_target="tpu_custom_call" | custom-call | flops 1000000000 | bytes 8388608 | tf_op jit(solution)/shard_map/edge0/pallas_call | solution.py:160
  56.7 3.8 %all-to-all-start.2 = ((bf16[16,16,512]{2,1,0:T(8,128)(2,1)}), bf16[16,16,512]{2,1,0:T(8,128)(2,1)S(1)}, u32[]{:S(2)}, u32[]{:S(2)}) async-start(bf16[16,16,512]{2,1,0:T(8,128)(2,1)} %bitcast.13), calls=%async_computation.2 | async-start | bytes 524288 | tf_op jit(solution)/shard_map/all_to_all | solution.py:451
  60.5 7.8 %local1.1.refs_3_ = bf16[8,384,512]{2,1,0:T(8,128)(2,1)} custom-call(s32[8,384]{1,0:T(8,128)} %bitcast.17, bf16[384,512]{1,0:T(8,128)(2,1)} %get-tuple-element.25.refs_1_.refs_4_, bf16[2,1536,512]{2,1,0:T(8,128)(2,1)} %refs_2_.10, bf16[384,512]{1,0:T(8,128)(2,1)} %get-tuple-element.26.refs_3_, bf16[8,384,512]{2,1,0:T(8,128)(2,1)} %get-tuple-element.27.refs_4_, ...), custom_call_target="tpu_custom_call" | custom-call | flops 10000000000 | bytes 8388608 | tf_op jit(solution)/shard_map/local1/pallas_call | solution.py:160
  68.4 1.9 %all-to-all-done.2 = bf16[16,16,512]{2,1,0:T(8,128)(2,1)S(1)} async-done(((bf16[16,16,512]{2,1,0:T(8,128)(2,1)}), bf16[16,16,512]{2,1,0:T(8,128)(2,1)S(1)}, u32[]{:S(2)}, u32[]{:S(2)}) %all-to-all-start.2) | async-done | bytes 262176 | tf_op jit(solution)/shard_map/all_to_all | solution.py:451
  70.3 0.0 copy-start.2
  70.3 0.7 copy-done.2
  71.0 8.9 %edge1.1 = bf16[384,512]{1,0:T(8,128)(2,1)} custom-call(s32[8,384]{1,0:T(8,128)} %bitcast.18, bf16[256,512]{1,0:T(8,128)(2,1)} %bitcast.11, bf16[2,512,512]{2,1,0:T(8,128)(2,1)} %refs_2_.11, bf16[8,384,512]{2,1,0:T(8,128)(2,1)} %local1.1.refs_3_, bf16[384,512]{1,0:T(8,128)(2,1)} %get-tuple-element.25.refs_1_.refs_4_, bf16[2,1024,512]{2,1,0:T(8,128)(2,1)} %refs_5_.5, ...), custom_call_target="tpu_custom_call" | custom-call | flops 1000000000 | bytes 8388608 | tf_op jit(solution)/shard_map/edge1/pallas_call | solution.py:160
Async XLA Ops:
  2.3 21.9 %all-to-all-start = ((bf16[16,32,512]{2,1,0:T(8,128)(2,1)}), bf16[16,32,512]{2,1,0:T(8,128)(2,1)S(1)}, u32[]{:S(2)}, u32[]{:S(2)}) async-start(bf16[16,32,512]{2,1,0:T(8,128)(2,1)} %bitcast.12), calls=%async_computation | async-start | bytes 1048576 | tf_op jit(solution)/shard_map/all_to_all | solution.py:451
  24.2 0.8 copy-start
  32.0 14.2 %all-to-all-start.1 = ((bf16[16,16,512]{2,1,0:T(8,128)(2,1)}), bf16[16,16,512]{2,1,0:T(8,128)(2,1)S(1)}, u32[]{:S(2)}, u32[]{:S(2)}) async-start(bf16[16,16,512]{2,1,0:T(8,128)(2,1)} %bitcast.14), calls=%async_computation.1 | async-start | bytes 524288 | tf_op jit(solution)/shard_map/all_to_all | solution.py:451
  46.1 0.7 copy-start.1
  56.7 13.6 %all-to-all-start.2 = ((bf16[16,16,512]{2,1,0:T(8,128)(2,1)}), bf16[16,16,512]{2,1,0:T(8,128)(2,1)S(1)}, u32[]{:S(2)}, u32[]{:S(2)}) async-start(bf16[16,16,512]{2,1,0:T(8,128)(2,1)} %bitcast.13), calls=%async_computation.2 | async-start | bytes 524288 | tf_op jit(solution)/shard_map/all_to_all | solution.py:451
  70.3 0.7 copy-start.2

commit v6 on v5

--- a/solution.py
+++ b/solution.py
@@ -23,11 +23,6 @@
 
 def silu(values):
     half = 0.5 * values
-    return half + half * jnp.tanh(half)
-
-
-def silu16(values):
-    half = (0.5 * values).astype(bf16)
     return half + half * jnp.tanh(half)
 
 
@@ -225,12 +220,12 @@
     store(0, dot(select, columns[...], 1, 1).astype(bf16))
 
 
-def side_kernel(loads, store, pieces, turned, table):
+def side_kernel(sizes, gather, loads, store, pieces, turned, table):
     features, embed, edge_first, start, link_receiver, update_start, lists = loads
     owned, width = start.target.shape
     edges = features.target.shape[1]
     degree = edges // owned
-    devices, slots = lists.target.shape[1:]
+    devices, far, slots = sizes
     pieces[...] = jnp.zeros_like(pieces)
     turned[...] = jnp.zeros_like(turned)
     table[...] = jnp.zeros_like(table)
@@ -246,14 +241,53 @@
     store(2, dot(start()[...], link_receiver()[...]).astype(bf16))
     store(3, dot(start()[...], update_start()[...]))
     lists = lists()[0]
-    rows = devices * slots
-    row = iota((rows, 1), 0)
-    picks = jnp.where(iota((rows, devices), 1) == row // slots, 1.0, 0.0).astype(bf16)
+    rows = devices * far + (2 * slots if gather else 0)
+    reader, place = outgoing_slots(rows, devices, far, slots)
+    picks = jnp.where(iota((rows, devices), 1) == reader, 1.0, 0.0).astype(bf16)
     high = dot(picks, (lists >> 4).astype(f32).astype(bf16))
     low = dot(picks, (lists & 15).astype(f32).astype(bf16))
-    chosen = jnp.where(iota((rows, slots), 1) == row % slots, high * 16.0 + low, 0.0)
+    chosen = jnp.where(iota((rows, slots), 1) == place, high * 16.0 + low, 0.0)
     column = jnp.sum(chosen, axis=1, keepdims=True).astype(jnp.int32)
     store(4, jnp.where(iota((rows, owned), 1) == column, 1.0, 0.0).astype(bf16))
+
+
+def neighbours(devices):
+    me = lax.axis_index("rows")
+    return (me + devices - 1) % devices, (me + 1) % devices
+
+
+def outgoing_slots(rows, devices, far, slots):
+    before, after = neighbours(devices)
+    row = iota((rows, 1), 0)
+    near = row - devices * far
+    reader = jnp.where(near < 0, row // far, jnp.where(near < slots, after, before))
+    return reader, jnp.where(near < 0, row % far, near % slots)
+
+
+def gathered_rows(rows, devices, far, slots):
+    me = lax.axis_index("rows")
+    before, after = neighbours(devices)
+    each = devices * far + 2 * slots
+    row = iota((rows, 1), 0)
+    near = row - devices * far
+    from_far = row // far * each + me * far + row % far
+    from_before = before * each + devices * far + near
+    from_after = after * each + devices * far + near
+    found = jnp.where(near < 0, from_far, jnp.where(near < slots, from_before, from_after))
+    return jnp.where(near < 2 * slots, found, -1)
+
+
+def halo_index(senders, owned, devices, far, slots):
+    if far == slots:
+        return senders - owned
+    before, after = neighbours(devices)
+    halo = senders - owned
+    owner = halo // slots
+    place = halo % slots
+    index = owner * far + place
+    index = jnp.where(owner == before, devices * far + place, index)
+    index = jnp.where(owner == after, devices * far + slots + place, index)
+    return jnp.where(halo < 0, -1, index)
 
 
 def update(state, summand, second, gain):
@@ -356,26 +390,32 @@
         store(0, (part + kept).astype(bf16), j)
 
 
-def edge_kernel(step, last, loads, store, summands, hiddens, results, total):
+def edge_kernel(step, last, sizes, loads, store, summands, hiddens, results, total, table):
     senders, incoming, second, sums = loads[:4]
     (state, state_first, summed_first, update_second, gain) = loads[4:9]
     degree, owned = senders.target.shape
-    rows = incoming.target.shape[0]
-    columns = jnp.transpose((senders()[...] - owned).astype(f32)).astype(jnp.int32)
+    devices, far, slots = sizes
+    rows = table.shape[0]
+    index = halo_index(senders()[...], owned, *sizes)
+    columns = jnp.transpose(index.astype(f32)).astype(jnp.int32)
+    count = incoming.target.shape[0]
+    if count == rows:
+        table[...] = incoming()[...]
+    else:
+        found = gathered_rows(rows, *sizes)
+        collect = jnp.where(iota((rows, count), 1) == found, 1.0, 0.0).astype(bf16)
+        table[...] = dot(collect, incoming()[...]).astype(bf16)
 
     def lead(j):
         pick = jnp.where(iota((owned, rows), 1) == columns[:, j : j + 1], 1.0, 0.0)
-        summands[j % 2] = dot(pick.astype(bf16), incoming()[...])
+        summands[j % 2] = dot(pick.astype(bf16), table[...])
 
     def middle(j):
-        if j in (0, 2):
-            for load in sums[j : 2 if j == 0 else degree]:
-                load()
-        part = sums[j].target
+        part = sums[j]()
         for begin in range(0, owned, CHUNK):
             some = slice(begin, begin + CHUNK)
             summand = part[some, :].astype(f32) + summands[j % 2, some, :]
-            hiddens[j % 2, some, :] = silu16(summand)
+            hiddens[j % 2, some, :] = silu(summand).astype(bf16)
         results[j % 2] = dot(hiddens[j % 2], second()[...])
 
     def tail(j):
@@ -391,7 +431,7 @@
         if last:
             fill(None)
         else:
-            store(3, fill, j, j % 4 != 3)
+            store(3, fill, j)
 
     lead(0)
     middle(0)
@@ -443,7 +483,10 @@
     degree = edge_senders.shape[1]
     edges = owned * degree
     halo_slots = halo_lists.shape[2]
-    halo_rows = devices * halo_slots
+    gather = devices <= 32
+    far = 4 if gather else halo_slots
+    sizes = (devices, far, halo_slots)
+    halo_rows = devices * far + (2 * halo_slots if gather else 0)
     senders = edge_senders.T
 
     def exchange(values):
@@ -462,7 +505,7 @@
     )
     terms = exchange(packed)
     edge_state, parts, receiver, base, select = run(
-        side_kernel,
+        functools.partial(side_kernel, sizes, gather),
         "side",
         [
             ((degree, owned, width), bf16, degree),
@@ -520,7 +563,10 @@
     steps = process_first.shape[0]
     for step in range(steps):
         last = step + 1 == steps
-        incoming = exchange(outgoing)
+        if gather:
+            incoming = lax.all_gather(outgoing, "rows", axis=0, tiled=True)
+        else:
+            incoming = exchange(outgoing)
         extra = []
         if step:
             extra = [(process_first, rows_of(2 * width, 3 * width, step), 1)]
@@ -548,7 +594,7 @@
             outs += sending + [((degree, owned, width), bf16, degree)]
             extra = [(process_first, rows_of(0, width, step + 1), 1), select]
         results = run(
-            functools.partial(edge_kernel, step, last),
+            functools.partial(edge_kernel, step, last, sizes),
             f"edge{step}",
             outs,
             [
@@ -568,6 +614,7 @@
                 pltpu.VMEM((2, owned, width), bf16),
                 pltpu.VMEM((2, owned, width), f32),
                 pltpu.VMEM((owned, width), f32),
+                pltpu.VMEM((-(-halo_rows // 128) * 128, width), bf16),
             ],
         )
         if last:

time: 80.9 us -> 143 us (1.77)
  waiting for transfers between devices: 12.2 us -> 69.9 us
  between operations: 0.26 us -> 13.5 us
  starting transfers between devices: 15.3 us -> 7.67 us
    all_gather x0 -> x2, waiting for transfers between devices: none -> 64.2 us  [body(): incoming = lax.all_gather(outgoing, 'rows', axis=0, tiled=True)]
    all_to_all x3 -> x1, starting transfers between devices: 15.3 us -> 7.41 us  [exchange(): lax.all_to_all(values, 'rows', split_axis=0, concat_axis=0, tiled=True)]
    all_to_all x3 -> x1, waiting for transfers between devices: 12.2 us -> 5.7 us  [exchange(): lax.all_to_all(values, 'rows', split_axis=0, concat_axis=0, tiled=True)]
  transfers between devices with their start and end apart: 3 -> 3, of which waited for: 3 -> 3; matrix products, arithmetic and copies ran while one was open for 0% -> 0% of each run, Pallas kernels for 28% -> 16%
where the time goes in v6:
time: 143 us
  waiting for transfers between devices  69.9 us (49%)
  Pallas kernels  51 us (36%)
  between operations  13.5 us (9%)
  starting transfers between devices  7.67 us (5%)
    all_gather x2, waiting for transfers between devices, body(): incoming = lax.all_gather(outgoing, 'rows', axis=0, tiled=True)  64.2 us
    pallas_call x7, Pallas kernels, run(): pl.pallas_call(whole, out_shape=[jax.ShapeDtypeStruct(out[0], out[1]) for...  51 us
    all_to_all x1, starting transfers between devices, exchange(): lax.all_to_all(values, 'rows', split_axis=0, concat_axis=0, tiled=True)  7.41 us
    all_to_all x1, waiting for transfers between devices, exchange(): lax.all_to_all(values, 'rows', split_axis=0, concat_axis=0, tiled=True)  5.7 us
  transfers between devices with their start and end apart: 3, of which 3 were waited for; matrix products, arithmetic and copies ran while one was open for 0% of the time, Pallas kernels for 16%

profile of v6, /device:TPU:0, one launch (start us, length us, event | category | flops | bytes accessed | tf_op | source)
XLA Modules:
  0.0 142.8 jit_solution(2435137850511854837)
XLA Ops:
  6.5 2.3 %pack.1 = bf16[512,512]{1,0:T(8,128)(2,1)} custom-call(bf16[474,128]{1,0:T(8,128)(2,1)} %refs_0_.2, f32[4,256]{1,0:T(4,128)} %refs_1_.3, s32[2,128]{1,0:T(2,128)} %bitcast.11, s32[2,128]{1,0:T(2,128)} %bitcast.12), custom_call_target="tpu_custom_call" | custom-call | flops 1000000000 | bytes 8388608 | tf_op jit(solution)/shard_map/pack/pallas_call | solution.py:155
  8.8 7.4 %all-to-all-start = ((bf16[16,32,512]{2,1,0:T(8,128)(2,1)}), bf16[16,32,512]{2,1,0:T(8,128)(2,1)S(1)}, u32[]{:S(2)}, u32[]{:S(2)}) async-start(bf16[16,32,512]{2,1,0:T(8,128)(2,1)} %bitcast.6), calls=%async_computation | async-start | bytes 1048576 | tf_op jit(solution)/shard_map/all_to_all | solution.py:494
  16.3 0.0 all-gather.3.cloned.1.call-start
  16.3 8.7 %side.1 = (bf16[8,384,512]{2,1,0:T(8,128)(2,1)}, bf16[8,384,512]{2,1,0:T(8,128)(2,1)}, bf16[384,512]{1,0:T(8,128)(2,1)}, f32[384,512]{1,0:T(8,128)}, bf16[96,384]{1,0:T(8,128)(2,1)}) custom-call(f32[4,3072]{1,0:T(4,128)} %refs_0_.3, f32[4,512]{1,0:T(4,128)} %refs_1_.4, bf16[2,1536,512]{2,1,0:T(8,128)(2,1)} %refs_2_.10, bf16[384,512]{1,0:T(8,128)(2,1)} %refs_11_.1, ...), custom_call_target="tpu_custom_call" | custom-call | flops 10000000000 | bytes 8388608 | tf_op jit(solution)/shard_map/side/pallas_call | solution.py:155
  25.0 5.7 %all-to-all-done = bf16[16,32,512]{2,1,0:T(8,128)(2,1)S(1)} async-done(((bf16[16,32,512]{2,1,0:T(8,128)(2,1)}), bf16[16,32,512]{2,1,0:T(8,128)(2,1)S(1)}, u32[]{:S(2)}, u32[]{:S(2)}) %all-to-all-start) | async-done | bytes 524320 | tf_op jit(solution)/shard_map/all_to_all | solution.py:494
  30.7 0.0 copy-start
  30.7 0.8 copy-done
  31.5 6.9 %link.1 = (bf16[384,512]{1,0:T(8,128)(2,1)}, bf16[96,512]{1,0:T(8,128)(2,1)}, bf16[384,512]{1,0:T(8,128)(2,1)}) custom-call(bf16[512,512]{1,0:T(8,128)(2,1)} %bitcast.5, bf16[474,512]{1,0:T(8,128)(2,1)} %refs_1_.5, f32[4,512]{1,0:T(4,128)} %refs_2_.7, bf16[512,512]{1,0:T(8,128)(2,1)} %refs_3_.3, bf16[1536,512]{1,0:T(8,128)(2,1)} %refs_4_.3, ...), custom_call_target="tpu_custom_call" | custom-call | flops 1000000000 | bytes 8388608 | tf_op jit(solution)/shard_map/link/pallas_call | solution.py:155
  38.4 0.0 all-gather.3.cloned.1.call-update
  38.4 0.2 all-gather.5.cloned.1.call-start
  38.7 5.5 %local0.1.refs_3_ = bf16[8,384,512]{2,1,0:T(8,128)(2,1)} custom-call(s32[8,384]{1,0:T(8,128)} %bitcast.7, bf16[384,512]{1,0:T(8,128)(2,1)} %get-tuple-element.21.refs_1_.refs_4_, bf16[2,1536,512]{2,1,0:T(8,128)(2,1)} %refs_2_.10, bf16[384,512]{1,0:T(8,128)(2,1)} %get-tuple-element.22.refs_3_, bf16[8,384,512]{2,1,0:T(8,128)(2,1)} %get-tuple-element.23.refs_4_), custom_call_target="tpu_custom_call" | custom-call | flops 10000000000 | bytes 8388608 | tf_op jit(solution)/shard_map/local0/pallas_call | solution.py:155
  44.2 33.5 %all-gather.3.cloned.1.call-done.refs_1_ = bf16[1536,512]{1,0:T(8,128)(2,1)} async-done(((bf16[96,512]{1,0:T(8,128)(2,1)}), bf16[1536,512]{1,0:T(8,128)(2,1)}) %all-gather.3.cloned.1.call-update) | async-done | bytes 1572880 | tf_op jit(solution)/shard_map/all_gather | solution.py:567
  77.7 10.2 %edge0.1 = (bf16[384,512]{1,0:T(8,128)(2,1)}, bf16[96,512]{1,0:T(8,128)(2,1)}, bf16[384,512]{1,0:T(8,128)(2,1)}, bf16[8,384,512]{2,1,0:T(8,128)(2,1)}) custom-call(s32[8,384]{1,0:T(8,128)} %bitcast.8, bf16[1536,512]{1,0:T(8,128)(2,1)} %all-gather.3.cloned.1.call-done.refs_1_, bf16[2,512,512]{2,1,0:T(8,128)(2,1)} %refs_2_.11, ...), custom_call_target="tpu_custom_call" | custom-call | flops 1000000000 | bytes 8388608 | tf_op jit(solution)/shard_map/edge0/pallas_call | solution.py:155
  87.8 0.0 all-gather.5.cloned.1.call-update
  87.9 8.1 %local1.1.refs_3_ = bf16[8,384,512]{2,1,0:T(8,128)(2,1)} custom-call(s32[8,384]{1,0:T(8,128)} %bitcast.9, bf16[384,512]{1,0:T(8,128)(2,1)} %get-tuple-element.25.refs_1_.refs_4_, bf16[2,1536,512]{2,1,0:T(8,128)(2,1)} %refs_2_.10, bf16[384,512]{1,0:T(8,128)(2,1)} %get-tuple-element.26.refs_3_, bf16[8,384,512]{2,1,0:T(8,128)(2,1)} %get-tuple-element.27.refs_4_, ...), custom_call_target="tpu_custom_call" | custom-call | flops 10000000000 | bytes 8388608 | tf_op jit(solution)/shard_map/local1/pallas_call | solution.py:155
  95.9 30.7 %all-gather.5.cloned.1.call-done.refs_1_ = bf16[1536,512]{1,0:T(8,128)(2,1)} async-done(((bf16[96,512]{1,0:T(8,128)(2,1)}), bf16[1536,512]{1,0:T(8,128)(2,1)}) %all-gather.5.cloned.1.call-update) | async-done | bytes 1572880 | tf_op jit(solution)/shard_map/all_gather | solution.py:567
  126.6 9.4 %edge1.1 = bf16[384,512]{1,0:T(8,128)(2,1)} custom-call(s32[8,384]{1,0:T(8,128)} %bitcast.10, bf16[1536,512]{1,0:T(8,128)(2,1)} %all-gather.5.cloned.1.call-done.refs_1_, bf16[2,512,512]{2,1,0:T(8,128)(2,1)} %refs_2_.11, bf16[8,384,512]{2,1,0:T(8,128)(2,1)} %local1.1.refs_3_, bf16[384,512]{1,0:T(8,128)(2,1)} %get-tuple-element.25.refs_1_.refs_4_, ...), custom_call_target="tpu_custom_call" | custom-call | flops 1000000000 | bytes 8388608 | tf_op jit(solution)/shard_map/edge1/pallas_call | solution.py:155
Async XLA Ops:
  8.8 21.9 %all-to-all-start = ((bf16[16,32,512]{2,1,0:T(8,128)(2,1)}), bf16[16,32,512]{2,1,0:T(8,128)(2,1)S(1)}, u32[]{:S(2)}, u32[]{:S(2)}) async-start(bf16[16,32,512]{2,1,0:T(8,128)(2,1)} %bitcast.6), calls=%async_computation | async-start | bytes 1048576 | tf_op jit(solution)/shard_map/all_to_all | solution.py:494
  16.3 61.4 %all-gather.3.cloned.1.call-start = ((), (), s32[]{:S(2)}) async-start(), calls=%async_computation.1 | async-start | bytes 1671168 | tf_op jit(solution)/shard_map/all_gather | solution.py:567
  30.7 0.8 copy-start
  38.4 88.2 %all-gather.5.cloned.1.call-start = ((), (), s32[]{:S(2)}) async-start(), calls=%async_computation.2 | async-start | bytes 1671168 | tf_op jit(solution)/shard_map/all_gather | solution.py:567
Sparse Core Ops, SparseCore 0:
  38.5 39.0 all-gather.2
  88.0 38.5 all-gather.4

commit v7 on v5

--- a/solution.py
+++ b/solution.py
@@ -26,16 +26,26 @@
     return half + half * jnp.tanh(half)
 
 
-def silu16(values):
-    half = (0.5 * values).astype(bf16)
-    return half + half * jnp.tanh(half)
-
-
 def normalize(values):
     scale = 1.0 / values.shape[-1]
     center = values - jnp.sum(values, axis=-1, keepdims=True) * scale
     spread = jnp.sum(center * center, axis=-1, keepdims=True) * scale
     return center * lax.rsqrt(spread + epsilon)
+
+
+def each(values, function):
+    parts = [values[i : i + CHUNK, :] for i in range(0, values.shape[0], CHUNK)]
+    return jnp.concatenate([function(part).astype(bf16) for part in parts], axis=0)
+
+
+def one_hot(columns, block, count):
+    rows = slice(block * CHUNK, (block + 1) * CHUNK)
+    lanes = iota((CHUNK, count), 1)
+    picks = [
+        jnp.where(lanes == columns[rows, j : j + 1], 1.0, 0.0).astype(bf16)
+        for j in range(columns.shape[1])
+    ]
+    return jnp.concatenate(picks, axis=0)
 
 
 def iota(shape, dim):
@@ -74,7 +84,7 @@
         return self.target
 
 
-def run(kernel, name, outs, args, scratch=(), flops=10**9):
+def run(kernel, name, outs, args, scratch=(), flops=10**9, reuse=None):
     plans = []
     for arg in args:
         if not isinstance(arg, tuple):
@@ -86,6 +96,7 @@
             shape = jax.eval_shape(lambda x, take=take: take(x, 0), array).shape
         plans.append((array, take, count, shape))
     n_in, n_out = len(plans), len(outs)
+    spare = [] if reuse is None else [plans[reuse][0]]
     starts, total = [], 0
     for plan in plans:
         starts.append(total)
@@ -112,7 +123,7 @@
     def whole(*refs):
         ins = refs[: len(arrays)]
         out_refs = refs[len(arrays) : len(arrays) + n_out]
-        rest = refs[len(arrays) + n_out :]
+        rest = refs[len(arrays) + n_out + len(spare) :]
         in_vmem, out_vmem = rest[:n_in], rest[n_in : n_in + n_out]
         in_sems, out_sems = rest[n_in + n_out : n_in + n_out + 2]
         loads = [[None] * count for _, _, count, _ in plans]
@@ -157,11 +168,13 @@
         pltpu.VMEM(shape if count == 1 else (count,) + shape, array.dtype)
         for array, _, count, shape in plans
     ]
-    return pl.pallas_call(
+    results = pl.pallas_call(
         whole,
-        out_shape=[jax.ShapeDtypeStruct(out[0], out[1]) for out in outs],
+        out_shape=[jax.ShapeDtypeStruct(out[0], out[1]) for out in outs]
+        + [jax.ShapeDtypeStruct(array.shape, array.dtype) for array in spare],
         in_specs=[spec] * len(arrays),
-        out_specs=[spec] * n_out,
+        out_specs=[spec] * (n_out + len(spare)),
+        input_output_aliases={places[reuse]: n_out} if spare else {},
         scratch_shapes=in_scratch
         + [pltpu.VMEM(out[0], out[1]) for out in outs]
         + [pltpu.SemaphoreType.DMA((total,)), pltpu.SemaphoreType.DMA((out_total,))]
@@ -170,6 +183,7 @@
         cost_estimate=pl.CostEstimate(flops=flops, bytes_accessed=8 * MIB, transcendentals=0),
         name=name,
     )(*arrays)
+    return results[:n_out]
 
 
 def rows_of(start, stop, step=None):
@@ -238,11 +252,15 @@
     turned[:, 0:EXTRA] = jnp.transpose(pieces[...])
     store_pieces(table, embed()[...], RIGHT_ORDER)
     matrix = table[...].astype(bf16)
-    for j in range(degree):
-        left = turned[pl.ds(j, owned, stride=degree), :].astype(bf16)
-        edge_state = normalize(silu(dot(left, matrix))).astype(bf16)
-        store(0, edge_state, j)
-        store(1, dot(edge_state, edge_first()[...]).astype(bf16), j)
+    for block in range(owned // CHUNK):
+        base = block * CHUNK * degree
+        left = jnp.concatenate(
+            [turned[pl.ds(base + j, CHUNK, stride=degree), :] for j in range(degree)], axis=0
+        )
+        linear = dot(left.astype(bf16), matrix)
+        edge_state = each(linear, lambda x: normalize(silu(x)))
+        store(0, edge_state, block)
+        store(1, dot(edge_state, edge_first()[...]).astype(bf16), block)
     store(2, dot(start()[...], link_receiver()[...]).astype(bf16))
     store(3, dot(start()[...], update_start()[...]))
     lists = lists()[0]
@@ -294,10 +312,6 @@
         lanes == tail - EXTRA + 24, 16.0, jnp.where(lanes == tail - EXTRA + 25, 1.0, 0.0)
     ).astype(bf16)
     chunks = [slice(begin, begin + 128) for begin in range(0, slots, 128)]
-
-    def each(values, function):
-        parts = [values[i : i + CHUNK, :] for i in range(0, values.shape[0], CHUNK)]
-        return jnp.concatenate([function(part).astype(bf16) for part in parts], axis=0)
 
     table[...] = jnp.zeros_like(table)
     first[channels // 16 * 16 :, :] = jnp.zeros((width - channels // 16 * 16, width), bf16)
@@ -338,71 +352,77 @@
     send(store, 1, state, sender_first()[...], select()[...])
 
 
-def local_kernel(step, last, loads, store):
+def local_kernel(step, last, loads, store, kept):
     senders, state, receiver_first, sent = loads[:4]
     parts = loads[5 if step else 4]
     degree, owned = senders.target.shape
     columns = jnp.transpose(senders()[...].astype(f32)).astype(jnp.int32)
-    kept = dot(state()[...], receiver_first()[...]).astype(bf16).astype(f32)
-    for j in range(degree):
-        local = jnp.where(iota((owned, owned), 1) == columns[:, j : j + 1], 1.0, 0.0)
-        part = parts[j]()[...]
+    kept[...] = dot(state()[...], receiver_first()[...]).astype(bf16).astype(f32)
+    for block in range(owned // CHUNK):
+        summand = dot(one_hot(columns, block, owned), sent()[...])
+        part = parts[block]()[...]
         if step:
-            edge_state = (part.astype(f32) + loads[6][j]()[...].astype(f32)).astype(bf16)
+            message = loads[6][block]()[...]
+            edge_state = (part.astype(f32) + message.astype(f32)).astype(bf16)
             if not last:
-                store(1, edge_state, j)
-            part = dot(edge_state, loads[4]()[...])
-        part = dot(local.astype(bf16), sent()[...]) + part.astype(f32)
-        store(0, (part + kept).astype(bf16), j)
+                store(1, edge_state, block)
+            summand = summand + dot(edge_state, loads[4]()[...])
+        receiver = kept[block * CHUNK : (block + 1) * CHUNK, :]
+
+        def finish(j):
+            rows = slice(j * CHUNK, (j + 1) * CHUNK)
+            values = summand[rows, :] + receiver
+            if not step:
+                values = values + part[rows, :].astype(f32)
+            return values.astype(bf16)
+
+        store(0, jnp.concatenate([finish(j) for j in range(degree)], axis=0), block)
 
 
 def edge_kernel(step, last, loads, store, summands, hiddens, results, total):
     senders, incoming, second, sums = loads[:4]
     (state, state_first, summed_first, update_second, gain) = loads[4:9]
     degree, owned = senders.target.shape
+    blocks = owned // CHUNK
     rows = incoming.target.shape[0]
     columns = jnp.transpose((senders()[...] - owned).astype(f32)).astype(jnp.int32)
 
-    def lead(j):
-        pick = jnp.where(iota((owned, rows), 1) == columns[:, j : j + 1], 1.0, 0.0)
-        summands[j % 2] = dot(pick.astype(bf16), incoming()[...])
-
-    def middle(j):
-        if j in (0, 2):
-            for load in sums[j : 2 if j == 0 else degree]:
-                load()
-        part = sums[j].target
-        for begin in range(0, owned, CHUNK):
-            some = slice(begin, begin + CHUNK)
-            summand = part[some, :].astype(f32) + summands[j % 2, some, :]
-            hiddens[j % 2, some, :] = silu16(summand)
-        results[j % 2] = dot(hiddens[j % 2], second()[...])
-
-    def tail(j):
+    def lead(block):
+        summands[block % 2] = dot(one_hot(columns, block, rows), incoming()[...])
+
+    def middle(block):
+        part = sums[block]()
+        for j in range(degree):
+            some = slice(j * CHUNK, (j + 1) * CHUNK)
+            summand = part[some, :].astype(f32) + summands[block % 2, some, :]
+            hiddens[block % 2, some, :] = silu(summand).astype(bf16)
+        results[block % 2] = dot(hiddens[block % 2], second()[...])
+
+    def tail(block):
         def fill(target):
-            for begin in range(0, owned, CHUNK):
-                some = slice(begin, begin + CHUNK)
-                message = normalize(results[j % 2, some, :]).astype(bf16)
+            added = jnp.zeros((CHUNK, total.shape[1]), f32)
+            for j in range(degree):
+                some = slice(j * CHUNK, (j + 1) * CHUNK)
+                message = normalize(results[block % 2, some, :])
                 if target is not None:
+                    message = message.astype(bf16)
                     target[some, :] = message
-                message = message.astype(f32)
-                total[some, :] = message if j == 0 else total[some, :] + message
+                added = added + message.astype(f32)
+            total[block * CHUNK : (block + 1) * CHUNK, :] = added.astype(bf16)
 
         if last:
             fill(None)
         else:
-            store(3, fill, j, j % 4 != 3)
+            store(3, fill, block, block % 3 != 2)
 
     lead(0)
     middle(0)
-    for j in range(degree):
-        if j + 1 < degree:
-            lead(j + 1)
-            middle(j + 1)
-        tail(j)
-    summand = dot(state()[...], state_first()[...]) + dot(
-        total[...].astype(bf16), summed_first()[...]
-    )
+    for block in range(blocks):
+        if block + 1 < blocks:
+            lead(block + 1)
+            middle(block + 1)
+        tail(block)
+    summand = dot(state()[...], state_first()[...]) + dot(total[...], summed_first()[...])
     state = update(
         state()[...], summand, update_second()[...], gain()[step + 1 : step + 2, :]
     )
@@ -442,6 +462,8 @@
     slots = 2 * links
     degree = edge_senders.shape[1]
     edges = owned * degree
+    blocks = owned // CHUNK
+    edge_shape = (blocks, CHUNK * degree, width)
     halo_slots = halo_lists.shape[2]
     halo_rows = devices * halo_slots
     senders = edge_senders.T
@@ -465,8 +487,8 @@
         side_kernel,
         "side",
         [
-            ((degree, owned, width), bf16, degree),
-            ((degree, owned, width), bf16, degree),
+            (edge_shape, bf16, blocks),
+            (edge_shape, bf16, blocks),
             ((owned, width), bf16, 1),
             ((owned, width), f32, 1),
             ((halo_rows, owned), bf16, 1),
@@ -516,6 +538,7 @@
             pltpu.VMEM((slots, width), bf16),
             pltpu.VMEM((slots, owned), bf16),
         ],
+        reuse=0,
     )
     steps = process_first.shape[0]
     for step in range(steps):
@@ -528,7 +551,7 @@
         (sums, *kept) = run(
             functools.partial(local_kernel, step, last),
             f"local{step}",
-            [((degree, owned, width), bf16, degree)] * (1 if last or step == 0 else 2),
+            [(edge_shape, bf16, blocks)] * (1 if last or step == 0 else 2),
             [
                 senders,
                 state,
@@ -536,8 +559,9 @@
                 sent,
             ]
             + extra
-            + [(parts, piece_of, degree)]
-            + ([(message, piece_of, degree)] if step else []),
+            + [(parts, piece_of, blocks)]
+            + ([(message, piece_of, blocks)] if step else []),
+            [pltpu.VMEM((owned, width), f32)],
             flops=10**10,
         )
         if kept:
@@ -545,7 +569,7 @@
         outs = [((owned, width), bf16, 1)]
         extra = []
         if not last:
-            outs += sending + [((degree, owned, width), bf16, degree)]
+            outs += sending + [(edge_shape, bf16, blocks)]
             extra = [(process_first, rows_of(0, width, step + 1), 1), select]
         results = run(
             functools.partial(edge_kernel, step, last),
@@ -555,7 +579,7 @@
                 senders,
                 incoming,
                 (process_second, fixed(step), 1),
-                (sums, piece_of, degree),
+                (sums, piece_of, blocks),
                 state,
                 (process_update_first, rows_of(0, width, step), 1),
                 (process_update_first, rows_of(width, 2 * width, step), 1),
@@ -564,11 +588,12 @@
             ]
             + extra,
             [
-                pltpu.VMEM((2, owned, width), f32),
-                pltpu.VMEM((2, owned, width), bf16),
-                pltpu.VMEM((2, owned, width), f32),
-                pltpu.VMEM((owned, width), f32),
+                pltpu.VMEM((2,) + edge_shape[1:], f32),
+                pltpu.VMEM((2,) + edge_shape[1:], bf16),
+                pltpu.VMEM((2,) + edge_shape[1:], f32),
+                pltpu.VMEM((owned, width), bf16),
             ],
+            reuse=1,
         )
         if last:
             return results[0]

time: 80.9 us -> 81.9 us (1.012)
  Pallas kernels: 50.2 us -> 54.4 us
  waiting for transfers between devices: 12.2 us -> 9.02 us
    pallas_call x7, Pallas kernels: 50.2 us -> 54.4 us  [run(): pl.pallas_call(whole, out_shape=[jax.ShapeDtypeStruct(out[0], out[1]) for...]
    all_to_all x3, waiting for transfers between devices: 12.2 us -> 9.02 us  [exchange(): lax.all_to_all(values, 'rows', split_axis=0, concat_axis=0, tiled=True)]
  transfers between devices with their start and end apart: 3 -> 3, of which waited for: 3 -> 3; matrix products, arithmetic and copies ran while one was open for 0% -> 0% of each run, Pallas kernels for 28% -> 31%
where the time goes in v7:
time: 81.9 us; the launch traced here: 81.2 us
  Pallas kernels  54.4 us (66%)
  starting transfers between devices  15.3 us (19%)
  waiting for transfers between devices  9.02 us (11%)
  local copies, waits for them, and re-layouts  2.23 us (3%)
    pallas_call x7, Pallas kernels, run(): pl.pallas_call(whole, out_shape=[jax.ShapeDtypeStruct(out[0], out[1]) for...  54.4 us
    all_to_all x3, starting transfers between devices, exchange(): lax.all_to_all(values, 'rows', split_axis=0, concat_axis=0, tiled=True)  15.3 us
    all_to_all x3, waiting for transfers between devices, exchange(): lax.all_to_all(values, 'rows', split_axis=0, concat_axis=0, tiled=True)  9.02 us
    unnamed x6, local copies, waits for them, and re-layouts  2.23 us
  transfers between devices with their start and end apart: 3, of which 3 were waited for; matrix products, arithmetic and copies ran while one was open for 0% of the time, Pallas kernels for 31%

profile of v7, /device:TPU:0, one launch (start us, length us, event | category | flops | bytes accessed | tf_op | source)
XLA Modules:
  0.0 81.2 jit_solution(16655880917453884610)
XLA Ops:
  0.0 2.3 %pack.1 = bf16[512,512]{1,0:T(8,128)(2,1)} custom-call(bf16[474,128]{1,0:T(8,128)(2,1)} %refs_0_.2, f32[4,256]{1,0:T(4,128)} %refs_1_.3, s32[2,128]{1,0:T(2,128)} %bitcast.19, s32[2,128]{1,0:T(2,128)} %bitcast.20), custom_call_target="tpu_custom_call" | custom-call | flops 1000000000 | bytes 8388608 | tf_op jit(solution)/shard_map/pack/pallas_call | solution.py:171
  2.3 7.4 %all-to-all-start = ((bf16[16,32,512]{2,1,0:T(8,128)(2,1)}), bf16[16,32,512]{2,1,0:T(8,128)(2,1)S(1)}, u32[]{:S(2)}, u32[]{:S(2)}) async-start(bf16[16,32,512]{2,1,0:T(8,128)(2,1)} %bitcast.12), calls=%async_computation | async-start | bytes 1048576 | tf_op jit(solution)/shard_map/all_to_all | solution.py:473
  9.7 9.7 %side.1 = (bf16[12,256,512]{2,1,0:T(8,128)(2,1)}, bf16[12,256,512]{2,1,0:T(8,128)(2,1)}, bf16[384,512]{1,0:T(8,128)(2,1)}, f32[384,512]{1,0:T(8,128)}, bf16[256,384]{1,0:T(8,128)(2,1)}) custom-call(f32[4,3072]{1,0:T(4,128)} %refs_0_.3, f32[4,512]{1,0:T(4,128)} %refs_1_.4, bf16[2,1536,512]{2,1,0:T(8,128)(2,1)} %refs_2_.10, bf16[384,512]{1,0:T(8,128)(2,1)} %refs_11_.1, ...), custom_call_target="tpu_custom_call" | custom-call | flops 10000000000 | bytes 8388608 | tf_op jit(solution)/shard_map/side/pallas_call | solution.py:171
  19.5 4.7 %all-to-all-done = bf16[16,32,512]{2,1,0:T(8,128)(2,1)S(1)} async-done(((bf16[16,32,512]{2,1,0:T(8,128)(2,1)}), bf16[16,32,512]{2,1,0:T(8,128)(2,1)S(1)}, u32[]{:S(2)}, u32[]{:S(2)}) %all-to-all-start) | async-done | bytes 524320 | tf_op jit(solution)/shard_map/all_to_all | solution.py:473
  24.2 0.0 copy-start
  24.2 0.8 copy-done
  25.0 7.0 %link.1 = (bf16[384,512]{1,0:T(8,128)(2,1)}, bf16[256,512]{1,0:T(8,128)(2,1)}, bf16[384,512]{1,0:T(8,128)(2,1)}, bf16[512,512]{1,0:T(8,128)(2,1)}) custom-call(bf16[512,512]{1,0:T(8,128)(2,1)} %bitcast.9, bf16[474,512]{1,0:T(8,128)(2,1)} %refs_1_.5, f32[4,512]{1,0:T(4,128)} %refs_2_.7, bf16[512,512]{1,0:T(8,128)(2,1)} %refs_3_.3, ...), custom_call_target="tpu_custom_call", output_to_operand_aliasing={{3}: (0, {})} | custom-call | flops 1000000000 | bytes 8388608 | tf_op jit(solution)/shard_map/link/pallas_call | solution.py:171
  32.0 4.1 %all-to-all-start.1 = ((bf16[16,16,512]{2,1,0:T(8,128)(2,1)}), bf16[16,16,512]{2,1,0:T(8,128)(2,1)S(1)}, u32[]{:S(2)}, u32[]{:S(2)}) async-start(bf16[16,16,512]{2,1,0:T(8,128)(2,1)} %bitcast.14), calls=%async_computation.1 | async-start | bytes 524288 | tf_op jit(solution)/shard_map/all_to_all | solution.py:473
  36.1 6.8 %local0.1.refs_3_ = bf16[12,256,512]{2,1,0:T(8,128)(2,1)} custom-call(s32[8,384]{1,0:T(8,128)} %bitcast.15, bf16[384,512]{1,0:T(8,128)(2,1)} %get-tuple-element.22.refs_1_.refs_4_, bf16[2,1536,512]{2,1,0:T(8,128)(2,1)} %refs_2_.10, bf16[384,512]{1,0:T(8,128)(2,1)} %get-tuple-element.23.refs_3_, bf16[12,256,512]{2,1,0:T(8,128)(2,1)} %get-tuple-element.24.refs_4_), custom_call_target="tpu_custom_call" | custom-call | flops 10000000000 | bytes 8388608 | tf_op jit(solution)/shard_map/local0/pallas_call | solution.py:171
  43.0 3.2 %all-to-all-done.1 = bf16[16,16,512]{2,1,0:T(8,128)(2,1)S(1)} async-done(((bf16[16,16,512]{2,1,0:T(8,128)(2,1)}), bf16[16,16,512]{2,1,0:T(8,128)(2,1)S(1)}, u32[]{:S(2)}, u32[]{:S(2)}) %all-to-all-start.1) | async-done | bytes 262176 | tf_op jit(solution)/shard_map/all_to_all | solution.py:473
  46.2 0.0 copy-start.2
  46.2 0.7 copy-done.2
  46.9 10.4 %edge0.1 = (bf16[384,512]{1,0:T(8,128)(2,1)}, bf16[256,512]{1,0:T(8,128)(2,1)}, bf16[384,512]{1,0:T(8,128)(2,1)}, bf16[12,256,512]{2,1,0:T(8,128)(2,1)}, bf16[256,512]{1,0:T(8,128)(2,1)}) custom-call(s32[8,384]{1,0:T(8,128)} %bitcast.16, bf16[256,512]{1,0:T(8,128)(2,1)} %bitcast.11, bf16[2,512,512]{2,1,0:T(8,128)(2,1)} %refs_2_.11, ...), custom_call_target="tpu_custom_call", output_to_operand_aliasing={{4}: (1, {})} | custom-call | flops 1000000000 | bytes 8388608 | tf_op jit(solution)/shard_map/edge0/pallas_call | solution.py:171
  57.2 3.8 %all-to-all-start.2 = ((bf16[16,16,512]{2,1,0:T(8,128)(2,1)}), bf16[16,16,512]{2,1,0:T(8,128)(2,1)S(1)}, u32[]{:S(2)}, u32[]{:S(2)}) async-start(bf16[16,16,512]{2,1,0:T(8,128)(2,1)} %bitcast.13), calls=%async_computation.2 | async-start | bytes 524288 | tf_op jit(solution)/shard_map/all_to_all | solution.py:473
  61.0 8.7 %local1.1.refs_3_ = bf16[12,256,512]{2,1,0:T(8,128)(2,1)} custom-call(s32[8,384]{1,0:T(8,128)} %bitcast.17, bf16[384,512]{1,0:T(8,128)(2,1)} %get-tuple-element.26.refs_1_.refs_4_, bf16[2,1536,512]{2,1,0:T(8,128)(2,1)} %refs_2_.10, bf16[384,512]{1,0:T(8,128)(2,1)} %get-tuple-element.27.refs_3_, bf16[12,256,512]{2,1,0:T(8,128)(2,1)} %get-tuple-element.28.refs_4_, ...), custom_call_target="tpu_custom_call" | custom-call | flops 10000000000 | bytes 8388608 | tf_op jit(solution)/shard_map/local1/pallas_call | solution.py:171
  69.7 1.1 %all-to-all-done.2 = bf16[16,16,512]{2,1,0:T(8,128)(2,1)S(1)} async-done(((bf16[16,16,512]{2,1,0:T(8,128)(2,1)}), bf16[16,16,512]{2,1,0:T(8,128)(2,1)S(1)}, u32[]{:S(2)}, u32[]{:S(2)}) %all-to-all-start.2) | async-done | bytes 262176 | tf_op jit(solution)/shard_map/all_to_all | solution.py:473
  70.8 0.0 copy-start.1
  70.8 0.7 copy-done.1
  71.5 9.5 %edge1.1 = (bf16[384,512]{1,0:T(8,128)(2,1)}, bf16[256,512]{1,0:T(8,128)(2,1)}) custom-call(s32[8,384]{1,0:T(8,128)} %bitcast.18, bf16[256,512]{1,0:T(8,128)(2,1)} %bitcast.10, bf16[2,512,512]{2,1,0:T(8,128)(2,1)} %refs_2_.11, bf16[12,256,512]{2,1,0:T(8,128)(2,1)} %local1.1.refs_3_, ...), custom_call_target="tpu_custom_call", output_to_operand_aliasing={{1}: (1, {})} | custom-call | flops 1000000000 | bytes 8388608 | tf_op jit(solution)/shard_map/edge1/pallas_call | solution.py:171
Async XLA Ops:
  2.3 21.9 %all-to-all-start = ((bf16[16,32,512]{2,1,0:T(8,128)(2,1)}), bf16[16,32,512]{2,1,0:T(8,128)(2,1)S(1)}, u32[]{:S(2)}, u32[]{:S(2)}) async-start(bf16[16,32,512]{2,1,0:T(8,128)(2,1)} %bitcast.12), calls=%async_computation | async-start | bytes 1048576 | tf_op jit(solution)/shard_map/all_to_all | solution.py:473
  24.2 0.8 copy-start
  32.0 14.2 %all-to-all-start.1 = ((bf16[16,16,512]{2,1,0:T(8,128)(2,1)}), bf16[16,16,512]{2,1,0:T(8,128)(2,1)S(1)}, u32[]{:S(2)}, u32[]{:S(2)}) async-start(bf16[16,16,512]{2,1,0:T(8,128)(2,1)} %bitcast.14), calls=%async_computation.1 | async-start | bytes 524288 | tf_op jit(solution)/shard_map/all_to_all | solution.py:473
  46.2 0.7 copy-start.2
  57.2 13.6 %all-to-all-start.2 = ((bf16[16,16,512]{2,1,0:T(8,128)(2,1)}), bf16[16,16,512]{2,1,0:T(8,128)(2,1)S(1)}, u32[]{:S(2)}, u32[]{:S(2)}) async-start(bf16[16,16,512]{2,1,0:T(8,128)(2,1)} %bitcast.13), calls=%async_computation.2 | async-start | bytes 524288 | tf_op jit(solution)/shard_map/all_to_all | solution.py:473
  70.8 0.7 copy-start.1

commit v8 on v5

--- a/solution.py
+++ b/solution.py
@@ -13,6 +13,8 @@
 MIB = 2**20
 EXTRA = 32
 CHUNK = 32
+EDGE_GROUP = 2
+LOCAL_GROUP = 4
 
 
 def dot(left, right, left_dim=1, right_dim=0):
@@ -23,11 +25,6 @@
 
 def silu(values):
     half = 0.5 * values
-    return half + half * jnp.tanh(half)
-
-
-def silu16(values):
-    half = (0.5 * values).astype(bf16)
     return half + half * jnp.tanh(half)
 
 
@@ -36,6 +33,16 @@
     center = values - jnp.sum(values, axis=-1, keepdims=True) * scale
     spread = jnp.sum(center * center, axis=-1, keepdims=True) * scale
     return center * lax.rsqrt(spread + epsilon)
+
+
+def one_hot(columns, group, count):
+    lanes = iota((columns.shape[0], count), 1)
+    picks = [jnp.where(lanes == columns[:, j : j + 1], 1.0, 0.0).astype(bf16) for j in group]
+    return jnp.concatenate(picks, axis=0)
+
+
+def groups_of(degree, size):
+    return [range(begin, begin + size) for begin in range(0, degree, size)]
 
 
 def iota(shape, dim):
@@ -123,32 +130,33 @@
             target = in_vmem[i] if count == 1 else in_vmem[i].at[piece]
             loads[i][piece] = Load(view, target, in_sems.at[starts[i] + piece])
         loads = [pieces if len(pieces) > 1 else pieces[0] for pieces in loads]
-        pending, waiting = [], []
-
-        def store(i, value, piece=None, hold=False):
+        pending = []
+
+        def start(i, piece):
             target = out_vmem[i] if piece is None else out_vmem[i].at[piece]
             out = out_refs[i] if piece is None else out_refs[i].at[piece]
+            copy = pltpu.make_async_copy(target, out, out_sems.at[out_starts[i] + (piece or 0)])
+            copy.start()
+            pending.append(copy)
+
+        def store(i, value, piece=None):
+            target = out_vmem[i] if piece is None else out_vmem[i].at[piece]
             if callable(value):
                 value(target)
             else:
                 target[...] = value
-            copy = pltpu.make_async_copy(target, out, out_sems.at[out_starts[i] + (piece or 0)])
-            waiting.append(copy)
-            if not hold:
-                flush()
-
-        def flush():
-            for copy in waiting:
-                copy.start()
-            pending.extend(waiting)
-            waiting.clear()
-
-        store.flush = flush
+            start(i, piece)
+
+        def many(i, fill, pieces):
+            fill([out_vmem[i].at[piece] for piece in pieces])
+            for piece in pieces:
+                start(i, piece)
+
+        store.many = many
         kernel(loads, store, *rest[n_in + n_out + 2 :])
         for pieces in loads:
             for load in pieces if isinstance(pieces, list) else [pieces]:
                 load()
-        flush()
         for copy in pending:
             copy.wait()
 
@@ -293,7 +301,7 @@
     weights = jnp.where(
         lanes == tail - EXTRA + 24, 16.0, jnp.where(lanes == tail - EXTRA + 25, 1.0, 0.0)
     ).astype(bf16)
-    chunks = [slice(begin, begin + 128) for begin in range(0, slots, 128)]
+    chunks = [slice(begin, begin + 256) for begin in range(0, slots, 256)]
 
     def each(values, function):
         parts = [values[i : i + CHUNK, :] for i in range(0, values.shape[0], CHUNK)]
@@ -338,22 +346,37 @@
     send(store, 1, state, sender_first()[...], select()[...])
 
 
-def local_kernel(step, last, loads, store):
+def local_kernel(step, last, loads, store, summands, kept):
     senders, state, receiver_first, sent = loads[:4]
     parts = loads[5 if step else 4]
     degree, owned = senders.target.shape
+    groups = groups_of(degree, LOCAL_GROUP)
     columns = jnp.transpose(senders()[...].astype(f32)).astype(jnp.int32)
-    kept = dot(state()[...], receiver_first()[...]).astype(bf16).astype(f32)
-    for j in range(degree):
-        local = jnp.where(iota((owned, owned), 1) == columns[:, j : j + 1], 1.0, 0.0)
-        part = parts[j]()[...]
+    kept[...] = dot(state()[...], receiver_first()[...]).astype(bf16).astype(f32)
+    for group in groups:
+        summands[...] = dot(one_hot(columns, group, owned), sent()[...])
+        olds = [parts[j]() for j in group]
         if step:
-            edge_state = (part.astype(f32) + loads[6][j]()[...].astype(f32)).astype(bf16)
+            states = [
+                (olds[i][...].astype(f32) + loads[6][j]()[...].astype(f32)).astype(bf16)
+                for i, j in enumerate(group)
+            ]
             if not last:
-                store(1, edge_state, j)
-            part = dot(edge_state, loads[4]()[...])
-        part = dot(local.astype(bf16), sent()[...]) + part.astype(f32)
-        store(0, (part + kept).astype(bf16), j)
+                for i, j in enumerate(group):
+                    store(1, states[i], j)
+            summands[...] += dot(jnp.concatenate(states, axis=0), loads[4]()[...])
+        for i, j in enumerate(group):
+
+            def fill(target):
+                for begin in range(0, owned, CHUNK):
+                    some = slice(begin, begin + CHUNK)
+                    values = summands[i * owned + begin : i * owned + begin + CHUNK, :]
+                    values = values + kept[some, :]
+                    if not step:
+                        values = values + olds[i][some, :].astype(f32)
+                    target[some, :] = values.astype(bf16)
+
+            store(0, fill, j)
 
 
 def edge_kernel(step, last, loads, store, summands, hiddens, results, total):
@@ -361,45 +384,50 @@
     (state, state_first, summed_first, update_second, gain) = loads[4:9]
     degree, owned = senders.target.shape
     rows = incoming.target.shape[0]
+    groups = groups_of(degree, EDGE_GROUP)
     columns = jnp.transpose((senders()[...] - owned).astype(f32)).astype(jnp.int32)
 
-    def lead(j):
-        pick = jnp.where(iota((owned, rows), 1) == columns[:, j : j + 1], 1.0, 0.0)
-        summands[j % 2] = dot(pick.astype(bf16), incoming()[...])
-
-    def middle(j):
-        if j in (0, 2):
-            for load in sums[j : 2 if j == 0 else degree]:
-                load()
-        part = sums[j].target
-        for begin in range(0, owned, CHUNK):
-            some = slice(begin, begin + CHUNK)
-            summand = part[some, :].astype(f32) + summands[j % 2, some, :]
-            hiddens[j % 2, some, :] = silu16(summand)
-        results[j % 2] = dot(hiddens[j % 2], second()[...])
-
-    def tail(j):
-        def fill(target):
+    def lead(g):
+        summands[g % 2] = dot(one_hot(columns, groups[g], rows), incoming()[...])
+
+    def middle(g):
+        for i, j in enumerate(groups[g]):
+            part = sums[j]()
             for begin in range(0, owned, CHUNK):
-                some = slice(begin, begin + CHUNK)
-                message = normalize(results[j % 2, some, :]).astype(bf16)
-                if target is not None:
-                    target[some, :] = message
-                message = message.astype(f32)
-                total[some, :] = message if j == 0 else total[some, :] + message
+                some = slice(i * owned + begin, i * owned + begin + CHUNK)
+                summand = part[begin : begin + CHUNK, :].astype(f32) + summands[g % 2, some, :]
+                hiddens[g % 2, some, :] = silu(summand).astype(bf16)
+        results[g % 2] = dot(hiddens[g % 2], second()[...])
+
+    def tail(g):
+        group = groups[g]
+
+        def fill(targets):
+            for begin in range(0, owned, CHUNK):
+                here = slice(begin, begin + CHUNK)
+                added = total[here, :] if g else None
+                for i, j in enumerate(group):
+                    some = slice(i * owned + begin, i * owned + begin + CHUNK)
+                    message = normalize(results[g % 2, some, :])
+                    if targets is not None:
+                        message = message.astype(bf16)
+                        targets[i][here, :] = message
+                        message = message.astype(f32)
+                    added = message if added is None else added + message
+                total[here, :] = added
 
         if last:
             fill(None)
         else:
-            store(3, fill, j, j % 4 != 3)
+            store.many(3, fill, group)
 
     lead(0)
     middle(0)
-    for j in range(degree):
-        if j + 1 < degree:
-            lead(j + 1)
-            middle(j + 1)
-        tail(j)
+    for g in range(len(groups)):
+        if g + 1 < len(groups):
+            lead(g + 1)
+            middle(g + 1)
+        tail(g)
     summand = dot(state()[...], state_first()[...]) + dot(
         total[...].astype(bf16), summed_first()[...]
     )
@@ -538,6 +566,10 @@
             + extra
             + [(parts, piece_of, degree)]
             + ([(message, piece_of, degree)] if step else []),
+            [
+                pltpu.VMEM((LOCAL_GROUP * owned, width), f32),
+                pltpu.VMEM((owned, width), f32),
+            ],
             flops=10**10,
         )
         if kept:
@@ -564,9 +596,9 @@
             ]
             + extra,
             [
-                pltpu.VMEM((2, owned, width), f32),
-                pltpu.VMEM((2, owned, width), bf16),
-                pltpu.VMEM((2, owned, width), f32),
+                pltpu.VMEM((2, EDGE_GROUP * owned, width), f32),
+                pltpu.VMEM((2, EDGE_GROUP * owned, width), bf16),
+                pltpu.VMEM((2, EDGE_GROUP * owned, width), f32),
                 pltpu.VMEM((owned, width), f32),
             ],
         )

time: 80.9 us -> 81.8 us (1.011)
  Pallas kernels: 50.2 us -> 51.3 us
    pallas_call x7, Pallas kernels: 50.2 us -> 51.3 us  [run(): pl.pallas_call(whole, out_shape=[jax.ShapeDtypeStruct(out[0], out[1]) for...]
  transfers between devices with their start and end apart: 3 -> 3, of which waited for: 3 -> 3; matrix products, arithmetic and copies ran while one was open for 0% -> 0% of each run, Pallas kernels for 28% -> 27%
where the time goes in v8:
time: 81.8 us; the launch traced here: 81.1 us
  Pallas kernels  51.3 us (63%)
  starting transfers between devices  15.3 us (19%)
  waiting for transfers between devices  12.1 us (15%)
  local copies, waits for them, and re-layouts  2.2 us (3%)
    pallas_call x7, Pallas kernels, run(): pl.pallas_call(whole, out_shape=[jax.ShapeDtypeStruct(out[0], out[1]) for...  51.3 us
    all_to_all x3, starting transfers between devices, exchange(): lax.all_to_all(values, 'rows', split_axis=0, concat_axis=0, tiled=True)  15.3 us
    all_to_all x3, waiting for transfers between devices, exchange(): lax.all_to_all(values, 'rows', split_axis=0, concat_axis=0, tiled=True)  12.1 us
    unnamed x6, local copies, waits for them, and re-layouts  2.2 us
  transfers between devices with their start and end apart: 3, of which 3 were waited for; matrix products, arithmetic and copies ran while one was open for 0% of the time, Pallas kernels for 27%

profile of v8, /device:TPU:0, one launch (start us, length us, event | category | flops | bytes accessed | tf_op | source)
XLA Modules:
  0.0 81.1 jit_solution(16614774790188564797)
XLA Ops:
  0.0 2.3 %pack.1 = bf16[512,512]{1,0:T(8,128)(2,1)} custom-call(bf16[474,128]{1,0:T(8,128)(2,1)} %refs_0_.2, f32[4,256]{1,0:T(4,128)} %refs_1_.3, s32[2,128]{1,0:T(2,128)} %bitcast.19, s32[2,128]{1,0:T(2,128)} %bitcast.20), custom_call_target="tpu_custom_call" | custom-call | flops 1000000000 | bytes 8388608 | tf_op jit(solution)/shard_map/pack/pallas_call | solution.py:168
  2.3 7.4 %all-to-all-start = ((bf16[16,32,512]{2,1,0:T(8,128)(2,1)}), bf16[16,32,512]{2,1,0:T(8,128)(2,1)S(1)}, u32[]{:S(2)}, u32[]{:S(2)}) async-start(bf16[16,32,512]{2,1,0:T(8,128)(2,1)} %bitcast.12), calls=%async_computation | async-start | bytes 1048576 | tf_op jit(solution)/shard_map/all_to_all | solution.py:479
  9.7 8.7 %side.1 = (bf16[8,384,512]{2,1,0:T(8,128)(2,1)}, bf16[8,384,512]{2,1,0:T(8,128)(2,1)}, bf16[384,512]{1,0:T(8,128)(2,1)}, f32[384,512]{1,0:T(8,128)}, bf16[256,384]{1,0:T(8,128)(2,1)}) custom-call(f32[4,3072]{1,0:T(4,128)} %refs_0_.3, f32[4,512]{1,0:T(4,128)} %refs_1_.4, bf16[2,1536,512]{2,1,0:T(8,128)(2,1)} %refs_2_.10, bf16[384,512]{1,0:T(8,128)(2,1)} %refs_11_.1, ...), custom_call_target="tpu_custom_call" | custom-call | flops 10000000000 | bytes 8388608 | tf_op jit(solution)/shard_map/side/pallas_call | solution.py:168
  18.5 5.7 %all-to-all-done = bf16[16,32,512]{2,1,0:T(8,128)(2,1)S(1)} async-done(((bf16[16,32,512]{2,1,0:T(8,128)(2,1)}), bf16[16,32,512]{2,1,0:T(8,128)(2,1)S(1)}, u32[]{:S(2)}, u32[]{:S(2)}) %all-to-all-start) | async-done | bytes 524320 | tf_op jit(solution)/shard_map/all_to_all | solution.py:479
  24.2 0.0 copy-start
  24.2 0.8 copy-done
  25.0 7.0 %link.1 = (bf16[384,512]{1,0:T(8,128)(2,1)}, bf16[256,512]{1,0:T(8,128)(2,1)}, bf16[384,512]{1,0:T(8,128)(2,1)}) custom-call(bf16[512,512]{1,0:T(8,128)(2,1)} %bitcast.9, bf16[474,512]{1,0:T(8,128)(2,1)} %refs_1_.5, f32[4,512]{1,0:T(4,128)} %refs_2_.7, bf16[512,512]{1,0:T(8,128)(2,1)} %refs_3_.3, bf16[1536,512]{1,0:T(8,128)(2,1)} %refs_4_.3, ...), custom_call_target="tpu_custom_call" | custom-call | flops 1000000000 | bytes 8388608 | tf_op jit(solution)/shard_map/link/pallas_call | solution.py:168
  32.0 4.1 %all-to-all-start.1 = ((bf16[16,16,512]{2,1,0:T(8,128)(2,1)}), bf16[16,16,512]{2,1,0:T(8,128)(2,1)S(1)}, u32[]{:S(2)}, u32[]{:S(2)}) async-start(bf16[16,16,512]{2,1,0:T(8,128)(2,1)} %bitcast.14), calls=%async_computation.1 | async-start | bytes 524288 | tf_op jit(solution)/shard_map/all_to_all | solution.py:479
  36.1 5.5 %local0.1.refs_3_ = bf16[8,384,512]{2,1,0:T(8,128)(2,1)} custom-call(s32[8,384]{1,0:T(8,128)} %bitcast.15, bf16[384,512]{1,0:T(8,128)(2,1)} %get-tuple-element.21.refs_1_.refs_4_, bf16[2,1536,512]{2,1,0:T(8,128)(2,1)} %refs_2_.10, bf16[384,512]{1,0:T(8,128)(2,1)} %get-tuple-element.22.refs_3_, bf16[8,384,512]{2,1,0:T(8,128)(2,1)} %get-tuple-element.23.refs_4_), custom_call_target="tpu_custom_call" | custom-call | flops 10000000000 | bytes 8388608 | tf_op jit(solution)/shard_map/local0/pallas_call | solution.py:168
  41.7 4.5 %all-to-all-done.1 = bf16[16,16,512]{2,1,0:T(8,128)(2,1)S(1)} async-done(((bf16[16,16,512]{2,1,0:T(8,128)(2,1)}), bf16[16,16,512]{2,1,0:T(8,128)(2,1)S(1)}, u32[]{:S(2)}, u32[]{:S(2)}) %all-to-all-start.1) | async-done | bytes 262176 | tf_op jit(solution)/shard_map/all_to_all | solution.py:479
  46.2 0.0 copy-start.1
  46.2 0.7 copy-done.1
  46.9 10.5 %edge0.1 = (bf16[384,512]{1,0:T(8,128)(2,1)}, bf16[256,512]{1,0:T(8,128)(2,1)}, bf16[384,512]{1,0:T(8,128)(2,1)}, bf16[8,384,512]{2,1,0:T(8,128)(2,1)}) custom-call(s32[8,384]{1,0:T(8,128)} %bitcast.16, bf16[256,512]{1,0:T(8,128)(2,1)} %bitcast.10, bf16[2,512,512]{2,1,0:T(8,128)(2,1)} %refs_2_.11, bf16[8,384,512]{2,1,0:T(8,128)(2,1)} %local0.1.refs_3_, ...), custom_call_target="tpu_custom_call" | custom-call | flops 1000000000 | bytes 8388608 | tf_op jit(solution)/shard_map/edge0/pallas_call | solution.py:168
  57.3 3.8 %all-to-all-start.2 = ((bf16[16,16,512]{2,1,0:T(8,128)(2,1)}), bf16[16,16,512]{2,1,0:T(8,128)(2,1)S(1)}, u32[]{:S(2)}, u32[]{:S(2)}) async-start(bf16[16,16,512]{2,1,0:T(8,128)(2,1)} %bitcast.13), calls=%async_computation.2 | async-start | bytes 524288 | tf_op jit(solution)/shard_map/all_to_all | solution.py:479
  61.1 7.9 %local1.1.refs_3_ = bf16[8,384,512]{2,1,0:T(8,128)(2,1)} custom-call(s32[8,384]{1,0:T(8,128)} %bitcast.17, bf16[384,512]{1,0:T(8,128)(2,1)} %get-tuple-element.25.refs_1_.refs_4_, bf16[2,1536,512]{2,1,0:T(8,128)(2,1)} %refs_2_.10, bf16[384,512]{1,0:T(8,128)(2,1)} %get-tuple-element.26.refs_3_, bf16[8,384,512]{2,1,0:T(8,128)(2,1)} %get-tuple-element.27.refs_4_, ...), custom_call_target="tpu_custom_call" | custom-call | flops 10000000000 | bytes 8388608 | tf_op jit(solution)/shard_map/local1/pallas_call | solution.py:168
  69.1 1.8 %all-to-all-done.2 = bf16[16,16,512]{2,1,0:T(8,128)(2,1)S(1)} async-done(((bf16[16,16,512]{2,1,0:T(8,128)(2,1)}), bf16[16,16,512]{2,1,0:T(8,128)(2,1)S(1)}, u32[]{:S(2)}, u32[]{:S(2)}) %all-to-all-start.2) | async-done | bytes 262176 | tf_op jit(solution)/shard_map/all_to_all | solution.py:479
  70.9 0.0 copy-start.2
  70.9 0.7 copy-done.2
  71.6 9.3 %edge1.1 = bf16[384,512]{1,0:T(8,128)(2,1)} custom-call(s32[8,384]{1,0:T(8,128)} %bitcast.18, bf16[256,512]{1,0:T(8,128)(2,1)} %bitcast.11, bf16[2,512,512]{2,1,0:T(8,128)(2,1)} %refs_2_.11, bf16[8,384,512]{2,1,0:T(8,128)(2,1)} %local1.1.refs_3_, bf16[384,512]{1,0:T(8,128)(2,1)} %get-tuple-element.25.refs_1_.refs_4_, bf16[2,1024,512]{2,1,0:T(8,128)(2,1)} %refs_5_.5, ...), custom_call_target="tpu_custom_call" | custom-call | flops 1000000000 | bytes 8388608 | tf_op jit(solution)/shard_map/edge1/pallas_call | solution.py:168
Async XLA Ops:
  2.3 21.9 %all-to-all-start = ((bf16[16,32,512]{2,1,0:T(8,128)(2,1)}), bf16[16,32,512]{2,1,0:T(8,128)(2,1)S(1)}, u32[]{:S(2)}, u32[]{:S(2)}) async-start(bf16[16,32,512]{2,1,0:T(8,128)(2,1)} %bitcast.12), calls=%async_computation | async-start | bytes 1048576 | tf_op jit(solution)/shard_map/all_to_all | solution.py:479
  24.2 0.8 copy-start
  32.0 14.2 %all-to-all-start.1 = ((bf16[16,16,512]{2,1,0:T(8,128)(2,1)}), bf16[16,16,512]{2,1,0:T(8,128)(2,1)S(1)}, u32[]{:S(2)}, u32[]{:S(2)}) async-start(bf16[16,16,512]{2,1,0:T(8,128)(2,1)} %bitcast.14), calls=%async_computation.1 | async-start | bytes 524288 | tf_op jit(solution)/shard_map/all_to_all | solution.py:479
  46.2 0.7 copy-start.1
  57.3 13.6 %all-to-all-start.2 = ((bf16[16,16,512]{2,1,0:T(8,128)(2,1)}), bf16[16,16,512]{2,1,0:T(8,128)(2,1)S(1)}, u32[]{:S(2)}, u32[]{:S(2)}) async-start(bf16[16,16,512]{2,1,0:T(8,128)(2,1)} %bitcast.13), calls=%async_computation.2 | async-start | bytes 524288 | tf_op jit(solution)/shard_map/all_to_all | solution.py:479
  70.9 0.7 copy-start.2

commit v9 on v5

--- a/solution.py
+++ b/solution.py
@@ -26,9 +26,19 @@
     return half + half * jnp.tanh(half)
 
 
-def silu16(values):
-    half = (0.5 * values).astype(bf16)
+def silu_of_half(half):
     return half + half * jnp.tanh(half)
+
+
+def centred(weights):
+    values = weights.astype(f32)
+    mean = jnp.sum(values, axis=-1, keepdims=True) * (1.0 / values.shape[-1])
+    return (values - mean).astype(bf16)
+
+
+def scale_rows(values):
+    spread = jnp.sum(values * values, axis=-1, keepdims=True) * (1.0 / values.shape[-1])
+    return values * lax.rsqrt(spread + epsilon)
 
 
 def normalize(values):
@@ -226,7 +236,8 @@
 
 
 def side_kernel(loads, store, pieces, turned, table):
-    features, embed, edge_first, start, link_receiver, update_start, lists = loads
+    features, embed, edge_first, start, link_receiver, update_start, lists = loads[:7]
+    singles, stacks = loads[7:10], loads[10:]
     owned, width = start.target.shape
     edges = features.target.shape[1]
     degree = edges // owned
@@ -242,7 +253,7 @@
         left = turned[pl.ds(j, owned, stride=degree), :].astype(bf16)
         edge_state = normalize(silu(dot(left, matrix))).astype(bf16)
         store(0, edge_state, j)
-        store(1, dot(edge_state, edge_first()[...]).astype(bf16), j)
+        store(1, (0.5 * dot(edge_state, edge_first()[...])).astype(bf16), j)
     store(2, dot(start()[...], link_receiver()[...]).astype(bf16))
     store(3, dot(start()[...], update_start()[...]))
     lists = lists()[0]
@@ -254,15 +265,20 @@
     chosen = jnp.where(iota((rows, slots), 1) == row % slots, high * 16.0 + low, 0.0)
     column = jnp.sum(chosen, axis=1, keepdims=True).astype(jnp.int32)
     store(4, jnp.where(iota((rows, owned), 1) == column, 1.0, 0.0).astype(bf16))
+    for place, load in enumerate(singles):
+        store(5 + place, centred(load()[...]))
+    for place, load in enumerate(stacks):
+        weights = load()[...]
+        store(8 + place, jnp.stack([centred(part) for part in weights], axis=0))
 
 
 def update(state, summand, second, gain):
     hidden = silu(summand).astype(bf16)
-    return (state.astype(f32) + gain * normalize(dot(hidden, second))).astype(bf16)
+    return (state.astype(f32) + gain * scale_rows(dot(hidden, second))).astype(bf16)
 
 
 def send(store, base, state, sender, select):
-    sent = dot(state, sender).astype(bf16)
+    sent = dot(state, sender).astype(bf16) * 0.5
     store(base, dot(select, sent).astype(bf16))
     store(base + 1, sent)
 
@@ -321,14 +337,14 @@
     for load in (embed_second, link_sender, link_edge, receiver, link_second):
         load()
     for rows in chunks:
-        hidden[rows, :] = each(dot(hidden[rows, :], embed_second()[...]), normalize)
+        hidden[rows, :] = each(dot(hidden[rows, :], embed_second()[...]), scale_rows)
     for rows in chunks:
         sender = dot(hidden[rows, :], link_sender()[...]).astype(bf16).astype(f32)
         link_terms = (sender + dot(edge_state[rows, :], link_edge()[...])).astype(bf16)
         summand = link_terms.astype(f32) + dot(picks[rows, :], receiver()[...])
         hidden[rows, :] = each(summand, silu)
     for rows in chunks:
-        messages[rows, :] = each(dot(hidden[rows, :], link_second()[...]), normalize)
+        messages[rows, :] = each(dot(hidden[rows, :], link_second()[...]), scale_rows)
     for load in (base, update_first, update_second, gain, start, sender_first, select):
         load()
     summed = dot(collect, messages[...]).astype(bf16)
@@ -343,7 +359,9 @@
     parts = loads[5 if step else 4]
     degree, owned = senders.target.shape
     columns = jnp.transpose(senders()[...].astype(f32)).astype(jnp.int32)
-    kept = dot(state()[...], receiver_first()[...]).astype(bf16).astype(f32)
+    kept = 0.5 * dot(state()[...], receiver_first()[...]).astype(bf16).astype(f32)
+    if step:
+        edge_first = loads[4]()[...] * 0.5
     for j in range(degree):
         local = jnp.where(iota((owned, owned), 1) == columns[:, j : j + 1], 1.0, 0.0)
         part = parts[j]()[...]
@@ -351,7 +369,7 @@
             edge_state = (part.astype(f32) + loads[6][j]()[...].astype(f32)).astype(bf16)
             if not last:
                 store(1, edge_state, j)
-            part = dot(edge_state, loads[4]()[...])
+            part = dot(edge_state, edge_first)
         part = dot(local.astype(bf16), sent()[...]) + part.astype(f32)
         store(0, (part + kept).astype(bf16), j)
 
@@ -368,30 +386,28 @@
         summands[j % 2] = dot(pick.astype(bf16), incoming()[...])
 
     def middle(j):
-        if j in (0, 2):
-            for load in sums[j : 2 if j == 0 else degree]:
-                load()
-        part = sums[j].target
+        part = sums[j]()
         for begin in range(0, owned, CHUNK):
             some = slice(begin, begin + CHUNK)
             summand = part[some, :].astype(f32) + summands[j % 2, some, :]
-            hiddens[j % 2, some, :] = silu16(summand)
+            hiddens[j % 2, some, :] = silu_of_half(summand).astype(bf16)
         results[j % 2] = dot(hiddens[j % 2], second()[...])
 
     def tail(j):
         def fill(target):
             for begin in range(0, owned, CHUNK):
                 some = slice(begin, begin + CHUNK)
-                message = normalize(results[j % 2, some, :]).astype(bf16)
+                message = scale_rows(results[j % 2, some, :])
                 if target is not None:
+                    message = message.astype(bf16)
                     target[some, :] = message
-                message = message.astype(f32)
+                    message = message.astype(f32)
                 total[some, :] = message if j == 0 else total[some, :] + message
 
         if last:
             fill(None)
         else:
-            store(3, fill, j, j % 4 != 3)
+            store(3, fill, j)
 
     lead(0)
     middle(0)
@@ -461,7 +477,10 @@
         [pltpu.VMEM((width, links), bf16), pltpu.VMEM((EXTRA, links), f32)],
     )
     terms = exchange(packed)
-    edge_state, parts, receiver, base, select = run(
+    steps = process_first.shape[0]
+    singles = (embed_second, link_second, update_second)
+    stacks = (process_second, process_update_second)
+    edge_state, parts, receiver, base, select, *seconds = run(
         side_kernel,
         "side",
         [
@@ -470,7 +489,8 @@
             ((owned, width), bf16, 1),
             ((owned, width), f32, 1),
             ((halo_rows, owned), bf16, 1),
-        ],
+        ]
+        + [(array.shape, bf16, 1) for array in singles + stacks],
         (
             edge_features,
             edge_embed,
@@ -479,7 +499,9 @@
             (link_first, rows_of(width, 2 * width), 1),
             (update_first, rows_of(0, width), 1),
             halo_lists,
-        ),
+        )
+        + singles
+        + stacks,
         [
             pltpu.VMEM((EXTRA, edges), f32),
             pltpu.VMEM((edges, 128), f32),
@@ -487,6 +509,7 @@
         ],
         flops=10**10,
     )
+    embed_second, link_second, update_second, process_second, process_update_second = seconds
     state, outgoing, sent = run(
         link_kernel,
         "link",
@@ -517,7 +540,6 @@
             pltpu.VMEM((slots, owned), bf16),
         ],
     )
-    steps = process_first.shape[0]
     for step in range(steps):
         last = step + 1 == steps
         incoming = exchange(outgoing)

time: 80.9 us -> 77.8 us (0.962)
  Pallas kernels: 50.2 us -> 48.5 us
  waiting for transfers between devices: 12.2 us -> 10.7 us
    pallas_call x7, Pallas kernels: 50.2 us -> 48.5 us  [run(): pl.pallas_call(whole, out_shape=[jax.ShapeDtypeStruct(out[0], out[1]) for...]
    all_to_all x3, waiting for transfers between devices: 12.2 us -> 10.7 us  [exchange(): lax.all_to_all(values, 'rows', split_axis=0, concat_axis=0, tiled=True)]
  transfers between devices with their start and end apart: 3 -> 3, of which waited for: 3 -> 3; matrix products, arithmetic and copies ran while one was open for 0% -> 0% of each run, Pallas kernels for 28% -> 31%
where the time goes in v9:
time: 77.8 us; the launch traced here: 77.1 us
  Pallas kernels  48.5 us (62%)
  starting transfers between devices  15.3 us (20%)
  waiting for transfers between devices  10.7 us (14%)
  local copies, waits for them, and re-layouts  2.28 us (3%)
    pallas_call x7, Pallas kernels, run(): pl.pallas_call(whole, out_shape=[jax.ShapeDtypeStruct(out[0], out[1]) for...  48.5 us
    all_to_all x3, starting transfers between devices, exchange(): lax.all_to_all(values, 'rows', split_axis=0, concat_axis=0, tiled=True)  15.3 us
    all_to_all x3, waiting for transfers between devices, exchange(): lax.all_to_all(values, 'rows', split_axis=0, concat_axis=0, tiled=True)  10.7 us
    unnamed x6, local copies, waits for them, and re-layouts  2.28 us
  transfers between devices with their start and end apart: 3, of which 3 were waited for; matrix products, arithmetic and copies ran while one was open for 0% of the time, Pallas kernels for 31%

profile of v9, /device:TPU:0, one launch (start us, length us, event | category | flops | bytes accessed | tf_op | source)
XLA Modules:
  0.0 77.1 jit_solution(17326656378910360284)
XLA Ops:
  0.0 2.4 %pack.1 = bf16[512,512]{1,0:T(8,128)(2,1)} custom-call(bf16[474,128]{1,0:T(8,128)(2,1)} %refs_0_.2, f32[4,256]{1,0:T(4,128)} %refs_1_.3, s32[2,128]{1,0:T(2,128)} %bitcast.19, s32[2,128]{1,0:T(2,128)} %bitcast.20), custom_call_target="tpu_custom_call" | custom-call | flops 1000000000 | bytes 8388608 | tf_op jit(solution)/shard_map/pack/pallas_call | solution.py:170
  2.4 7.4 %all-to-all-start = ((bf16[16,32,512]{2,1,0:T(8,128)(2,1)}), bf16[16,32,512]{2,1,0:T(8,128)(2,1)S(1)}, u32[]{:S(2)}, u32[]{:S(2)}) async-start(bf16[16,32,512]{2,1,0:T(8,128)(2,1)} %bitcast.12), calls=%async_computation | async-start | bytes 1048576 | tf_op jit(solution)/shard_map/all_to_all | solution.py:467
  9.8 10.2 %side.1 = (bf16[8,384,512]{2,1,0:T(8,128)(2,1)}, bf16[8,384,512]{2,1,0:T(8,128)(2,1)}, bf16[384,512]{1,0:T(8,128)(2,1)}, f32[384,512]{1,0:T(8,128)}, bf16[256,38...) custom-call(f32[4,3072]{1,0:T(4,128)} %refs_0_.3, ...), custom_call_target="tpu_custom_call" | custom-call | flops 10000000000 | bytes 8388608 | tf_op jit(solution)/shard_map/side/pallas_call | solution.py:170
  20.0 4.3 %all-to-all-done = bf16[16,32,512]{2,1,0:T(8,128)(2,1)S(1)} async-done(((bf16[16,32,512]{2,1,0:T(8,128)(2,1)}), bf16[16,32,512]{2,1,0:T(8,128)(2,1)S(1)}, u32[]{:S(2)}, u32[]{:S(2)}) %all-to-all-start) | async-done | bytes 524320 | tf_op jit(solution)/shard_map/all_to_all | solution.py:467
  24.3 0.0 copy-start
  24.3 0.9 %copy-done = bf16[16,32,512]{2,1,0:T(8,128)(2,1)} copy-done((bf16[16,32,512]{2,1,0:T(8,128)(2,1)}, bf16[16,32,512]{2,1,0:T(8,128)(2,1)S(1)}, u32[]{:S(2)}) %copy-start) | copy-done | bytes 524312
  25.1 6.6 %link.1 = (bf16[384,512]{1,0:T(8,128)(2,1)}, bf16[256,512]{1,0:T(8,128)(2,1)}, bf16[384,512]{1,0:T(8,128)(2,1)}) custom-call(bf16[512,512]{1,0:T(8,128)(2,1)} %bitcast.9, bf16[474,512]{1,0:T(8,128)(2,1)} %refs_1_.5, f32[4,512]{1,0:T(4,128)} %refs_2_.5, bf16[512,512]{1,0:T(8,128)(2,1)} %get-tuple-element.22.refs_3_, bf16[1536,512]{1,0:T(8,128)(2,1)} %refs_4_.3, ...), custom_call_target="tpu_custom_call" | custom-call | flops 1000000000 | bytes 8388608 | tf_op jit(solution)/shard_map/link/pallas_call | solution.py:170
  31.7 4.1 %all-to-all-start.1 = ((bf16[16,16,512]{2,1,0:T(8,128)(2,1)}), bf16[16,16,512]{2,1,0:T(8,128)(2,1)S(1)}, u32[]{:S(2)}, u32[]{:S(2)}) async-start(bf16[16,16,512]{2,1,0:T(8,128)(2,1)} %bitcast.13), calls=%async_computation.1 | async-start | bytes 524288 | tf_op jit(solution)/shard_map/all_to_all | solution.py:467
  35.9 5.5 %local0.1.refs_3_ = bf16[8,384,512]{2,1,0:T(8,128)(2,1)} custom-call(s32[8,384]{1,0:T(8,128)} %bitcast.15, bf16[384,512]{1,0:T(8,128)(2,1)} %get-tuple-element.30.refs_1_.refs_4_, bf16[2,1536,512]{2,1,0:T(8,128)(2,1)} %refs_2_.7, bf16[384,512]{1,0:T(8,128)(2,1)} %get-tuple-element.31.refs_3_, bf16[8,384,512]{2,1,0:T(8,128)(2,1)} %get-tuple-element.32.refs_4_), custom_call_target="tpu_custom_call" | custom-call | flops 10000000000 | bytes 8388608 | tf_op jit(solution)/shard_map/local0/pallas_call | solution.py:170
  41.4 4.5 %all-to-all-done.1 = bf16[16,16,512]{2,1,0:T(8,128)(2,1)S(1)} async-done(((bf16[16,16,512]{2,1,0:T(8,128)(2,1)}), bf16[16,16,512]{2,1,0:T(8,128)(2,1)S(1)}, u32[]{:S(2)}, u32[]{:S(2)}) %all-to-all-start.1) | async-done | bytes 262176 | tf_op jit(solution)/shard_map/all_to_all | solution.py:467
  45.9 0.0 copy-start.1
  45.9 0.7 copy-done.1
  46.6 8.5 %edge0.1 = (bf16[384,512]{1,0:T(8,128)(2,1)}, bf16[256,512]{1,0:T(8,128)(2,1)}, bf16[384,512]{1,0:T(8,128)(2,1)}, bf16[8,384,512]{2,1,0:T(8,128)(2,1)}) custom-call(s32[8,384]{1,0:T(8,128)} %bitcast.16, bf16[256,512]{1,0:T(8,128)(2,1)} %bitcast.10, bf16[2,512,512]{2,1,0:T(8,128)(2,1)} %get-tuple-element.29.refs_2_, bf16[8,384,512]{2,1,0:T(8,128)(2,1)} %local0.1.refs_3_, ...), custom_call_target="tpu_custom_call" | custom-call | flops 1000000000 | bytes 8388608 | tf_op jit(solution)/shard_map/edge0/pallas_call | solution.py:170
  55.1 3.8 %all-to-all-start.2 = ((bf16[16,16,512]{2,1,0:T(8,128)(2,1)}), bf16[16,16,512]{2,1,0:T(8,128)(2,1)S(1)}, u32[]{:S(2)}, u32[]{:S(2)}) async-start(bf16[16,16,512]{2,1,0:T(8,128)(2,1)} %bitcast.14), calls=%async_computation.2 | async-start | bytes 524288 | tf_op jit(solution)/shard_map/all_to_all | solution.py:467
  58.9 7.9 %local1.1.refs_3_ = bf16[8,384,512]{2,1,0:T(8,128)(2,1)} custom-call(s32[8,384]{1,0:T(8,128)} %bitcast.17, bf16[384,512]{1,0:T(8,128)(2,1)} %get-tuple-element.35.refs_1_.refs_4_, bf16[2,1536,512]{2,1,0:T(8,128)(2,1)} %refs_2_.7, bf16[384,512]{1,0:T(8,128)(2,1)} %get-tuple-element.36.refs_3_, bf16[8,384,512]{2,1,0:T(8,128)(2,1)} %get-tuple-element.37.refs_4_, ...), custom_call_target="tpu_custom_call" | custom-call | flops 10000000000 | bytes 8388608 | tf_op jit(solution)/shard_map/local1/pallas_call | solution.py:170
  66.8 1.9 %all-to-all-done.2 = bf16[16,16,512]{2,1,0:T(8,128)(2,1)S(1)} async-done(((bf16[16,16,512]{2,1,0:T(8,128)(2,1)}), bf16[16,16,512]{2,1,0:T(8,128)(2,1)S(1)}, u32[]{:S(2)}, u32[]{:S(2)}) %all-to-all-start.2) | async-done | bytes 262176 | tf_op jit(solution)/shard_map/all_to_all | solution.py:467
  68.7 0.0 copy-start.2
  68.7 0.7 copy-done.2
  69.4 7.5 %edge1.1 = bf16[384,512]{1,0:T(8,128)(2,1)} custom-call(s32[8,384]{1,0:T(8,128)} %bitcast.18, bf16[256,512]{1,0:T(8,128)(2,1)} %bitcast.11, bf16[2,512,512]{2,1,0:T(8,128)(2,1)} %get-tuple-element.29.refs_2_, bf16[8,384,512]{2,1,0:T(8,128)(2,1)} %local1.1.refs_3_, bf16[384,512]{1,0:T(8,128)(2,1)} %get-tuple-element.35.refs_1_.refs_4_, ...), custom_call_target="tpu_custom_call" | custom-call | flops 1000000000 | bytes 8388608 | tf_op jit(solution)/shard_map/edge1/pallas_call | solution.py:170
Async XLA Ops:
  2.4 21.9 %all-to-all-start = ((bf16[16,32,512]{2,1,0:T(8,128)(2,1)}), bf16[16,32,512]{2,1,0:T(8,128)(2,1)S(1)}, u32[]{:S(2)}, u32[]{:S(2)}) async-start(bf16[16,32,512]{2,1,0:T(8,128)(2,1)} %bitcast.12), calls=%async_computation | async-start | bytes 1048576 | tf_op jit(solution)/shard_map/all_to_all | solution.py:467
  24.3 0.9 %copy-start = (bf16[16,32,512]{2,1,0:T(8,128)(2,1)}, bf16[16,32,512]{2,1,0:T(8,128)(2,1)S(1)}, u32[]{:S(2)}) copy-start(bf16[16,32,512]{2,1,0:T(8,128)(2,1)S(1)} %all-to-all-done) | copy-start | bytes 1572868
  31.7 14.2 %all-to-all-start.1 = ((bf16[16,16,512]{2,1,0:T(8,128)(2,1)}), bf16[16,16,512]{2,1,0:T(8,128)(2,1)S(1)}, u32[]{:S(2)}, u32[]{:S(2)}) async-start(bf16[16,16,512]{2,1,0:T(8,128)(2,1)} %bitcast.13), calls=%async_computation.1 | async-start | bytes 524288 | tf_op jit(solution)/shard_map/all_to_all | solution.py:467
  45.9 0.7 copy-start.1
  55.1 13.6 %all-to-all-start.2 = ((bf16[16,16,512]{2,1,0:T(8,128)(2,1)}), bf16[16,16,512]{2,1,0:T(8,128)(2,1)S(1)}, u32[]{:S(2)}, u32[]{:S(2)}) async-start(bf16[16,16,512]{2,1,0:T(8,128)(2,1)} %bitcast.14), calls=%async_computation.2 | async-start | bytes 524288 | tf_op jit(solution)/shard_map/all_to_all | solution.py:467
  68.7 0.7 copy-start.2

commit v10 on v9

--- a/solution.py
+++ b/solution.py
@@ -386,7 +386,13 @@
         summands[j % 2] = dot(pick.astype(bf16), incoming()[...])
 
     def middle(j):
-        part = sums[j]()
+        if j in (0, 2):
+            for load in sums[j : 2 if j == 0 else degree]:
+                load()
+        if j == 4:
+            for load in loads[4:]:
+                load()
+        part = sums[j].target
         for begin in range(0, owned, CHUNK):
             some = slice(begin, begin + CHUNK)
             summand = part[some, :].astype(f32) + summands[j % 2, some, :]
@@ -407,7 +413,7 @@
         if last:
             fill(None)
         else:
-            store(3, fill, j)
+            store(3, fill, j, j % 4 != 3)
 
     lead(0)
     middle(0)

time: 77.8 us -> 76.7 us (0.986)
  Pallas kernels: 48.5 us -> 47.3 us
    pallas_call x7, Pallas kernels: 48.5 us -> 47.3 us  [run(): pl.pallas_call(whole, out_shape=[jax.ShapeDtypeStruct(out[0], out[1]) for...]
where the time goes in v10:
time: 76.7 us; the launch traced here: 75.9 us
  Pallas kernels  47.3 us (62%)
  starting transfers between devices  15.3 us (20%)
  waiting for transfers between devices  10.7 us (14%)
  local copies, waits for them, and re-layouts  2.28 us (3%)
    pallas_call x7, Pallas kernels, run(): pl.pallas_call(whole, out_shape=[jax.ShapeDtypeStruct(out[0], out[1]) for...  47.3 us
    all_to_all x3, starting transfers between devices, exchange(): lax.all_to_all(values, 'rows', split_axis=0, concat_axis=0, tiled=True)  15.3 us
    all_to_all x3, waiting for transfers between devices, exchange(): lax.all_to_all(values, 'rows', split_axis=0, concat_axis=0, tiled=True)  10.7 us
    unnamed x6, local copies, waits for them, and re-layouts  2.28 us
  transfers between devices with their start and end apart: 3, of which 3 were waited for; matrix products, arithmetic and copies ran while one was open for 0% of the time, Pallas kernels for 31%

profile of v10, /device:TPU:0, one launch (start us, length us, event | category | flops | bytes accessed | tf_op | source)
XLA Modules:
  0.0 75.9 jit_solution(8932841263597142085)
XLA Ops:
  0.0 2.4 %pack.1 = bf16[512,512]{1,0:T(8,128)(2,1)} custom-call(bf16[474,128]{1,0:T(8,128)(2,1)} %refs_0_.2, f32[4,256]{1,0:T(4,128)} %refs_1_.3, s32[2,128]{1,0:T(2,128)} %bitcast.19, s32[2,128]{1,0:T(2,128)} %bitcast.20), custom_call_target="tpu_custom_call" | custom-call | flops 1000000000 | bytes 8388608 | tf_op jit(solution)/shard_map/pack/pallas_call | solution.py:170
  2.4 7.4 %all-to-all-start = ((bf16[16,32,512]{2,1,0:T(8,128)(2,1)}), bf16[16,32,512]{2,1,0:T(8,128)(2,1)S(1)}, u32[]{:S(2)}, u32[]{:S(2)}) async-start(bf16[16,32,512]{2,1,0:T(8,128)(2,1)} %bitcast.12), calls=%async_computation | async-start | bytes 1048576 | tf_op jit(solution)/shard_map/all_to_all | solution.py:473
  9.8 10.2 %side.1 = (bf16[8,384,512]{2,1,0:T(8,128)(2,1)}, bf16[8,384,512]{2,1,0:T(8,128)(2,1)}, bf16[384,512]{1,0:T(8,128)(2,1)}, f32[384,512]{1,0:T(8,128)}, bf16[256,38...) custom-call(f32[4,3072]{1,0:T(4,128)} %refs_0_.3, ...), custom_call_target="tpu_custom_call" | custom-call | flops 10000000000 | bytes 8388608 | tf_op jit(solution)/shard_map/side/pallas_call | solution.py:170
  20.0 4.3 %all-to-all-done = bf16[16,32,512]{2,1,0:T(8,128)(2,1)S(1)} async-done(((bf16[16,32,512]{2,1,0:T(8,128)(2,1)}), bf16[16,32,512]{2,1,0:T(8,128)(2,1)S(1)}, u32[]{:S(2)}, u32[]{:S(2)}) %all-to-all-start) | async-done | bytes 524320 | tf_op jit(solution)/shard_map/all_to_all | solution.py:473
  24.3 0.0 copy-start
  24.3 0.9 %copy-done = bf16[16,32,512]{2,1,0:T(8,128)(2,1)} copy-done((bf16[16,32,512]{2,1,0:T(8,128)(2,1)}, bf16[16,32,512]{2,1,0:T(8,128)(2,1)S(1)}, u32[]{:S(2)}) %copy-start) | copy-done | bytes 524312
  25.1 6.6 %link.1 = (bf16[384,512]{1,0:T(8,128)(2,1)}, bf16[256,512]{1,0:T(8,128)(2,1)}, bf16[384,512]{1,0:T(8,128)(2,1)}) custom-call(bf16[512,512]{1,0:T(8,128)(2,1)} %bitcast.9, bf16[474,512]{1,0:T(8,128)(2,1)} %refs_1_.5, f32[4,512]{1,0:T(4,128)} %refs_2_.5, bf16[512,512]{1,0:T(8,128)(2,1)} %get-tuple-element.22.refs_3_, bf16[1536,512]{1,0:T(8,128)(2,1)} %refs_4_.3, ...), custom_call_target="tpu_custom_call" | custom-call | flops 1000000000 | bytes 8388608 | tf_op jit(solution)/shard_map/link/pallas_call | solution.py:170
  31.7 4.1 %all-to-all-start.1 = ((bf16[16,16,512]{2,1,0:T(8,128)(2,1)}), bf16[16,16,512]{2,1,0:T(8,128)(2,1)S(1)}, u32[]{:S(2)}, u32[]{:S(2)}) async-start(bf16[16,16,512]{2,1,0:T(8,128)(2,1)} %bitcast.13), calls=%async_computation.1 | async-start | bytes 524288 | tf_op jit(solution)/shard_map/all_to_all | solution.py:473
  35.9 5.5 %local0.1.refs_3_ = bf16[8,384,512]{2,1,0:T(8,128)(2,1)} custom-call(s32[8,384]{1,0:T(8,128)} %bitcast.15, bf16[384,512]{1,0:T(8,128)(2,1)} %get-tuple-element.30.refs_1_.refs_4_, bf16[2,1536,512]{2,1,0:T(8,128)(2,1)} %refs_2_.7, bf16[384,512]{1,0:T(8,128)(2,1)} %get-tuple-element.31.refs_3_, bf16[8,384,512]{2,1,0:T(8,128)(2,1)} %get-tuple-element.32.refs_4_), custom_call_target="tpu_custom_call" | custom-call | flops 10000000000 | bytes 8388608 | tf_op jit(solution)/shard_map/local0/pallas_call | solution.py:170
  41.4 4.5 %all-to-all-done.1 = bf16[16,16,512]{2,1,0:T(8,128)(2,1)S(1)} async-done(((bf16[16,16,512]{2,1,0:T(8,128)(2,1)}), bf16[16,16,512]{2,1,0:T(8,128)(2,1)S(1)}, u32[]{:S(2)}, u32[]{:S(2)}) %all-to-all-start.1) | async-done | bytes 262176 | tf_op jit(solution)/shard_map/all_to_all | solution.py:473
  45.9 0.0 copy-start.1
  45.9 0.7 copy-done.1
  46.6 7.9 %edge0.1 = (bf16[384,512]{1,0:T(8,128)(2,1)}, bf16[256,512]{1,0:T(8,128)(2,1)}, bf16[384,512]{1,0:T(8,128)(2,1)}, bf16[8,384,512]{2,1,0:T(8,128)(2,1)}) custom-call(s32[8,384]{1,0:T(8,128)} %bitcast.16, bf16[256,512]{1,0:T(8,128)(2,1)} %bitcast.10, bf16[2,512,512]{2,1,0:T(8,128)(2,1)} %get-tuple-element.29.refs_2_, bf16[8,384,512]{2,1,0:T(8,128)(2,1)} %local0.1.refs_3_, ...), custom_call_target="tpu_custom_call" | custom-call | flops 1000000000 | bytes 8388608 | tf_op jit(solution)/shard_map/edge0/pallas_call | solution.py:170
  54.5 3.8 %all-to-all-start.2 = ((bf16[16,16,512]{2,1,0:T(8,128)(2,1)}), bf16[16,16,512]{2,1,0:T(8,128)(2,1)S(1)}, u32[]{:S(2)}, u32[]{:S(2)}) async-start(bf16[16,16,512]{2,1,0:T(8,128)(2,1)} %bitcast.14), calls=%async_computation.2 | async-start | bytes 524288 | tf_op jit(solution)/shard_map/all_to_all | solution.py:473
  58.3 7.9 %local1.1.refs_3_ = bf16[8,384,512]{2,1,0:T(8,128)(2,1)} custom-call(s32[8,384]{1,0:T(8,128)} %bitcast.17, bf16[384,512]{1,0:T(8,128)(2,1)} %get-tuple-element.35.refs_1_.refs_4_, bf16[2,1536,512]{2,1,0:T(8,128)(2,1)} %refs_2_.7, bf16[384,512]{1,0:T(8,128)(2,1)} %get-tuple-element.36.refs_3_, bf16[8,384,512]{2,1,0:T(8,128)(2,1)} %get-tuple-element.37.refs_4_, ...), custom_call_target="tpu_custom_call" | custom-call | flops 10000000000 | bytes 8388608 | tf_op jit(solution)/shard_map/local1/pallas_call | solution.py:170
  66.1 1.9 %all-to-all-done.2 = bf16[16,16,512]{2,1,0:T(8,128)(2,1)S(1)} async-done(((bf16[16,16,512]{2,1,0:T(8,128)(2,1)}), bf16[16,16,512]{2,1,0:T(8,128)(2,1)S(1)}, u32[]{:S(2)}, u32[]{:S(2)}) %all-to-all-start.2) | async-done | bytes 262176 | tf_op jit(solution)/shard_map/all_to_all | solution.py:473
  68.1 0.0 copy-start.2
  68.1 0.7 copy-done.2
  68.8 6.9 %edge1.1 = bf16[384,512]{1,0:T(8,128)(2,1)} custom-call(s32[8,384]{1,0:T(8,128)} %bitcast.18, bf16[256,512]{1,0:T(8,128)(2,1)} %bitcast.11, bf16[2,512,512]{2,1,0:T(8,128)(2,1)} %get-tuple-element.29.refs_2_, bf16[8,384,512]{2,1,0:T(8,128)(2,1)} %local1.1.refs_3_, bf16[384,512]{1,0:T(8,128)(2,1)} %get-tuple-element.35.refs_1_.refs_4_, ...), custom_call_target="tpu_custom_call" | custom-call | flops 1000000000 | bytes 8388608 | tf_op jit(solution)/shard_map/edge1/pallas_call | solution.py:170
Async XLA Ops:
  2.4 21.9 %all-to-all-start = ((bf16[16,32,512]{2,1,0:T(8,128)(2,1)}), bf16[16,32,512]{2,1,0:T(8,128)(2,1)S(1)}, u32[]{:S(2)}, u32[]{:S(2)}) async-start(bf16[16,32,512]{2,1,0:T(8,128)(2,1)} %bitcast.12), calls=%async_computation | async-start | bytes 1048576 | tf_op jit(solution)/shard_map/all_to_all | solution.py:473
  24.3 0.9 %copy-start = (bf16[16,32,512]{2,1,0:T(8,128)(2,1)}, bf16[16,32,512]{2,1,0:T(8,128)(2,1)S(1)}, u32[]{:S(2)}) copy-start(bf16[16,32,512]{2,1,0:T(8,128)(2,1)S(1)} %all-to-all-done) | copy-start | bytes 1572868
  31.7 14.2 %all-to-all-start.1 = ((bf16[16,16,512]{2,1,0:T(8,128)(2,1)}), bf16[16,16,512]{2,1,0:T(8,128)(2,1)S(1)}, u32[]{:S(2)}, u32[]{:S(2)}) async-start(bf16[16,16,512]{2,1,0:T(8,128)(2,1)} %bitcast.13), calls=%async_computation.1 | async-start | bytes 524288 | tf_op jit(solution)/shard_map/all_to_all | solution.py:473
  45.9 0.7 copy-start.1
  54.5 13.6 %all-to-all-start.2 = ((bf16[16,16,512]{2,1,0:T(8,128)(2,1)}), bf16[16,16,512]{2,1,0:T(8,128)(2,1)S(1)}, u32[]{:S(2)}, u32[]{:S(2)}) async-start(bf16[16,16,512]{2,1,0:T(8,128)(2,1)} %bitcast.14), calls=%async_computation.2 | async-start | bytes 524288 | tf_op jit(solution)/shard_map/all_to_all | solution.py:473
  68.1 0.7 copy-start.2
